TPU v7x, 32 devices: a whole 2x2x4 slice. The times are simulated.
32 devices in a mesh: seq: 2 (over y), wide: 16 (over z, x, core).
Axes of the slice: x: 2, y: 2, z: 4, core: 2. Of those that a mesh axis runs over, the one named last changes fastest.
Arguments:
- tokens: bfloat16 [2, 4096, 2048], P(None, ('seq', 'wide')), may hold values from -6 to 6
- attention_weights: bfloat16 [5, 2048, 2048], P(None, 'wide'), may hold values from -0.125 to 0.125
- lowrank_down: bfloat16 [2048, 224], P('wide'), may hold values from -0.125 to 0.125
- lowrank_up: bfloat16 [224, 2048], P(None, 'wide'), may hold values from -0.75 to 0.75
- feedforward_key: bfloat16 [2048, 7168], P('wide'), may hold values from -0.125 to 0.125
- feedforward_value: bfloat16 [7168, 2048], P('wide'), may hold values from -0.0625 to 0.0625
- feedforward_receptance: bfloat16 [2048, 2048], P('wide'), may hold values from -0.125 to 0.125
- vectors: bfloat16 [16, 2048], P(None, 'wide'), may hold values from -11 to 1.61
- output_gradient: bfloat16 [2, 4096, 2048], P(None, ('seq', 'wide')), may hold values from -6 to 6
Outputs:
- block_out: bfloat16 [2, 4096, 2048], P(None, ('seq', 'wide'))
- input_grad: float32 [2, 4096, 2048], P(None, ('seq', 'wide'))
- att_weights_grad: float32 [5, 2048, 2048], P(None, 'wide')
- lora_down_grad: float32 [2048, 224], P('wide')
- lora_up_grad: float32 [224, 2048], P(None, 'wide')
- ffn_key_grad: float32 [2048, 7168], P('wide')
- ffn_value_grad: float32 [7168, 2048], P('wide')
- ffn_recept_grad: float32 [2048, 2048], P('wide')
- vectors_grad: float32 [16, 2048], P(None, 'wide')
All inputs are finite; a program needn't handle non-finite values.
Results may differ from a plain program's by a relative error of at most 0.014.
Values may be sent and summed in bfloat16 or wider, within the bound.
No kernel may reach another device: no remote copies, remote signals or barrier semaphores. Data moves between devices by JAX's collectives and lax.ppermute only.
A program may use at most 768 MiB of HBM per device.

v0:
```python
import jax
import jax.numpy as jnp
from jax import lax
from jax.sharding import PartitionSpec as P

CHANNEL_GROUPS = 32
GROUP_BREADTH = 64
MIX_RANK = 32


exact_arithmetic = lax.Precision.HIGHEST


def from_behind(value, axis, steps):
    count = lax.axis_size(axis)
    leading, last = (max(0, -steps), min(count, count - steps))
    return lax.ppermute(value, axis, [(source, source + steps) for source in range(leading, last)])


def entering(part, axis, combine, identity, reverse):
    count = lax.axis_size(axis)
    place = lax.axis_index(axis)
    ahead = count - 1 - place if reverse else place
    gathered = jax.tree.map(lambda a: lax.all_gather(a, axis), part)
    state = jax.tree.map(lambda a, e: jnp.zeros_like(a) + jnp.asarray(e, a.dtype), part, identity)

    def one(hop, state):
        source = count - 1 - hop if reverse else hop
        return combine(
            state, jax.tree.map(lambda a: lax.dynamic_index_in_dim(a, source, 0, False), gathered)
        )

    return lax.fori_loop(0, ahead, one, state)


def layer_norm(values, gain_row, bias_row):
    mean_val = jnp.mean(values, -1, keepdims=True)
    centered = values - mean_val
    spread = jnp.mean(centered * centered, -1, keepdims=True)
    return centered * lax.rsqrt(spread + 1e-05) * gain_row + bias_row


def plain_product(left, right):
    return jnp.dot(left, right, preferred_element_type=jnp.float32)


def inner_rows(left, right):
    return lax.dot_general(
        left, right, (((0,), (0,)), ((), ())), preferred_element_type=jnp.float32
    )


def outer_cols(left, right):
    return lax.dot_general(
        left, right, (((1,), (1,)), ((), ())), preferred_element_type=jnp.float32
    )


def prior_rows(values, incoming, seq_count):
    shaped = values.reshape(seq_count, -1, values.shape[-1])
    joined = jnp.concatenate([incoming[:, None], shaped[:, :-1]], 1)
    return joined.reshape(values.shape)


def fold_prior(grad_prior, incoming, seq_count):
    shaped = grad_prior.reshape(seq_count, -1, grad_prior.shape[-1])
    joined = jnp.concatenate([shaped[:, 1:], incoming[:, None]], 1)
    return joined.reshape(grad_prior.shape)


def first_rows(values, seq_count):
    return values.reshape(seq_count, -1, values.shape[-1])[:, 0]


def last_rows(values, seq_count):
    return values.reshape(seq_count, -1, values.shape[-1])[:, -1]


def first_mix(normed, prior_all, maa_row):
    return normed + (prior_all - normed) * maa_row


def many_mix(normed, prior_all, maa_rows, offsets):
    return normed[:, None] + (prior_all - normed)[:, None] * (maa_rows[None] + offsets)


def channel_mix(normed, prior_all, maa_rows):
    return normed[:, None] + (prior_all - normed)[:, None] * maa_rows[None]


def decay_sums(logarithmic_fading):
    inclusive = jnp.cumsum(logarithmic_fading, 1)
    return (inclusive, inclusive - logarithmic_fading)


def block_state(address_entries, content_entries, logarithmic_fading):
    inclusive, exclusive = decay_sums(logarithmic_fading)
    final_log = inclusive[:, -1]
    weighted = address_entries * jnp.exp(final_log[:, None] - inclusive)
    return (
        jnp.exp(final_log),
        jnp.einsum("sthi,sthj->shij", weighted, content_entries, precision=exact_arithmetic),
    )


def weighted_key_value_local(
    acceptor_entries,
    address_entries,
    content_entries,
    logarithmic_fading,
    first_reward_entries,
    carried_memory_entry,
):
    block_len = acceptor_entries.shape[1]
    inclusive, exclusive = decay_sums(logarithmic_fading)
    middle = inclusive[:, block_len // 2][:, None]
    query_side = acceptor_entries * jnp.exp(exclusive - middle)
    key_side = address_entries * jnp.exp(middle - inclusive)
    scores = jnp.einsum("sthi,suhi->shtu", query_side, key_side, precision=exact_arithmetic)
    causal_mask = jnp.arange(block_len)[:, None] > jnp.arange(block_len)[None, :]
    scores = jnp.where(causal_mask, scores, 0.0)
    present_element = jnp.sum(acceptor_entries * first_reward_entries * address_entries, -1)
    layer_answer = (
        jnp.einsum("shtu,suhj->sthj", scores, content_entries, precision=exact_arithmetic)
        + present_element[..., None] * content_entries
    )
    layer_answer = layer_answer + jnp.einsum(
        "sthi,shij->sthj",
        acceptor_entries * jnp.exp(exclusive),
        carried_memory_entry,
        precision=exact_arithmetic,
    )
    final_log = inclusive[:, -1]
    state_out = jnp.exp(final_log)[..., None] * carried_memory_entry + jnp.einsum(
        "sthi,sthj->shij",
        address_entries * jnp.exp(final_log[:, None] - inclusive),
        content_entries,
        precision=exact_arithmetic,
    )
    return (layer_answer, state_out)


def gate_norm(wkv_out, gate_pre, gain_row, bias_row):
    mean_val = jnp.mean(wkv_out, -1, keepdims=True)
    centered = wkv_out - mean_val
    spread = jnp.mean(centered * centered, -1, keepdims=True)
    grouped = (centered * lax.rsqrt(spread + 0.00064)).reshape(gate_pre.shape) * gain_row + bias_row
    return grouped * jax.nn.silu(gate_pre)


def chain_step(earlier, later_part):
    return (earlier[0] * later_part[0], later_part[0][..., None] * earlier[1] + later_part[1])


def back_step(earlier, later_part):
    return (later_part[0] * earlier[0], later_part[1] + later_part[0][..., None] * earlier[1])


def body(
    tokens,
    attention_weights,
    lowrank_down,
    lowrank_up,
    feedforward_key,
    feedforward_value,
    feedforward_receptance,
    vectors,
    output_gradient,
):
    seq_count, block_len, model_width = tokens.shape
    tok_total = seq_count * block_len
    mix_columns = 5 * MIX_RANK

    def to_heads(values):
        return values.reshape(seq_count, block_len, CHANNEL_GROUPS, GROUP_BREADTH)

    def to_rows(values):
        return values.reshape(tok_total, model_width)

    att_full, down_full, up_full, vec_full, key_full, value_full, recept_full = (
        lax.all_gather(attention_weights, "wide", axis=1, tiled=True),
        lax.all_gather(lowrank_down, "wide", axis=0, tiled=True),
        lax.all_gather(lowrank_up, "wide", axis=1, tiled=True),
        lax.all_gather(vectors, "wide", axis=1, tiled=True),
        lax.all_gather(feedforward_key, "wide", axis=0, tiled=True),
        lax.all_gather(feedforward_value, "wide", axis=0, tiled=True),
        lax.all_gather(feedforward_receptance, "wide", axis=0, tiled=True),
    )
    entry_lines = vec_full.astype(jnp.float32)
    flat_in = to_rows(tokens.astype(jnp.float32))
    normed, norm_back = jax.vjp(layer_norm, flat_in, entry_lines[0], entry_lines[1])
    incoming = from_behind(last_rows(normed, seq_count), ("seq", "wide"), 1)
    prior_all = prior_rows(normed, incoming, seq_count)
    mix_input, first_back = jax.vjp(first_mix, normed, prior_all, entry_lines[2])
    mix_low = mix_input.astype(jnp.bfloat16)
    tanh_mix = jnp.tanh(plain_product(mix_low, down_full[:, :mix_columns]))
    mix_hidden = tanh_mix.astype(jnp.bfloat16).reshape(tok_total, 5, MIX_RANK)
    up_mix = up_full[:mix_columns].reshape(5, MIX_RANK, model_width)
    offsets = jnp.einsum("nfr,frd->nfd", mix_hidden, up_mix, preferred_element_type=jnp.float32)
    mixed_all, many_back = jax.vjp(many_mix, normed, prior_all, entry_lines[3:8], offsets)
    mixed_low = mixed_all.astype(jnp.bfloat16)
    decay_input, key_in, value_in, recept_in, gate_in = [
        mixed_low[:, position_index] for position_index in range(5)
    ]
    acceptor_entries = plain_product(recept_in, att_full[0])
    address_entries = plain_product(key_in, att_full[1])
    content_entries = plain_product(value_in, att_full[2])
    gate_pre = plain_product(gate_in, att_full[3])
    tanh_decay = jnp.tanh(plain_product(decay_input, down_full[:, mix_columns:]))
    decay_hidden = tanh_decay.astype(jnp.bfloat16)
    logarithmic_fading = -jnp.exp(
        entry_lines[8] + plain_product(decay_hidden, up_full[mix_columns:])
    )
    head_decay = to_heads(logarithmic_fading)
    carry_decay, carry_state = block_state(
        to_heads(address_entries), to_heads(content_entries), head_decay
    )
    neutral = (jnp.ones_like(carry_decay), jnp.zeros_like(carry_state))
    carried_memory_entry = entering(
        (carry_decay, carry_state), ("seq", "wide"), chain_step, neutral, False
    )[1]
    first_reward_entries = entry_lines[9].reshape(CHANNEL_GROUPS, GROUP_BREADTH)
    wkv_pair, wkv_back = jax.vjp(
        weighted_key_value_local,
        to_heads(acceptor_entries),
        to_heads(address_entries),
        to_heads(content_entries),
        head_decay,
        first_reward_entries,
        carried_memory_entry,
    )
    gated, gate_back = jax.vjp(gate_norm, wkv_pair[0], gate_pre, entry_lines[10], entry_lines[11])
    gated_low = gated.astype(jnp.bfloat16)
    first_sum = flat_in + plain_product(gated_low, att_full[4])
    normed_two, norm_two_back = jax.vjp(layer_norm, first_sum, entry_lines[12], entry_lines[13])
    incoming_two = from_behind(last_rows(normed_two, seq_count), ("seq", "wide"), 1)
    prior_two = prior_rows(normed_two, incoming_two, seq_count)
    pair_mix, pair_back = jax.vjp(channel_mix, normed_two, prior_two, entry_lines[14:16])
    pair_low = pair_mix.astype(jnp.bfloat16)
    key_pre = plain_product(pair_low[:, 0], key_full)
    relu_part = jnp.maximum(key_pre, 0.0)
    squared = (relu_part * relu_part).astype(jnp.bfloat16)
    value_out = plain_product(squared, value_full)
    recept_gate = jax.nn.sigmoid(plain_product(pair_low[:, 1], recept_full))
    block_out = (first_sum + recept_gate * value_out).astype(jnp.bfloat16).reshape(tokens.shape)
    grad_out = to_rows(output_gradient.astype(jnp.float32))
    key_back, value_back, recept_back = (
        lax.all_gather(feedforward_key, "wide", axis=0, tiled=True),
        lax.all_gather(feedforward_value, "wide", axis=0, tiled=True),
        lax.all_gather(feedforward_receptance, "wide", axis=0, tiled=True),
    )
    grad_value = (grad_out * recept_gate).astype(jnp.bfloat16)
    grad_gate_in = (grad_out * value_out * recept_gate * (1.0 - recept_gate)).astype(jnp.bfloat16)
    value_grad = inner_rows(squared, grad_value)
    grad_key_pre = (outer_cols(grad_value, value_back) * 2.0 * relu_part).astype(jnp.bfloat16)
    key_grad = inner_rows(pair_low[:, 0], grad_key_pre)
    recept_grad = inner_rows(pair_low[:, 1], grad_gate_in)
    grad_pair = jnp.stack(
        [outer_cols(grad_key_pre, key_back), outer_cols(grad_gate_in, recept_back)], 1
    )
    key_share, value_share, recept_share = (
        lax.psum_scatter(key_grad, "wide", scatter_dimension=0, tiled=True),
        lax.psum_scatter(value_grad, "wide", scatter_dimension=0, tiled=True),
        lax.psum_scatter(recept_grad, "wide", scatter_dimension=0, tiled=True),
    )
    grad_normed_two, grad_prior_two, grad_pair_maa = pair_back(grad_pair)
    returning_two = from_behind(first_rows(grad_prior_two, seq_count), ("seq", "wide"), -1)
    grad_normed_two = grad_normed_two + fold_prior(grad_prior_two, returning_two, seq_count)
    grad_first_norm, grad_gain_two, grad_bias_two = norm_two_back(grad_normed_two)
    grad_first = grad_out + grad_first_norm
    att_back, down_back, up_back = (
        lax.all_gather(attention_weights, "wide", axis=1, tiled=True),
        lax.all_gather(lowrank_down, "wide", axis=0, tiled=True),
        lax.all_gather(lowrank_up, "wide", axis=1, tiled=True),
    )
    grad_att = grad_first.astype(jnp.bfloat16)
    out_weight_grad = inner_rows(gated_low, grad_att)
    grad_wkv, grad_gate_pre, grad_norm_gain, grad_norm_bias = gate_back(
        outer_cols(grad_att, att_back[4])
    )
    exclusive = jnp.cumsum(head_decay, 1) - head_decay
    state_grad = jnp.einsum(
        "sthi,sthj->shij",
        to_heads(acceptor_entries) * jnp.exp(exclusive),
        grad_wkv,
        precision=exact_arithmetic,
    )
    grad_state_out = entering((carry_decay, state_grad), ("seq", "wide"), back_step, neutral, True)[
        1
    ]
    wkv_grads = wkv_back((grad_wkv, grad_state_out))
    grad_decay_term = to_rows(wkv_grads[3]) * logarithmic_fading
    grad_decay_low = grad_decay_term.astype(jnp.bfloat16)
    decay_up_grad = inner_rows(decay_hidden, grad_decay_low)
    grad_pre_decay = (
        outer_cols(grad_decay_low, up_back[mix_columns:]) * (1.0 - tanh_decay * tanh_decay)
    ).astype(jnp.bfloat16)
    decay_down_grad = inner_rows(decay_input, grad_pre_decay)
    grad_projs = [
        to_rows(wkv_grads[0]).astype(jnp.bfloat16),
        to_rows(wkv_grads[1]).astype(jnp.bfloat16),
        to_rows(wkv_grads[2]).astype(jnp.bfloat16),
        grad_gate_pre.astype(jnp.bfloat16),
    ]
    proj_inputs = [recept_in, key_in, value_in, gate_in]
    att_grad = jnp.stack(
        [
            inner_rows(proj_inputs[position_index], grad_projs[position_index])
            for position_index in range(4)
        ]
        + [out_weight_grad],
        0,
    )
    grad_mixed = jnp.stack(
        [
            outer_cols(grad_pre_decay, down_back[:, mix_columns:]),
            outer_cols(grad_projs[1], att_back[1]),
            outer_cols(grad_projs[2], att_back[2]),
            outer_cols(grad_projs[0], att_back[0]),
            outer_cols(grad_projs[3], att_back[3]),
        ],
        1,
    )
    grad_normed_many, grad_prior_many, grad_maa_many, grad_offsets = many_back(grad_mixed)
    grad_offsets_low = grad_offsets.astype(jnp.bfloat16)
    mix_up_grad = jnp.einsum(
        "nfr,nfd->frd", mix_hidden, grad_offsets_low, preferred_element_type=jnp.float32
    ).reshape(mix_columns, model_width)
    up_mix_back = up_back[:mix_columns].reshape(5, MIX_RANK, model_width)
    grad_hidden_mix = jnp.einsum(
        "nfd,frd->nfr", grad_offsets_low, up_mix_back, preferred_element_type=jnp.float32
    ).reshape(tok_total, mix_columns)
    grad_pre_mix = (grad_hidden_mix * (1.0 - tanh_mix * tanh_mix)).astype(jnp.bfloat16)
    mix_down_grad = inner_rows(mix_low, grad_pre_mix)
    grad_normed_first, grad_prior_first, grad_maa_first = first_back(
        outer_cols(grad_pre_mix, down_back[:, :mix_columns])
    )
    grad_prior_sum = grad_prior_many + grad_prior_first
    returning = from_behind(first_rows(grad_prior_sum, seq_count), ("seq", "wide"), -1)
    grad_normed = (
        grad_normed_many + grad_normed_first + fold_prior(grad_prior_sum, returning, seq_count)
    )
    grad_tokens, grad_gain_one, grad_bias_one = norm_back(grad_normed)
    input_grad = (grad_first + grad_tokens).reshape(tokens.shape)
    vec_grad = jnp.concatenate(
        [
            jnp.stack([grad_gain_one, grad_bias_one, grad_maa_first]),
            grad_maa_many,
            jnp.stack(
                [
                    jnp.sum(grad_decay_term, 0),
                    wkv_grads[4].reshape(-1),
                    grad_norm_gain,
                    grad_norm_bias,
                    grad_gain_two,
                    grad_bias_two,
                ]
            ),
            grad_pair_maa,
        ],
        0,
    )
    down_grad = jnp.concatenate([mix_down_grad, decay_down_grad], 1)
    up_grad = jnp.concatenate([mix_up_grad, decay_up_grad], 0)
    att_share, down_share, up_share, vec_share = (
        lax.psum_scatter(att_grad, "wide", scatter_dimension=1, tiled=True),
        lax.psum_scatter(down_grad, "wide", scatter_dimension=0, tiled=True),
        lax.psum_scatter(up_grad, "wide", scatter_dimension=1, tiled=True),
        lax.psum_scatter(vec_grad, "wide", scatter_dimension=1, tiled=True),
    )
    totals = lax.psum(
        (att_share, down_share, up_share, key_share, value_share, recept_share, vec_share), "seq"
    )
    return (
        block_out,
        input_grad,
        totals[0],
        totals[1],
        totals[2],
        totals[3],
        totals[4],
        totals[5],
        totals[6],
    )


def solution(mesh):
    placed = (
        P(None, ("seq", "wide"), None),
        P(None, "wide", None),
        P("wide", None),
        P(None, "wide"),
        P("wide", None),
        P("wide", None),
        P("wide", None),
        P(None, "wide"),
        P(None, ("seq", "wide"), None),
    )
    return jax.shard_map(
        body,
        mesh=mesh,
        in_specs=placed,
        out_specs=(
            P(None, ("seq", "wide"), None),
            P(None, ("seq", "wide"), None),
            P(None, "wide", None),
            P("wide", None),
            P(None, "wide"),
            P("wide", None),
            P("wide", None),
            P("wide", None),
            P(None, "wide"),
        ),
        check_vma=False,
    )
```

profile of v0, /device:TPU:0, one launch (start us, length us, event | category | flops | bytes accessed | tf_op | source)
XLA Modules:
  0.0 4104.1 jit_solution(4120650500180733311)
XLA Ops:
  8.0 23.6 all_gather.45
  35.1 27.4 all_gather.46
  62.5 27.9 all_gather.47
  118.5 118.6 %all-gather.10.cloned.1.call-done = bf16[5,2048,2048]{2,1,0:T(8,128)(2,1)} async-done(((bf16[5,128,2048]{2,1,0:T(8,128)(2,1)}), bf16[5,2048,2048]{2,1,0:T(8,128)(2,1)}) %all-gather.10.cloned.1.call-update) | async-done | bytes 41943056 | tf_op jit(solution)/shard_map/all_gather | solution.py:181
  237.1 16.8 slice_bitcast_fusion.7
  339.0 50.8 %all-gather = f32[64,1,32,64]{3,2,1,0:T(8,128)} all-gather(f32[2,1,32,64]{3,2,1,0:T(8,128)S(1)} %get-tuple-element.220), channel_id=2, replica_groups=mesh['seq'=2,'wide'=16] {'seq','wide'}, dimensions={0}, use_global_device_ids=true | all-gather | bytes 540672 | tf_op jit(solution)/shard_map/all_gather | solution.py:24
  420.9 277.1 %all-gather.18.cloned.1.call-done = f32[64,32,64,64]{3,2,1,0:T(8,128)} async-done(((f32[2,32,64,64]{3,2,1,0:T(8,128)}), f32[64,32,64,64]{3,2,1,0:T(8,128)}) %all-gather.18.cloned.1.call-update) | async-done | bytes 33554448 | tf_op jit(solution)/shard_map/all_gather | solution.py:24
  749.1 97.0 %all-gather.14.cloned.1.call-done = bf16[2048,7168]{1,0:T(8,128)(2,1)} async-done(((bf16[128,7168]{1,0:T(8,128)(2,1)}), bf16[2048,7168]{1,0:T(8,128)(2,1)}) %all-gather.14.cloned.1.call-update) | async-done | bytes 29360144 | tf_op jit(solution)/shard_map/all_gather | solution.py:185
  846.1 17.6 convolution_maximum_fusion
  863.8 132.4 %all-gather.16.cloned.1.call-done = bf16[7168,2048]{1,0:T(8,128)(2,1)} async-done(((bf16[448,2048]{1,0:T(8,128)(2,1)}), bf16[7168,2048]{1,0:T(8,128)(2,1)}) %all-gather.16.cloned.1.call-update) | async-done | bytes 29360144 | tf_op jit(solution)/shard_map/all_gather | solution.py:186
  996.1 16.9 fusion.90
  1013.0 60.0 %all-gather.12.cloned.1.call-done = bf16[2048,2048]{1,0:T(8,128)(2,1)} async-done(((bf16[128,2048]{1,0:T(8,128)(2,1)}), bf16[2048,2048]{1,0:T(8,128)(2,1)}) %all-gather.12.cloned.1.call-update) | async-done | bytes 8388624 | tf_op jit(solution)/shard_map/all_gather | solution.py:187
  1081.7 18.0 fusion.4
  1218.8 297.6 %all-gather.20.cloned.1.call-done = f32[64,32,64,64]{3,2,1,0:T(8,128)} async-done(((f32[2,32,64,64]{3,2,1,0:T(8,128)}), f32[64,32,64,64]{3,2,1,0:T(8,128)}) %all-gather.20.cloned.1.call-update) | async-done | bytes 33554448 | tf_op jit(solution)/shard_map/all_gather | solution.py:24
  1516.7 94.6 %while.27 = (s32[]{:T(128)}, f32[2,32,64,64]{3,2,1,0:T(8,128)S(1)}, s32[]{:T(128)}, f32[32,2,32,64,64]{4,3,2,1,0:T(8,128)}, f32[32,2,32,64]{3,2,1,0:T(8,128)}, /*index=5*/s32[]{:T(128)}, s32[]{:T(128)}, s32[]{:T(128)}, s32[]{:T(128)}) while((s32[]{:T(128)}, f32[2,32,64,64]{3,2,1,0:T(8,128)S(1)}, s32[]{:T(128)}, ...), condition=%wide.region_16.17_spmd, body=%wide.region_15.16_spmd.sunk | while | flops 524294 | bytes 3195027 | solution.py:33
  1632.1 18.2 fusion.142
  1651.8 28.1 negate_add_fusion
  1742.8 23.9 fusion.89
  1766.8 23.5 fusion.106
  1865.4 527.4 %reduce-scatter.16.cloned.1.call-done = f32[448,2048]{1,0:T(8,128)} async-done(((f32[7168,2048]{1,0:T(8,128)}), f32[448,2048]{1,0:T(8,128)}) %reduce-scatter.16.cloned.1.call-update) | async-done | bytes 3670032 | tf_op jit(solution)/shard_map/reduce_scatter | solution.py:263
  2392.9 540.9 %reduce-scatter.14.cloned.1.call-done = f32[128,7168]{1,0:T(8,128)} async-done(((f32[2048,7168]{1,0:T(8,128)}), f32[128,7168]{1,0:T(8,128)}) %reduce-scatter.14.cloned.1.call-update) | async-done | bytes 3670032 | tf_op jit(solution)/shard_map/reduce_scatter | solution.py:262
  2933.8 773.8 %reduce-scatter.8.cloned.1.call-done = f32[5,128,2048]{2,1,0:T(8,128)} async-done(((f32[5,2048,2048]{2,1,0:T(8,128)}), f32[5,128,2048]{2,1,0:T(8,128)}) %reduce-scatter.8.cloned.1.call-update) | async-done | bytes 5242896 | tf_op jit(solution)/shard_map/reduce_scatter | solution.py:366
  3713.3 50.0 %reduce-scatter.20.cloned.1.call-done = f32[16,128]{1,0:T(8,128)} async-done(((f32[16,2048]{1,0:T(8,128)}), f32[16,128]{1,0:T(8,128)}) %reduce-scatter.20.cloned.1.call-update) | async-done | bytes 8208 | tf_op jit(solution)/shard_map/reduce_scatter | solution.py:369
  3768.9 315.2 %all-reduce.5.cloned.1.call-done = (f32[5,128,2048]{2,1,0:T(8,128)}, f32[128,224]{0,1:T(8,128)}, f32[224,128]{1,0:T(8,128)}, f32[128,7168]{1,0:T(8,128)}, f32[448,2048]{1,0:T(8,128)}, /*index=5*/f32[128,2048]{1,0:T(8,128)}) async-done(((f32[5,128,2048]{2,1,0:T(8,128)}, f32[128,224]{0,1:T(8,128)}, f32[224,128]{1,0:T(8,128)}, f32[128,7168]{1,0:T(8,128)}, f32[448,2048]{1,0:T(8,128)}, ...) | async-done | bytes 13860880 | tf_op jit(solution)/shard_map/psum | solution.py:371
  (470 shorter events, 604.8 us)
Async XLA Ops:
  7.2 229.9 %all-gather.10.cloned.1.call-start = ((), (), s32[]{:S(2)}) async-start(), calls=%async_computation.7 | async-start | bytes 44564480 | tf_op jit(solution)/shard_map/all_gather | solution.py:181
  7.9 690.1 %all-gather.18.cloned.1.call-start = ((), (), s32[]{:S(2)}) async-start(), calls=%async_computation.18 | async-start | bytes 69206016 | tf_op jit(solution)/shard_map/all_gather | solution.py:24
  32.8 59.5 %collective-permute-start = (f32[2,2048]{1,0:T(2,128)S(1)}, f32[2,2048]{1,0:T(2,128)S(1)}, u32[]{:S(2)}, u32[]{:S(2)}) collective-permute-start(f32[2,2048]{1,0:T(2,128)S(1)} %bitcast.464), channel_id=1, source_target_pairs={{0,1},{1,2},{2,3},{3,4},{4,5},{5,6},{6,7},{7,8},{8,9},{9,10},{10,1... | collective-permute-start | bytes 49160 | tf_op jit(solution)/shard_map/ppermute | solution.py:17
  92.3 205.6 %copy-start.81 = (f32[32,64]{1,0:T(8,128)}, f32[32,64]{1,0:T(8,128)S(1)}, u32[]{:S(2)}) copy-start(f32[32,64]{1,0:T(8,128)S(1)} %mul.487) | copy-start | bytes 24580
  116.7 181.2 %copy-start.64 = (f32[2,32,64]{2,1,0:T(8,128)}, f32[2,32,64]{2,1,0:T(8,128)S(1)}, u32[]{:S(2)}) copy-start(f32[2,32,64]{2,1,0:T(8,128)S(1)} %get-tuple-element.218) | copy-start | bytes 49156
  116.7 181.2 %copy-start.78 = (f32[2,32,64]{2,1,0:T(8,128)}, f32[2,32,64]{2,1,0:T(8,128)S(1)}, u32[]{:S(2)}) copy-start(f32[2,32,64]{2,1,0:T(8,128)S(1)} %get-tuple-element.219) | copy-start | bytes 49156
  337.0 509.1 %all-gather.14.cloned.1.call-start = ((), (), s32[]{:S(2)}) async-start(), calls=%async_computation.9 | async-start | bytes 31195136 | tf_op jit(solution)/shard_map/all_gather | solution.py:185
  337.8 658.4 %all-gather.16.cloned.1.call-start = ((), (), s32[]{:S(2)}) async-start(), calls=%async_computation.10 | async-start | bytes 31195136 | tf_op jit(solution)/shard_map/all_gather | solution.py:186
  338.3 734.7 %all-gather.12.cloned.1.call-start = ((), (), s32[]{:S(2)}) async-start(), calls=%async_computation.8 | async-start | bytes 8912896 | tf_op jit(solution)/shard_map/all_gather | solution.py:187
  338.9 1177.5 %all-gather.20.cloned.1.call-start = ((), (), s32[]{:S(2)}) async-start(), calls=%async_computation.19 | async-start | bytes 69206016 | tf_op jit(solution)/shard_map/all_gather | solution.py:24
  339.0 365.4 %copy-start.70 = (pred[128,128]{1,0:T(8,128)(4,1)}, pred[128,128]{1,0:T(8,128)(4,1)S(1)}, u32[]{:S(2)}) copy-start(pred[128,128]{1,0:T(8,128)(4,1)S(1)} %iota_compare_fusion) | copy-start | bytes 49156
  411.4 292.9 %copy-start.74 = (f32[2,128,32]{1,2,0:T(8,128)}, f32[2,128,32]{1,2,0:T(8,128)S(1)}, u32[]{:S(2)}) copy-start(f32[2,128,32]{1,2,0:T(8,128)S(1)} %copy.194) | copy-start | bytes 98308
  738.9 6.1 collective-permute-start.1
  863.8 209.3 %copy-start.39 = (bf16[2,128,2048]{2,1,0:T(8,128)(2,1)S(1)}, bf16[2,128,2048]{2,1,0:T(8,128)(2,1)}, u32[]{:S(2)}) copy-start(bf16[2,128,2048]{2,1,0:T(8,128)(2,1)} %param.21) | copy-start | bytes 3145732
  1121.2 3.1 collective-permute-start.2
  1157.1 708.3 %reduce-scatter.18.cloned.1.call-start = ((), (), s32[]{:S(2)}) async-start(), calls=%async_computation.16 | async-start | bytes 17825792 | tf_op jit(solution)/shard_map/reduce_scatter | solution.py:264
  1166.9 698.5 %reduce-scatter.12.cloned.1.call-start = ((), (), s32[]{:S(2)}) async-start(), calls=%async_computation.13 | async-start | bytes 1949696 | tf_op jit(solution)/shard_map/reduce_scatter | solution.py:368
  1732.7 132.7 %reduce-scatter.10.cloned.1.call-start = ((), (), s32[]{:S(2)}) async-start(), calls=%async_computation.12 | async-start | bytes 1949696 | tf_op jit(solution)/shard_map/reduce_scatter | solution.py:367
  1742.5 650.4 %reduce-scatter.16.cloned.1.call-start = ((), (), s32[]{:S(2)}) async-start(), calls=%async_computation.15 | async-start | bytes 62390272 | tf_op jit(solution)/shard_map/reduce_scatter | solution.py:263
  1766.7 1167.0 %reduce-scatter.14.cloned.1.call-start = ((), (), s32[]{:S(2)}) async-start(), calls=%async_computation.14 | async-start | bytes 62390272 | tf_op jit(solution)/shard_map/reduce_scatter | solution.py:262
  1790.3 1917.2 %reduce-scatter.8.cloned.1.call-start = ((), (), s32[]{:S(2)}) async-start(), calls=%async_computation.11 | async-start | bytes 89128960 | tf_op jit(solution)/shard_map/reduce_scatter | solution.py:366
  1837.4 1925.8 %reduce-scatter.20.cloned.1.call-start = ((), (), s32[]{:S(2)}) async-start(), calls=%async_computation.17 | async-start | bytes 139264 | tf_op jit(solution)/shard_map/reduce_scatter | solution.py:369
  1849.6 3.1 collective-permute-start.3
  1865.3 2218.8 %all-reduce.5.cloned.1.call-start = ((), (), s32[]{:S(2)}) async-start(), calls=%async_computation.20 | async-start | bytes 27721728 | tf_op jit(solution)/shard_map/psum | solution.py:371
  (102 other events, 909.3 us)
Sparse Core Ops, SparseCore 0:
  9.6 227.4 all-gather.9
  337.1 360.7 all-gather.17
  699.6 146.5 all-gather.13
  847.6 148.4 all-gather.15
  998.1 74.8 all-gather.11
  1157.2 359.1 all-gather.19
  1520.5 176.7 reduce-scatter.17
  1732.8 56.3 reduce-scatter.11
  1793.0 59.5 reduce-scatter.9
  1856.6 536.2 reduce-scatter.15
  2397.1 536.6 reduce-scatter.13
  2937.8 769.6 reduce-scatter.7
  3711.8 51.3 reduce-scatter.19
  3766.0 318.0 all-reduce.4
where the time goes:
time: 4110 us; the launch traced here: 4100 us
  waiting for transfers between devices  3200 us (78%)
  matrix products  352 us (9%)
  local copies, waits for them, and re-layouts  210 us (5%)
  other arithmetic  183 us (4%)
  blocking collectives  135 us (3%)
    reduce_scatter x1, waiting for transfers between devices, body(): lax.psum_scatter(att_grad, 'wide', scatter_dimension=1, tiled=True)  774 us
    all_gather x2, waiting for transfers between devices, entering(): gathered = jax.tree.map(lambda a: lax.all_gather(a, axis), part)  575 us
    reduce_scatter x1, waiting for transfers between devices, body(): lax.psum_scatter(key_grad, 'wide', scatter_dimension=0, tiled=True)  541 us
    reduce_scatter x1, waiting for transfers between devices, body(): lax.psum_scatter(value_grad, 'wide', scatter_dimension=0, tiled=True)  527 us
    psum x1, waiting for transfers between devices, body(): lax.psum((att_share, down_share, up_share, key_share, value_share, recept...  315 us
    all_gather x1, waiting for transfers between devices, body(): lax.all_gather(feedforward_value, 'wide', axis=0, tiled=True)  132 us
    all_gather x1, waiting for transfers between devices, body(): lax.all_gather(attention_weights, 'wide', axis=1, tiled=True)  119 us
    dot_general x11, matrix products, inner_rows(): lax.dot_general(left, right, (((0,), (0,)), ((), ())), preferred_element_...  105 us
  transfers between devices with their start and end apart: 18, of which 14 were waited for; matrix products, arithmetic and copies ran while one was open for 13% of the time, Pallas kernels for 0%

commit v1 on v0

v1 whole, which is shorter than its diff:
```python
import jax
import jax.numpy as jnp
from jax import lax
from jax.experimental import pallas as pl
from jax.experimental.pallas import tpu as pltpu
from jax.sharding import Mesh
from jax.sharding import PartitionSpec as P

HEADS = 32
HEAD = 64
RANK = 32
MIXCOLS = 5 * RANK
LANES = 128
F32, BF16 = jnp.float32, jnp.bfloat16
WIDE = ("z", "x", "core")
ALL = ("y", "z", "x", "core")
exact = lax.Precision.HIGHEST


def nn(a, b):
    return jnp.dot(a, b, preferred_element_type=F32)


def nt(a, b):
    return lax.dot_general(a, b, (((1,), (1,)), ((), ())), preferred_element_type=F32)


def tn(a, b):
    return lax.dot_general(a, b, (((0,), (0,)), ((), ())), preferred_element_type=F32)


def low(a):
    return a.astype(BF16)


def swap(value, axis):
    return lax.ppermute(value, axis, [(0, 1), (1, 0)])


def along(value, step):
    count = lax.axis_size(ALL)
    if step > 0:
        pairs = [(i, i + 1) for i in range(count - 1)]
    else:
        pairs = [(i + 1, i) for i in range(count - 1)]
    return lax.ppermute(value, ALL, pairs)


def piece(value, index, size, axis):
    start = [0] * value.ndim
    start[axis] = index * size
    shape = list(value.shape)
    shape[axis] = size
    return lax.dynamic_slice(value, start, shape)


def line_sum(block):
    count = lax.axis_size("z")
    place = lax.axis_index("z")

    def own(index):
        return lax.dynamic_index_in_dim(block, jnp.clip(index, 0, count - 1), 0, False).astype(F32)

    up = down = None
    for t in range(1, count):
        right = own(count - t + place)
        left = own(place + t - count)
        if up is not None:
            right = right + up.astype(F32)
            left = left + down.astype(F32)
        up = lax.ppermute(low(right), "z", [(i, i + 1) for i in range(count - 1) if i <= t - 1])
        down = lax.ppermute(
            low(left), "z", [(i, i - 1) for i in range(1, count) if count - 1 - i <= t - 1]
        )
    return own(place) + up.astype(F32) + down.astype(F32)


def x_halves(value):
    x = lax.axis_index("x")
    z = lax.axis_size("z")
    width = value.shape[1] // (2 * z)

    def take(which):
        return jnp.concatenate([piece(value, 2 * i + which, width, 1) for i in range(z)], 1)

    return take(1 - x), take(x)


def plane_sum(left_send, left_own, right):
    z = lax.axis_size("z")
    got = swap(low(tn(left_send, right)), "x")
    acc = low(tn(left_own, right) + got.astype(F32))
    return line_sum(acc.reshape(z, acc.shape[0] // z, acc.shape[1]))


def chip_grad(left, right):
    core = lax.axis_index("core")
    half = right.shape[1] // 2
    mine = piece(right, core, half, 1)
    theirs = piece(right, 1 - core, half, 1)
    left = jnp.concatenate([left, swap(left, "core")], 0)
    right = jnp.concatenate([mine, swap(theirs, "core")], 0)
    send, own = x_halves(left)
    part = plane_sum(send, own, right)
    part = part + swap(low(part), "y").astype(F32)
    rows = part.shape[0] // 2
    keep = piece(part, core, rows, 0)
    give = swap(piece(part, 1 - core, rows, 0), "core")
    first = core == 0
    return jnp.concatenate([jnp.where(first, keep, give), jnp.where(first, give, keep)], 1)


def group_rows(value):
    across = swap(value, "y")
    near = swap(value, "core")
    far = swap(across, "core")
    return jnp.concatenate([value, near, across, far], 0)


def group_sum(value):
    rows = value.shape[0] // 4
    own, near, across, far = [value[i * rows : (i + 1) * rows] for i in range(4)]
    across = across + swap(far, "core")
    got_y = swap(low(across), "y")
    own = own + swap(near, "core")
    return own + got_y.astype(F32)


def chain_kernel(decay_ref, state_ref, out_ref, *, reverse):
    count = state_ref.shape[0]

    def one(hop, held):
        b = count - 1 - hop if reverse else hop
        out_ref[b] = held
        return decay_ref[b] * held + state_ref[b]

    lax.fori_loop(0, count, one, jnp.zeros(state_ref.shape[1:], F32))


def chain(log_decay, state, reverse):
    count = lax.axis_size(ALL)
    rows = state.size // HEAD // count
    wide_rows = rows * HEAD // LANES
    pad = -rows % LANES
    logs = jnp.pad(log_decay.reshape(count, rows), ((0, 0), (0, pad))).reshape(count, -1, LANES)
    packed = jnp.concatenate([state.reshape(count, wide_rows, LANES), logs], 1)
    packed = lax.all_to_all(packed, ALL, 0, 0, tiled=True)
    logs = packed[:, wide_rows:].reshape(count, -1)[:, :rows]
    fade = jnp.repeat(jnp.exp(logs), HEAD, axis=1).reshape(count, wide_rows, LANES)
    spec = pl.BlockSpec(memory_space=pltpu.VMEM)
    entering = pl.pallas_call(
        lambda d, s, o: chain_kernel(d, s, o, reverse=reverse),
        out_shape=jax.ShapeDtypeStruct((count, wide_rows, LANES), F32),
        in_specs=[spec, spec],
        out_specs=spec,
        name="chain",
    )(fade, packed[:, :wide_rows])
    return lax.all_to_all(entering, ALL, 0, 0, tiled=True).reshape(state.shape)


def decay_sums(logs):
    inclusive = jnp.cumsum(logs, 1)
    return inclusive, inclusive - logs


def block_state(keys, values, logs):
    inclusive, _ = decay_sums(logs)
    final = inclusive[:, -1]
    weighted = keys * jnp.exp(final[:, None] - inclusive)
    return final, jnp.einsum("sthi,sthj->shij", weighted, values, precision=exact)


def wkv_local(recept, keys, values, logs, bonus, carried):
    length = recept.shape[1]
    inclusive, exclusive = decay_sums(logs)
    middle = inclusive[:, length // 2][:, None]
    query = recept * jnp.exp(exclusive - middle)
    key_side = keys * jnp.exp(middle - inclusive)
    scores = jnp.einsum("sthi,suhi->shtu", query, key_side, precision=exact)
    causal = jnp.arange(length)[:, None] > jnp.arange(length)[None, :]
    scores = jnp.where(causal, scores, 0.0)
    present = jnp.sum(recept * bonus * keys, -1)
    answer = (
        jnp.einsum("shtu,suhj->sthj", scores, values, precision=exact)
        + present[..., None] * values
    )
    answer = answer + jnp.einsum(
        "sthi,shij->sthj", recept * jnp.exp(exclusive), carried, precision=exact
    )
    final = inclusive[:, -1]
    state_out = jnp.exp(final)[..., None] * carried + jnp.einsum(
        "sthi,sthj->shij", keys * jnp.exp(final[:, None] - inclusive), values, precision=exact
    )
    return answer, state_out


def gate_norm(wkv, gate_pre, gain, bias):
    mean = jnp.mean(wkv, -1, keepdims=True)
    centered = wkv - mean
    spread = jnp.mean(centered * centered, -1, keepdims=True)
    grouped = (centered * lax.rsqrt(spread + 0.00064)).reshape(gate_pre.shape) * gain + bias
    return grouped * jax.nn.silu(gate_pre)


def norm_forward(values, gain, bias):
    mean = jnp.mean(values, -1, keepdims=True)
    centered = values - mean
    rstd = lax.rsqrt(jnp.mean(centered * centered, -1, keepdims=True) + 1e-05)
    hat = centered * rstd
    return hat * gain + bias, hat, rstd


def norm_backward(grad, hat, rstd, gain):
    d = grad * gain
    back = rstd * (
        d - jnp.mean(d, -1, keepdims=True) - hat * jnp.mean(d * hat, -1, keepdims=True)
    )
    return back, jnp.sum(grad * hat, 0), jnp.sum(grad, 0)


def prior_of(values, seqs):
    shaped = values.reshape(seqs, -1, values.shape[-1])
    incoming = along(shaped[:, -1], 1)
    return jnp.concatenate([incoming[:, None], shaped[:, :-1]], 1).reshape(values.shape)


def prior_back(grad, seqs):
    shaped = grad.reshape(seqs, -1, grad.shape[-1])
    incoming = along(shaped[:, 0], -1)
    return jnp.concatenate([shaped[:, 1:], incoming[:, None]], 1).reshape(grad.shape)


def row_gather(value):
    return lax.all_gather(value, WIDE, axis=0, tiled=True)


def body(tokens, att_w, down_w, up_w, key_w, value_w, rec_w, vectors, out_grad):
    seqs, length, width = tokens.shape
    total = seqs * length
    y, core = lax.axis_index("y"), lax.axis_index("core")
    zs = lax.axis_size("z")
    ff = key_w.shape[1]
    share = value_w.shape[0]
    half = share // 2
    quarter = ff // 4

    def heads(v):
        return v.reshape(seqs, length, HEADS, HEAD)

    def rows(v):
        return v.reshape(total, width)

    small = jnp.concatenate([up_w, down_w.T, vectors], 0)
    small = lax.all_gather(small, WIDE, axis=0)
    small = jnp.swapaxes(small, 0, 1).reshape(small.shape[1], width)
    cols = up_w.shape[0]
    up, down_t, vec = small[:cols], small[cols : 2 * cols], small[2 * cols :].astype(F32)
    w_key, w_value, w_rec, w_gate, w_out = [row_gather(att_w[i]) for i in (1, 2, 0, 3, 4)]
    key_sh = key_w.reshape(width // (4 * zs), zs, 2, 2, 2, half)
    key_sh = lax.dynamic_index_in_dim(key_sh, y, 4, False)
    key_sh = key_sh.transpose(0, 3, 2, 1, 4).reshape(-1, 2 * quarter)
    f_key = piece(row_gather(key_sh), core, quarter, 1)
    f_rec = row_gather(rec_w)
    value_sh = piece(value_w, y, half, 0)
    f_value = row_gather(value_sh).reshape(zs, 2, 2, half, width)
    f_value = lax.dynamic_index_in_dim(f_value, core, 2, False)
    f_value = jnp.swapaxes(f_value, 0, 1).reshape(quarter, width)

    x = rows(tokens.astype(F32))
    normed, hat, rstd = norm_forward(x, vec[0], vec[1])
    delta = prior_of(normed, seqs) - normed
    mix_low = low(normed + delta * vec[2])
    tanh_mix = jnp.tanh(nt(mix_low, down_t[:MIXCOLS]))
    hidden = low(tanh_mix)
    hid = [hidden[:, i * RANK : (i + 1) * RANK] for i in range(5)]
    ups = [up[i * RANK : (i + 1) * RANK] for i in range(5)]
    mixed = [low(normed + delta * (vec[3 + i] + nn(hid[i], ups[i]))) for i in range(5)]
    decay_in, key_in, value_in, rec_in, gate_in = mixed
    tanh_decay = jnp.tanh(nt(decay_in, down_t[MIXCOLS:]))
    hidden_decay = low(tanh_decay)
    logdecay = -jnp.exp(vec[8] + nn(hidden_decay, up[MIXCOLS:]))
    keys = nn(key_in, w_key)
    values = nn(value_in, w_value)
    final, state = block_state(heads(keys), heads(values), heads(logdecay))
    carried = chain(final, state, False)
    recept = nn(rec_in, w_rec)
    gate_pre = nn(gate_in, w_gate)
    wkv_pair, wkv_back = jax.vjp(
        wkv_local, heads(recept), heads(keys), heads(values), heads(logdecay),
        vec[9].reshape(HEADS, HEAD), carried,
    )
    gated, gate_back = jax.vjp(gate_norm, wkv_pair[0], gate_pre, vec[10], vec[11])
    gated = low(gated)
    first_sum = x + nn(gated, w_out)

    normed_two, hat_two, rstd_two = norm_forward(first_sum, vec[12], vec[13])
    delta_two = prior_of(normed_two, seqs) - normed_two
    key_mix = low(normed_two + delta_two * vec[14])
    rec_mix = low(normed_two + delta_two * vec[15])
    key_all = group_rows(key_mix)
    relu = jnp.maximum(nn(key_all, f_key), 0.0)
    squared = low(relu * relu)
    value_out = group_sum(nn(squared, f_value))
    rec_gate = jax.nn.sigmoid(nn(rec_mix, f_rec))
    block_out = low(first_sum + rec_gate * value_out).reshape(tokens.shape)

    g = rows(out_grad.astype(F32))
    grad_value = low(g * rec_gate)
    grad_gate_in = low(g * value_out * rec_gate * (1.0 - rec_gate))
    value_all = group_rows(grad_value)
    grad_key_pre = low(nt(value_all, f_value) * 2.0 * relu)
    g_key_mix = group_sum(nt(grad_key_pre, f_key))
    g_rec_mix = nt(grad_gate_in, f_rec)
    xi = lax.axis_index("x")
    value_part = low(
        plane_sum(piece(squared, 1 - xi, quarter // 2, 1), piece(squared, xi, quarter // 2, 1), value_all)
    )
    other = swap(value_part, "y")
    first = y == 0
    value_share = jnp.concatenate(
        [jnp.where(first, value_part, other), jnp.where(first, other, value_part)], 0
    ).astype(F32)
    send, own = x_halves(key_all)
    part = low(plane_sum(send, own, grad_key_pre))
    n = part.shape[0] // 2
    keep = piece(part, core, n, 0)
    give = swap(piece(part, 1 - core, n, 0), "core")
    first_c = core == 0
    key_part = jnp.stack([jnp.where(first_c, keep, give), jnp.where(first_c, give, keep)], 0)
    other = swap(key_part, "y")
    key_share = jnp.stack([jnp.where(first, key_part, other), jnp.where(first, other, key_part)], 0)
    key_share = key_share.reshape(2, 2, n, 2, zs, half).transpose(2, 4, 3, 1, 0, 5)
    key_share = key_share.reshape(n, ff).astype(F32)
    rec_share = chip_grad(rec_mix, grad_gate_in)

    g_prior = prior_back(g_key_mix * vec[14] + g_rec_mix * vec[15], seqs)
    g_normed_two = g_key_mix * (1.0 - vec[14]) + g_rec_mix * (1.0 - vec[15]) + g_prior
    g_maa_key = jnp.sum(g_key_mix * delta_two, 0)
    g_maa_rec = jnp.sum(g_rec_mix * delta_two, 0)
    back_two, g_gain_two, g_bias_two = norm_backward(g_normed_two, hat_two, rstd_two, vec[12])
    grad_first = g + back_two

    grad_att = low(grad_first)
    out_share = chip_grad(gated, grad_att)
    g_wkv, g_gate_pre, g_gain_x, g_bias_x = gate_back(nt(grad_att, w_out))
    exclusive = decay_sums(heads(logdecay))[1]
    state_grad = jnp.einsum(
        "sthi,sthj->shij", heads(recept) * jnp.exp(exclusive), g_wkv, precision=exact
    )
    g_state_out = chain(final, state_grad, True)
    g_rec, g_key, g_val, g_log, g_bonus, _ = wkv_back((g_wkv, g_state_out))
    g_decay = rows(g_log) * logdecay
    g_decay_low = low(g_decay)
    projs = [low(rows(g_rec)), low(rows(g_key)), low(rows(g_val)), low(g_gate_pre)]
    shares = [chip_grad(a, b) for a, b in zip((rec_in, key_in, value_in, gate_in), projs)]
    att_share = jnp.stack(shares + [out_share], 0)

    decay_up_grad = tn(hidden_decay, g_decay_low)
    g_pre_decay = low(nt(g_decay_low, up[MIXCOLS:]) * (1.0 - tanh_decay * tanh_decay))
    decay_down_grad = tn(g_pre_decay, decay_in)
    g_mixed = [
        nn(g_pre_decay, down_t[MIXCOLS:]),
        nt(projs[1], w_key),
        nt(projs[2], w_value),
        nt(projs[0], w_rec),
        nt(projs[3], w_gate),
    ]
    g_normed = g_prior_sum = None
    maa_rows, up_grads, hid_grads = [], [], []
    for i in range(5):
        offset = vec[3 + i] + nn(hid[i], ups[i])
        g_off = g_mixed[i] * delta
        maa_rows.append(jnp.sum(g_off, 0))
        off_low = low(g_off)
        up_grads.append(tn(hid[i], off_low))
        hid_grads.append(nt(off_low, ups[i]))
        here = g_mixed[i] * (1.0 - offset)
        back = g_mixed[i] * offset
        g_normed = here if g_normed is None else g_normed + here
        g_prior_sum = back if g_prior_sum is None else g_prior_sum + back
    g_pre_mix = low(jnp.concatenate(hid_grads, 1) * (1.0 - tanh_mix * tanh_mix))
    mix_down_grad = tn(g_pre_mix, mix_low)
    g_first_mix = nn(g_pre_mix, down_t[:MIXCOLS])
    maa_first = jnp.sum(g_first_mix * delta, 0)
    g_prior_sum = g_prior_sum + g_first_mix * vec[2]
    g_normed = g_normed + g_first_mix * (1.0 - vec[2]) + prior_back(g_prior_sum, seqs)
    back_one, g_gain, g_bias = norm_backward(g_normed, hat, rstd, vec[0])
    input_grad = (grad_first + back_one).reshape(tokens.shape)

    vec_rows = jnp.stack(
        [g_gain, g_bias, maa_first] + maa_rows
        + [jnp.sum(g_decay, 0), g_bonus.reshape(-1), g_gain_x, g_bias_x, g_gain_two, g_bias_two,
           g_maa_key, g_maa_rec], 0,
    )
    packed = jnp.concatenate(up_grads + [decay_up_grad, mix_down_grad, decay_down_grad, vec_rows], 0)
    packed = lax.psum_scatter(packed, WIDE, scatter_dimension=1, tiled=True)
    packed = packed + swap(packed, "y")
    return (
        block_out, input_grad, att_share, packed[cols : 2 * cols].T, packed[:cols],
        key_share, value_share, rec_share, packed[2 * cols :],
    )


def solution(mesh):
    seq, wide = mesh.devices.shape
    fine = Mesh(mesh.devices.reshape(seq, wide // 4, 2, 2), ALL)
    token = P(None, ALL, None)
    by_row, by_col, stacked = P(WIDE, None), P(None, WIDE), P(None, WIDE, None)
    return jax.shard_map(
        body,
        mesh=fine,
        in_specs=(token, stacked, by_row, by_col, by_row, by_row, by_row, by_col, token),
        out_specs=(token, token, stacked, by_row, by_col, by_row, by_row, by_row, by_col),
        check_vma=False,
    )
```

time: 4110 us -> 1900 us (0.46)
  waiting for transfers between devices: 3200 us -> 755 us
  starting transfers between devices: 11.5 us -> 290 us
  blocking collectives: 135 us -> 55.6 us
    reduce_scatter x7 -> x1, waiting for transfers between devices: 1890 us -> 0.01 us  [body(): packed = lax.psum_scatter(packed, WIDE, scatter_dimension=1, tiled=True)]
    all_gather x6 -> x9, waiting for transfers between devices: 983 us -> 396 us  [the longest x8 364 us: row_gather(): return lax.all_gather(value, WIDE, axis=0, tiled=True)]
    ppermute x4 -> x100, waiting for transfers between devices: 2.49 us -> 346 us  [the longest x48 209 us: swap(): return lax.ppermute(value, axis, [(0, 1), (1, 0)])]
    psum x1 -> x0, waiting for transfers between devices: 315 us -> none  [body(): lax.psum((att_share, down_share, up_share, key_share, value_share, recept...]
    ppermute x4 -> x100, starting transfers between devices: 10.1 us -> 166 us  [the longest x24 95.6 us: line_sum(): lax.ppermute(low(right), 'z', [(i, i + 1) for i in range(count - 1) if i...]
    all_gather x4 -> x0, blocking collectives: 130 us -> none  [the longest x1 50.8 us: entering(): gathered = jax.tree.map(lambda a: lax.all_gather(a, axis), part)]
    all_to_all x0 -> x3, starting transfers between devices: none -> 123 us  [the longest x1 117 us: chain(): packed = lax.all_to_all(packed, ALL, 0, 0, tiled=True)]
    add x34 -> x11, other arithmetic: 74.8 us -> 9.92 us  [the longest x1 4.41 us: body(): input_grad = (grad_first + back_one).reshape(tokens.shape)]
  transfers between devices with their start and end apart: 18 -> 113, of which waited for: 14 -> 44; matrix products, arithmetic and copies ran while one was open for 13% -> 39% of each run, Pallas kernels for 0% -> 0%
where the time goes in v1:
time: 1900 us; the launch traced here: 1890 us
  waiting for transfers between devices  755 us (40%)
  matrix products  319 us (17%)
  starting transfers between devices  290 us (15%)
  local copies, waits for them, and re-layouts  234 us (12%)
  other arithmetic  211 us (11%)
  blocking collectives  55.6 us (3%)
    all_gather x8, waiting for transfers between devices, row_gather(): return lax.all_gather(value, WIDE, axis=0, tiled=True)  364 us
    ppermute x48, waiting for transfers between devices, swap(): return lax.ppermute(value, axis, [(0, 1), (1, 0)])  209 us
    all_to_all x1, starting transfers between devices, chain(): packed = lax.all_to_all(packed, ALL, 0, 0, tiled=True)  117 us
    ppermute x24, starting transfers between devices, line_sum(): lax.ppermute(low(right), 'z', [(i, i + 1) for i in range(count - 1) if i...  95.6 us
    ppermute x24, waiting for transfers between devices, line_sum(): lax.ppermute(low(right), 'z', [(i, i + 1) for i in range(count - 1) if i...  90.1 us
    dot_general x16, matrix products, nn(): return jnp.dot(a, b, preferred_element_type=F32)  81.6 us
    dot_general x24, matrix products, tn(): lax.dot_general(a, b, (((0,), (0,)), ((), ())), preferred_element_type=F32)  73 us
    dot_general x16, matrix products, nt(): lax.dot_general(a, b, (((1,), (1,)), ((), ())), preferred_element_type=F32)  71.3 us
  transfers between devices with their start and end apart: 113, of which 44 were waited for; matrix products, arithmetic and copies ran while one was open for 39% of the time, Pallas kernels for 0%

profile of v1, /device:TPU:0, one launch (start us, length us, event | category | flops | bytes accessed | tf_op | source)
XLA Modules:
  0.0 1888.9 jit_solution(16025462588871716311)
XLA Ops:
  22.9 31.5 %all-gather.22.cloned.1.call-done = bf16[7424,128]{1,0:T(8,128)(2,1)} async-done(((bf16[464,128]{1,0:T(8,128)(2,1)}), bf16[7424,128]{1,0:T(8,128)(2,1)}) %all-gather.22.cloned.1.call-update) | async-done | bytes 1900560 | tf_op jit(solution)/shard_map/all_gather | solution.py:254
  86.5 44.3 %all-gather.28.cloned.1.call-done = bf16[1,2048,2048]{2,1,0:T(8,128)(2,1)} async-done(((bf16[1,128,2048]{2,1,0:T(8,128)(2,1)}), bf16[1,2048,2048]{2,1,0:T(8,128)(2,1)}) %all-gather.28.cloned.1.call-update) | async-done | bytes 8388624 | tf_op jit(solution)/shard_map/all_gather | solution.py:234
  143.1 63.6 %all-gather.26.cloned.1.call-done = bf16[1,2048,2048]{2,1,0:T(8,128)(2,1)} async-done(((bf16[1,128,2048]{2,1,0:T(8,128)(2,1)}), bf16[1,2048,2048]{2,1,0:T(8,128)(2,1)}) %all-gather.26.cloned.1.call-update) | async-done | bytes 8388624 | tf_op jit(solution)/shard_map/all_gather | solution.py:234
  235.2 46.7 %all-gather.24.cloned.1.call-done = bf16[1,2048,2048]{2,1,0:T(8,128)(2,1)} async-done(((bf16[1,128,2048]{2,1,0:T(8,128)(2,1)}), bf16[1,2048,2048]{2,1,0:T(8,128)(2,1)}) %all-gather.24.cloned.1.call-update) | async-done | bytes 8388624 | tf_op jit(solution)/shard_map/all_gather | solution.py:234
  304.4 55.6 %all_to_all.20 = f32[32,65,128]{2,1,0:T(8,128)S(1)} all-to-all(f32[32,65,128]{2,1,0:T(8,128)S(1)} %pad_maximum_fusion.7), channel_id=1, replica_groups=mesh['y'=2,'z'=4,'x'=2,'core'=2] {'y','z','x','core'}, dimensions={0} | all-to-all | bytes 2129920 | tf_op jit(solution)/shard_map/all_to_all | solution.py:147
  482.4 18.2 collective-permute-done.3
  500.7 76.8 %all-gather.20.cloned.1.call-done = bf16[3584,2048]{1,0:T(8,128)(2,1)} async-done(((bf16[224,2048]{1,0:T(8,128)(2,1)}), bf16[3584,2048]{1,0:T(8,128)(2,1)}) %all-gather.20.cloned.1.call-update) | async-done | bytes 14680080 | tf_op jit(solution)/shard_map/all_gather | solution.py:234
  586.5 108.5 %all-gather.18.cloned.1.call-done = bf16[2048,3584]{0,1:T(8,128)(2,1)} async-done(((bf16[128,3584]{0,1:T(8,128)(2,1)}), bf16[2048,3584]{0,1:T(8,128)(2,1)}) %all-gather.18.cloned.1.call-update) | async-done | bytes 14680080 | tf_op jit(solution)/shard_map/all_gather | solution.py:234
  695.0 15.1 multiply_convert_fusion.1
  750.5 19.8 %all-gather.16.cloned.1.call-done = bf16[2048,2048]{1,0:T(8,128)(2,1)} async-done(((bf16[128,2048]{1,0:T(8,128)(2,1)}), bf16[2048,2048]{1,0:T(8,128)(2,1)}) %all-gather.16.cloned.1.call-update) | async-done | bytes 8388624 | tf_op jit(solution)/shard_map/all_gather | solution.py:234
  818.3 15.9 multiply_convert_fusion
  846.0 18.0 collective-permute-done.91
  985.4 116.5 %all-to-all-start.2 = ((f32[32,65,128]{2,1,0:T(8,128)}), f32[32,65,128]{2,1,0:T(8,128)S(1)}, u32[]{:S(2)}, u32[]{:S(2)}) async-start(f32[32,65,128]{2,1,0:T(8,128)} %pad_maximum_fusion.6), calls=%async_computation.2 | async-start | bytes 2359296 | tf_op jit(solution)/shard_map/all_to_all | solution.py:147
  1118.3 12.4 fusion.46
  1226.4 11.8 collective-permute-done.82
  1274.8 41.6 %collective-permute-done.62 = bf16[1024,1024]{1,0:T(8,128)(2,1)} collective-permute-done((bf16[1024,1024]{1,0:T(8,128)(2,1)}, bf16[1024,1024]{1,0:T(8,128)(2,1)}, u32[]{:S(2)}, u32[]{:S(2)}) %collective-permute-start.62) | collective-permute-done | bytes 2097184 | tf_op jit(solution)/shard_map/ppermute | solution.py:37
  1351.9 21.1 %collective-permute-done.53 = bf16[256,1024]{1,0:T(8,128)(2,1)S(1)} collective-permute-done((bf16[256,1024]{1,0:T(8,128)(2,1)S(1)}, bf16[256,1024]{1,0:T(8,128)(2,1)S(1)}, u32[]{:S(2)}, u32[]{:S(2)}) %collective-permute-start.53) | collective-permute-done | bytes 524320 | tf_op jit(solution)/shard_map/ppermute | solution.py:71
  1410.3 17.7 fusion.403
  1446.5 28.4 %negate_add_fusion = f32[2,128,32,64]{3,2,1,0:T(8,128)} fusion(f32[2,1,32,64]{3,2,1,0:T(8,128)S(1)} %add_bitcast_fusion, f32[2,128,32,64]{3,2,1,0:T(8,128)} %get-tuple-element.90, f32[2,1,32,64]{3,2,1,0:T(8,128)S(1)} %fusion.356, f32[2,128,32,64]{3,2,1,0:T(8,128)} %get-tuple-element.69, f32[2,128,32,64]{3,2,1,0:T(8,128)} %get-tuple-element.101, ...), kind=kOutput, calls=%fused_computation.64 | output fusion | flops 77070336 | bytes 14729216 | tf_op jit(solution)/shard_map/transpose(jvp(jit(cumsum)))/reduce_window_sum | solution.py:162
  1559.6 13.6 concatenate.168
  1612.2 13.2 collective-permute-done.57
  1670.6 37.8 %collective-permute-done.29 = bf16[1024,1024]{1,0:T(8,128)(2,1)S(1)} collective-permute-done((bf16[1024,1024]{1,0:T(8,128)(2,1)}, bf16[1024,1024]{1,0:T(8,128)(2,1)S(1)}, u32[]{:S(2)}, u32[]{:S(2)}) %collective-permute-start.29) | collective-permute-done | bytes 2097184 | tf_op jit(solution)/shard_map/ppermute | solution.py:37
  1710.6 42.5 %collective-permute-done.40 = bf16[1024,1024]{1,0:T(8,128)(2,1)S(1)} collective-permute-done((bf16[1024,1024]{1,0:T(8,128)(2,1)}, bf16[1024,1024]{1,0:T(8,128)(2,1)S(1)}, u32[]{:S(2)}, u32[]{:S(2)}) %collective-permute-start.40) | collective-permute-done | bytes 2097184 | tf_op jit(solution)/shard_map/ppermute | solution.py:37
  1823.7 13.8 collective-permute-start.43
  (964 shorter events, 986.0 us)
Async XLA Ops:
  8.9 121.9 %all-gather.28.cloned.1.call-start = ((), (), s32[]{:S(2)}) async-start(), calls=%async_computation.12 | async-start | bytes 8912896 | tf_op jit(solution)/shard_map/all_gather | solution.py:234
  12.2 194.5 %all-gather.26.cloned.1.call-start = ((), (), s32[]{:S(2)}) async-start(), calls=%async_computation.11 | async-start | bytes 8912896 | tf_op jit(solution)/shard_map/all_gather | solution.py:234
  12.9 269.0 %all-gather.24.cloned.1.call-start = ((), (), s32[]{:S(2)}) async-start(), calls=%async_computation.10 | async-start | bytes 8912896 | tf_op jit(solution)/shard_map/all_gather | solution.py:234
  13.5 436.3 %all-gather.30.cloned.1.call-start = ((), (), s32[]{:S(2)}) async-start(), calls=%async_computation.13 | async-start | bytes 8912896 | tf_op jit(solution)/shard_map/all_gather | solution.py:234
  14.1 448.4 %all-gather.32.cloned.1.call-start = ((), (), s32[]{:S(2)}) async-start(), calls=%async_computation.14 | async-start | bytes 8912896 | tf_op jit(solution)/shard_map/all_gather | solution.py:234
  14.7 562.8 %all-gather.20.cloned.1.call-start = ((), (), s32[]{:S(2)}) async-start(), calls=%async_computation.7 | async-start | bytes 15597568 | tf_op jit(solution)/shard_map/all_gather | solution.py:234
  15.8 679.1 %all-gather.18.cloned.1.call-start = ((), (), s32[]{:S(2)}) async-start(), calls=%async_computation.6 | async-start | bytes 15597568 | tf_op jit(solution)/shard_map/all_gather | solution.py:234
  374.1 396.1 %all-gather.16.cloned.1.call-start = ((), (), s32[]{:S(2)}) async-start(), calls=%async_computation.5 | async-start | bytes 8912896 | tf_op jit(solution)/shard_map/all_gather | solution.py:234
  482.4 104.1 %collective-permute-start.2 = (bf16[256,2048]{1,0:T(8,128)(2,1)S(1)}, bf16[256,2048]{1,0:T(8,128)(2,1)}, u32[]{:S(2)}, u32[]{:S(2)}) collective-permute-start(bf16[256,2048]{1,0:T(8,128)(2,1)S(1)} %get-tuple-element.77), channel_id=1, source_target_pairs={{0,1},{1,0},{2,3},{3,2},{4,5},{5,4},{6,7},{7,6},{8,9},{9,8},{10,11... | collective-permute-start | bytes 3145736 | tf_op jit(solution)/shard_map/ppermute | solution.py:37
  893.4 270.0 %collective-permute-start.72 = (bf16[1024,1792]{1,0:T(8,128)(2,1)}, bf16[1024,1792]{1,0:T(8,128)(2,1)}, u32[]{:S(2)}, u32[]{:S(2)}) collective-permute-start(bf16[1024,1792]{1,0:T(8,128)(2,1)} %convolution_convert_fusion), channel_id=1, source_target_pairs={{0,2},{2,0},{1,3},{3,1},{4,6},{6,4},{5,7},{7,5},{8,10},{10,8},{9,1... | collective-permute-start | bytes 11010056 | tf_op jit(solution)/shard_map/ppermute | solution.py:37
  913.1 263.9 %collective-permute-start.81 = (bf16[896,2048]{1,0:T(8,128)(2,1)}, bf16[896,2048]{1,0:T(8,128)(2,1)}, u32[]{:S(2)}, u32[]{:S(2)}) collective-permute-start(bf16[896,2048]{1,0:T(8,128)(2,1)} %convolution_convert_fusion.1), channel_id=1, source_target_pairs={{0,2},{2,0},{1,3},{3,1},{4,6},{6,4},{5,7},{7,5},{8,10},{10,8},{9,1... | collective-permute-start | bytes 11010056 | tf_op jit(solution)/shard_map/ppermute | solution.py:37
  937.2 267.9 %collective-permute-start.99 = (f32[128,1024]{1,0:T(8,128)S(1)}, f32[128,1024]{1,0:T(8,128)}, u32[]{:S(2)}, u32[]{:S(2)}) collective-permute-start(f32[128,1024]{1,0:T(8,128)S(1)} %constant_dynamic-slice_fusion), channel_id=1, source_target_pairs={{0,1},{1,0},{2,3},{3,2},{4,5},{5,4},{6,7},{7,6},{8,9},{9,8},{10,11... | collective-permute-start | bytes 1572872 | tf_op jit(solution)/shard_map/ppermute | solution.py:37
  985.4 260.5 %all-to-all-start.2 = ((f32[32,65,128]{2,1,0:T(8,128)}), f32[32,65,128]{2,1,0:T(8,128)S(1)}, u32[]{:S(2)}, u32[]{:S(2)}) async-start(f32[32,65,128]{2,1,0:T(8,128)} %pad_maximum_fusion.6), calls=%async_computation.2 | async-start | bytes 2359296 | tf_op jit(solution)/shard_map/all_to_all | solution.py:147
  1208.8 112.2 %collective-permute-start.85 = (bf16[224,2048]{1,0:T(8,128)(2,1)}, bf16[224,2048]{1,0:T(8,128)(2,1)}, u32[]{:S(2)}, u32[]{:S(2)}) collective-permute-start(bf16[224,2048]{1,0:T(8,128)(2,1)} %get-tuple-element.119), channel_id=1, source_target_pairs={{12,8},{13,9},{14,10},{15,11},{28,24},{29,25},{30,26},{31,27}} | collective-permute-start | bytes 2752520 | tf_op jit(solution)/shard_map/ppermute | solution.py:72
  1219.5 96.9 %collective-permute-start.62 = (bf16[1024,1024]{1,0:T(8,128)(2,1)}, bf16[1024,1024]{1,0:T(8,128)(2,1)}, u32[]{:S(2)}, u32[]{:S(2)}) collective-permute-start(bf16[1024,1024]{1,0:T(8,128)(2,1)} %convolution_convert_fusion.3), channel_id=1, source_target_pairs={{0,2},{2,0},{1,3},{3,1},{4,6},{6,4},{5,7},{7,5},{8,10},{10,8},{9,1... | collective-permute-start | bytes 6291464 | tf_op jit(solution)/shard_map/ppermute | solution.py:37
  1254.3 137.0 %all-to-all-start.3 = ((f32[32,64,128]{2,1,0:T(8,128)}), f32[32,64,128]{2,1,0:T(8,128)S(1)}, u32[]{:S(2)}, u32[]{:S(2)}) async-start(f32[32,64,128]{2,1,0:T(8,128)} %chain.3), calls=%async_computation.3 | async-start | bytes 2097152 | tf_op jit(solution)/shard_map/all_to_all | solution.py:158
  1257.1 614.9 %reduce-scatter.2.cloned.1.call-start = ((), (), s32[]{:S(2)}) async-start(), calls=%async_computation.8 | async-start | bytes 4038656 | tf_op jit(solution)/shard_map/reduce_scatter | solution.py:396
  1330.9 246.8 %collective-permute-start.84 = (bf16[224,2048]{1,0:T(8,128)(2,1)}, bf16[224,2048]{1,0:T(8,128)(2,1)}, u32[]{:S(2)}, u32[]{:S(2)}) collective-permute-start(bf16[224,2048]{1,0:T(8,128)(2,1)} %get-tuple-element.116), channel_id=1, source_target_pairs={{0,4},{4,8},{8,12},{1,5},{5,9},{9,13},{2,6},{6,10},{10,14},{3,7},{... | collective-permute-start | bytes 2752520 | tf_op jit(solution)/shard_map/ppermute | solution.py:71
  1373.1 206.8 %collective-permute-start.87 = (bf16[224,2048]{1,0:T(8,128)(2,1)}, bf16[224,2048]{1,0:T(8,128)(2,1)}, u32[]{:S(2)}, u32[]{:S(2)}) collective-permute-start(bf16[224,2048]{1,0:T(8,128)(2,1)} %fusion.111), channel_id=1, source_target_pairs={{4,0},{8,4},{12,8},{5,1},{9,5},{13,9},{6,2},{10,6},{14,10},{7,3},{... | collective-permute-start | bytes 2752520 | tf_op jit(solution)/shard_map/ppermute | solution.py:72
  1375.8 206.7 %collective-permute-start.56 = (bf16[256,1024]{1,0:T(8,128)(2,1)}, bf16[256,1024]{1,0:T(8,128)(2,1)}, u32[]{:S(2)}, u32[]{:S(2)}) collective-permute-start(bf16[256,1024]{1,0:T(8,128)(2,1)} %get-tuple-element.163), channel_id=1, source_target_pairs={{8,4},{12,8},{9,5},{13,9},{10,6},{14,10},{11,7},{15,11},{24,20},{2... | collective-permute-start | bytes 1572872 | tf_op jit(solution)/shard_map/ppermute | solution.py:72
  1382.7 227.5 %collective-permute-start.54 = (bf16[256,1024]{1,0:T(8,128)(2,1)}, bf16[256,1024]{1,0:T(8,128)(2,1)}, u32[]{:S(2)}, u32[]{:S(2)}) collective-permute-start(bf16[256,1024]{1,0:T(8,128)(2,1)} %get-tuple-element.162), channel_id=1, source_target_pairs={{0,4},{4,8},{8,12},{1,5},{5,9},{9,13},{2,6},{6,10},{10,14},{3,7},{... | collective-permute-start | bytes 1572872 | tf_op jit(solution)/shard_map/ppermute | solution.py:71
  1627.0 126.1 %collective-permute-start.40 = (bf16[1024,1024]{1,0:T(8,128)(2,1)}, bf16[1024,1024]{1,0:T(8,128)(2,1)S(1)}, u32[]{:S(2)}, u32[]{:S(2)}) collective-permute-start(bf16[1024,1024]{1,0:T(8,128)(2,1)} %convolution_convert_fusion.5), channel_id=1, source_target_pairs={{0,2},{2,0},{1,3},{3,1},{4,6},{6,4},{5,7},{7,5},{8,10},{10,8},{9,1... | collective-permute-start | bytes 6291464 | tf_op jit(solution)/shard_map/ppermute | solution.py:37
  1656.3 103.3 %collective-permute-start.59 = (f32[128,1024]{1,0:T(8,128)S(1)}, f32[128,1024]{1,0:T(8,128)S(1)}, u32[]{:S(2)}, u32[]{:S(2)}) collective-permute-start(f32[128,1024]{1,0:T(8,128)S(1)} %constant_dynamic-slice_fusion.22), channel_id=1, source_target_pairs={{0,1},{1,0},{2,3},{3,2},{4,5},{5,4},{6,7},{7,6},{8,9},{9,8},{10,11... | collective-permute-start | bytes 1572872 | tf_op jit(solution)/shard_map/ppermute | solution.py:37
  1665.5 155.8 %collective-permute-start.70 = (f32[128,1024]{1,0:T(8,128)S(1)}, f32[128,1024]{1,0:T(8,128)S(1)}, u32[]{:S(2)}, u32[]{:S(2)}) collective-permute-start(f32[128,1024]{1,0:T(8,128)S(1)} %constant_dynamic-slice_fusion.19), channel_id=1, source_target_pairs={{0,1},{1,0},{2,3},{3,2},{4,5},{5,4},{6,7},{7,6},{8,9},{9,8},{10,11... | collective-permute-start | bytes 1572872 | tf_op jit(solution)/shard_map/ppermute | solution.py:37
  (313 other events, 6855.3 us)
Sparse Core Ops, SparseCore 0:
  10.8 43.5 all-gather.21
  57.1 73.6 all-gather.27
  133.5 73.1 all-gather.25
  208.7 73.1 all-gather.23
  283.9 88.2 all-gather.29
  374.2 88.2 all-gather.31
  464.9 112.6 all-gather.19
  579.7 115.2 all-gather.17
  697.1 73.0 all-gather.15
  1573.4 87.2 reduce-scatter.1

commit v2 on v1

v2 whole, which is shorter than its diff:
```python
import jax
import jax.numpy as jnp
from jax import lax
from jax.experimental import pallas as pl
from jax.experimental.pallas import tpu as pltpu
from jax.sharding import Mesh
from jax.sharding import PartitionSpec as P

HEAD = 64
RANK = 32
MIXCOLS = 5 * RANK
LANES = 128
F32, BF16 = jnp.float32, jnp.bfloat16
WIDE = ("z", "x", "core")
ALL = ("y", "z", "x", "core")


def nn(a, b):
    return jnp.dot(a, b, preferred_element_type=F32)


def nt(a, b):
    return lax.dot_general(a, b, (((1,), (1,)), ((), ())), preferred_element_type=F32)


def tn(a, b):
    return lax.dot_general(a, b, (((0,), (0,)), ((), ())), preferred_element_type=F32)


def low(a):
    return a.astype(BF16)


def swap(value, axis):
    return lax.ppermute(value, axis, [(0, 1), (1, 0)])


def along(value, step):
    count = lax.axis_size(ALL)
    if step > 0:
        pairs = [(i, i + 1) for i in range(count - 1)]
    else:
        pairs = [(i + 1, i) for i in range(count - 1)]
    return lax.ppermute(value, ALL, pairs)


def piece(value, index, size, axis):
    start = [0] * value.ndim
    start[axis] = index * size
    shape = list(value.shape)
    shape[axis] = size
    return lax.dynamic_slice(value, start, shape)


def line_sum(block):
    count = lax.axis_size("z")
    place = lax.axis_index("z")

    def own(index):
        return lax.dynamic_index_in_dim(block, jnp.clip(index, 0, count - 1), 0, False).astype(F32)

    up = down = None
    for t in range(1, count):
        right = own(count - t + place)
        left = own(place + t - count)
        if up is not None:
            right = right + up.astype(F32)
            left = left + down.astype(F32)
        up = lax.ppermute(low(right), "z", [(i, i + 1) for i in range(count - 1) if i <= t - 1])
        down = lax.ppermute(
            low(left), "z", [(i, i - 1) for i in range(1, count) if count - 1 - i <= t - 1]
        )
    return own(place) + up.astype(F32) + down.astype(F32)


def small_sum(value):
    z, rows = lax.axis_size("z"), value.shape[0]
    for axis in ("core", "x"):
        place = lax.axis_index(axis)
        parts = value.reshape(rows, z, 2, -1) if axis == "x" else value.reshape(rows, 2 * z, 2, -1)
        give = lax.dynamic_index_in_dim(parts, 1 - place, 2, False).reshape(rows, -1)
        keep = lax.dynamic_index_in_dim(parts, place, 2, False).reshape(rows, -1)
        value = keep + swap(give if axis == "core" else low(give), axis).astype(F32)
    value = line_sum(jnp.swapaxes(value.reshape(rows, z, -1), 0, 1))
    return value + swap(value, "y")


def quarter_cols(right):
    y, core = lax.axis_index("y"), lax.axis_index("core")
    half = right.shape[2] // 2
    near = piece(right, y, half, 2)
    across = swap(piece(right, 1 - y, half, 2), "y")
    both = jnp.concatenate([near, across], 0)
    mine = piece(both, core, half // 2, 2)
    other = swap(piece(both, 1 - core, half // 2, 2), "core")
    rows = right.shape[0]
    return jnp.concatenate([mine[:rows], other[:rows], mine[rows:], other[rows:]], 0)


def spread_cols(part):
    y, core = lax.axis_index("y"), lax.axis_index("core")
    rows = part.shape[0] // 2
    keep = piece(part, core, rows, 0)
    give = swap(piece(part, 1 - core, rows, 0), "core")
    first = core == 0
    part = jnp.stack([jnp.where(first, keep, give), jnp.where(first, give, keep)], 0)
    other = swap(part, "y")
    first = y == 0
    part = jnp.stack([jnp.where(first, part, other), jnp.where(first, other, part)], 0)
    part = part.transpose(3, 2, 0, 1, 4)
    return part.reshape(part.shape[0], rows, -1).astype(F32)


def quad_grads(lefts, rights):
    right = quarter_cols(jnp.stack(rights, 1))
    quarter = right.shape[2]
    parts = [low(tn(a, right[:, i])) for i, a in enumerate(lefts)]
    part = jnp.concatenate(parts, 1)
    part = lax.psum_scatter(part, ("z", "x"), scatter_dimension=0, tiled=True)
    return spread_cols(part.reshape(part.shape[0], len(lefts), quarter))


def group_many(values):
    value = jnp.stack(values, 0)
    near = swap(value, "core")
    across = swap(value, "y")
    far = swap(across, "core")
    return [jnp.concatenate([v[i] for v in (value, near, across, far)], 0) for i in range(len(values))]


def group_sum(value):
    rows = value.shape[0] // 4
    pair = value.reshape(2, 2, rows, -1)
    got = swap(pair[:, 1], "core")
    across = swap(low(pair[1, 0].astype(F32) + got[1].astype(F32)), "y")
    return pair[0, 0].astype(F32) + got[0].astype(F32) + across.astype(F32)


SPAN = 256
GROUP = SPAN // HEAD
SUB = 32


def lane_head(shape, dim):
    return lax.broadcasted_iota(jnp.int32, shape, dim) // HEAD


def head_block(rows, cols):
    shape = (rows, cols)
    return jnp.where(lane_head(shape, 0) == lane_head(shape, 1), 1.0, 0.0).astype(BF16)


def head_sum(value):
    coarse = low(value)
    fine = low(value - coarse.astype(F32))
    ones = head_block(SPAN, SPAN)
    return nn(coarse, ones) + nn(fine, ones)


def exact_product(left, value):
    coarse = low(value)
    rest = value - coarse.astype(F32)
    fine = low(rest)
    last = low(rest - fine.astype(F32))
    return nn(left, coarse) + (nn(left, fine) + nn(left, last))


def triangle(length, keep):
    shape = (length, length)
    row = lax.broadcasted_iota(jnp.int32, shape, 0)
    col = lax.broadcasted_iota(jnp.int32, shape, 1)
    return jnp.where(keep(row, col), 1.0, 0.0).astype(BF16)


def spread_heads(value):
    lane = lane_head(value.shape, 1)
    return jnp.concatenate([low(jnp.where(lane == h, value, 0.0)) for h in range(GROUP)], 0)


def pick_heads(value):
    rows = value.shape[0] // GROUP
    lane = lane_head((rows, SPAN), 1)
    out = value[:rows]
    for h in range(1, GROUP):
        out = jnp.where(lane == h, value[h * rows : (h + 1) * rows], out)
    return out


def widen_state(ref):
    state = jnp.concatenate([ref[0, 0], ref[0, 1]], 1)
    return jnp.concatenate(
        [jnp.where(lane_head(state.shape, 1) == h, state, jnp.zeros_like(state)) for h in range(GROUP)], 0
    )


def store_state(ref, value):
    state = low(pick_heads(value))
    ref[0, 0] = state[:, :LANES]
    ref[0, 1] = state[:, LANES:]


def exclusive_of(inclusive):
    return jnp.concatenate([jnp.zeros_like(inclusive[:1]), inclusive[:-1]], 0)


def cap(value):
    return jnp.exp(jnp.minimum(value, 80.0))


def state_kernel(key_ref, value_ref, log_ref, inc_ref, state_ref, final_ref):
    length = log_ref.shape[0]
    inclusive = exact_product(triangle(length, lambda r, c: r >= c), log_ref[...])
    inc_ref[...] = inclusive
    final = inclusive[length - 1 :]
    weighted = low(key_ref[...] * jnp.exp(final - inclusive))
    store_state(state_ref, tn(weighted, low(value_ref[...])))
    coarse = low(final)
    fine = low(final - coarse.astype(F32))
    rows = jnp.concatenate([coarse, fine, jnp.zeros((14, SPAN), BF16)], 0)
    final_ref[0, 0] = rows[:, :LANES]
    final_ref[0, 1] = rows[:, LANES:]


def sub_block(q, inclusive, exclusive, length):
    start, stop = q * SUB, (q + 1) * SUB
    middle = inclusive[start + SUB // 2 - 1 : start + SUB // 2]
    query = cap(exclusive[start:stop] - middle)
    key = cap(middle - inclusive[:stop])
    shape = (GROUP * SUB, stop)
    row = lax.rem(lax.broadcasted_iota(jnp.int32, shape, 0), SUB) + start
    mask = row > lax.broadcasted_iota(jnp.int32, shape, 1)
    return start, stop, query, key, mask


def wkv_kernel(rec_ref, key_ref, value_ref, inc_ref, state_ref, gate_ref, row_ref, wkv_ref, gated_ref):
    length = rec_ref.shape[0]
    inclusive = inc_ref[...]
    exclusive = exclusive_of(inclusive)
    rec, key, value = rec_ref[...], key_ref[...], value_ref[...]
    value_low = low(value)
    bonus, gain, bias = row_ref[9:10], row_ref[10:11], row_ref[11:12]
    answer = nn(low(rec * jnp.exp(exclusive)), widen_state(state_ref))
    answer = answer + head_sum(rec * bonus * key) * value
    parts = []
    for q in range(length // SUB):
        start, stop, query, fade, mask = sub_block(q, inclusive, exclusive, length)
        left = spread_heads(rec[start:stop] * query)
        scores = nt(left, low(key[:stop] * fade))
        scores = low(jnp.where(mask, scores, 0.0))
        parts.append(pick_heads(nn(scores, value_low[:stop])))
    answer = answer + jnp.concatenate(parts, 0)
    wkv_ref[...] = answer
    centered = answer - head_sum(answer) * (1.0 / HEAD)
    spread = head_sum(centered * centered) * (1.0 / HEAD)
    grouped = centered * lax.rsqrt(spread + 0.00064) * gain + bias
    gate = gate_ref[...]
    gated_ref[...] = low(grouped * gate / (1.0 + jnp.exp(-gate)))


def gate_back_kernel(grad_ref, wkv_ref, gate_ref, rec_ref, inc_ref, row_ref, gwkv_ref, ggate_ref, state_ref, sum_ref):
    gain, bias = row_ref[10:11], row_ref[11:12]
    answer, gate, grad = wkv_ref[...], gate_ref[...], grad_ref[...]
    centered = answer - head_sum(answer) * (1.0 / HEAD)
    rstd = lax.rsqrt(head_sum(centered * centered) * (1.0 / HEAD) + 0.00064)
    hat = centered * rstd
    grouped = hat * gain + bias
    sig = 1.0 / (1.0 + jnp.exp(-gate))
    g_grouped = grad * gate * sig
    ggate_ref[...] = low(grad * grouped * sig * (1.0 + gate * (1.0 - sig)))
    g_gain = jnp.sum(g_grouped * hat, 0, keepdims=True)
    g_bias = jnp.sum(g_grouped, 0, keepdims=True)
    sum_ref[0] = jnp.concatenate([g_gain, g_bias, jnp.zeros((6, SPAN), F32)], 0)
    g_hat = g_grouped * gain
    back = rstd * (
        g_hat - head_sum(g_hat) * (1.0 / HEAD) - hat * (head_sum(g_hat * hat) * (1.0 / HEAD))
    )
    back = low(back)
    gwkv_ref[...] = back
    query = low(rec_ref[...] * jnp.exp(exclusive_of(inc_ref[...])))
    store_state(state_ref, tn(query, back))


def wkv_back_kernel(
    rec_ref, key_ref, value_ref, inc_ref, log_ref, state_ref, gstate_ref, gwkv_ref, row_ref,
    grec_ref, gkey_ref, gvalue_ref, gdecay_ref, sum_ref, key_acc, value_acc, pair_acc,
):
    length = rec_ref.shape[0]
    inclusive = inc_ref[...]
    exclusive = exclusive_of(inclusive)
    final = inclusive[length - 1 :]
    rec, key, value = rec_ref[...], key_ref[...], value_ref[...]
    value_low = low(value)
    grad_low = gwkv_ref[...]
    grad = grad_low.astype(F32)
    bonus = row_ref[9:10]
    state, gstate = widen_state(state_ref), widen_state(gstate_ref)
    pair = head_sum(grad * value)
    shared = pair * bonus
    g_key = shared * rec
    g_value = head_sum(rec * bonus * key) * grad
    g_bonus = jnp.sum(rec * key * pair, 0, keepdims=True)
    fade = jnp.exp(exclusive)
    back = nt(grad_low, state)
    from_state = low(rec * fade).astype(F32) * back
    g_rec = shared * key + fade * back
    fade = jnp.exp(final - inclusive)
    weighted = low(key * fade)
    back = nt(value_low, gstate)
    to_state = weighted.astype(F32) * back
    key_acc[...] = g_key + fade * back
    value_acc[...] = g_value + nn(weighted, gstate)
    pair_acc[...] = jnp.zeros_like(pair_acc)
    rec_parts, own_parts = [], []
    for q in range(length // SUB):
        start, stop, query, fade, mask = sub_block(q, inclusive, exclusive, length)
        left = rec[start:stop] * query
        spread = spread_heads(left)
        right = low(key[:stop] * fade)
        gspread = spread_heads(grad[start:stop])
        scores = low(jnp.where(mask, nt(spread, right), 0.0))
        weight = low(jnp.where(mask, nt(gspread, value_low[:stop]), 0.0))
        back = pick_heads(nn(weight, right))
        rec_parts.append(g_rec[start:stop] + query * back)
        own_parts.append(low(left).astype(F32) * back)
        back = tn(weight, spread)
        key_acc[:stop] += fade * back
        pair_acc[:stop] += right.astype(F32) * back
        value_acc[:stop] += tn(scores, gspread)
    grec_ref[...] = low(jnp.concatenate(rec_parts, 0))
    gkey_ref[...] = low(key_acc[...])
    gvalue_ref[...] = low(value_acc[...])
    inner, pairs = jnp.concatenate(own_parts, 0), pair_acc[...]
    both = head_sum(
        jnp.concatenate([state_ref[0, 0], state_ref[0, 1]], 1).astype(F32)
        * jnp.concatenate([gstate_ref[0, 0], gstate_ref[0, 1]], 1).astype(F32)
    )
    shape = both.shape
    here = lax.rem(lax.broadcasted_iota(jnp.int32, shape, 1), HEAD) == lax.broadcasted_iota(
        jnp.int32, shape, 0
    )
    through = jnp.exp(final) * jnp.sum(jnp.where(here, both, 0.0), 0, keepdims=True)
    later = exact_product(triangle(length, lambda r, c: r < c), inner + from_state - pairs)
    earlier = exact_product(triangle(length, lambda r, c: r > c), to_state)
    g_log = later - pairs + earlier + through
    g_decay = g_log * log_ref[...]
    gdecay_ref[...] = low(g_decay)
    sum_ref[0] = jnp.concatenate(
        [g_bonus, jnp.sum(g_decay, 0, keepdims=True), jnp.zeros((6, SPAN), F32)], 0
    )


def wkv_call(kernel, seqs, ins, outs, name, flops, scratch=()):
    width = ins[0].shape[1]
    length = ins[0].shape[0] // seqs

    def spec(a):
        if len(a.shape) == 4:
            return pl.BlockSpec((1, 2, a.shape[2], LANES), lambda s, g: (s, g, 0, 0))
        if len(a.shape) == 3:
            return pl.BlockSpec((1, 8, SPAN), lambda s, g: (s, 0, g))
        if a.shape[0] == 16:
            return pl.BlockSpec((16, SPAN), lambda s, g: (0, g))
        return pl.BlockSpec((length, SPAN), lambda s, g: (s, g))

    moved = sum(a.size * a.dtype.itemsize for a in ins + outs)
    return pl.pallas_call(
        kernel,
        grid=(seqs, width // SPAN),
        in_specs=[spec(a) for a in ins],
        out_specs=[spec(a) for a in outs],
        out_shape=outs,
        scratch_shapes=scratch,
        compiler_params=pltpu.CompilerParams(vmem_limit_bytes=40 << 20),
        cost_estimate=pl.CostEstimate(flops=flops, transcendentals=0, bytes_accessed=moved),
        name=name,
    )(*ins)


def chain_kernel(first_ref, packed_ref, out_ref, held_fade, *, rows, reverse):
    count = packed_ref.shape[0]
    logs = packed_ref[:, rows : rows + 1], packed_ref[:, rows + 1 : rows + 2]
    shape = (count, rows, LANES)
    lane = lax.rem(lax.broadcasted_iota(jnp.int32, shape, 2), HEAD)
    here = lane == lax.broadcasted_iota(jnp.int32, shape, 1) + first_ref[0]
    ones = head_block(LANES, LANES)
    total = None
    for part in logs:
        part = jnp.where(here, part.astype(F32), 0.0)
        part = nn(low(part.reshape(count * rows, LANES)), ones)
        total = part if total is None else total + part
    held_fade[...] = jnp.exp(total).reshape(shape)

    def one(hop, held):
        b = count - 1 - hop if reverse else hop
        out_ref[b] = low(held)
        return held_fade[b] * held + packed_ref[b, :rows].astype(F32)

    lax.fori_loop(0, count, one, jnp.zeros((rows, LANES), F32))


def chain(state, finals, reverse):
    count = lax.axis_size(ALL)
    pairs = state.shape[0] * state.shape[1]
    split = count // pairs
    rows = state.shape[2] // split
    logs = finals.reshape(pairs, finals.shape[2], LANES)
    if split > 1:
        logs = jnp.repeat(logs, split, axis=0)
    packed = jnp.concatenate([state.reshape(count, rows, LANES), logs], 1)
    packed = lax.all_to_all(packed, ALL, 0, 0, tiled=True)
    first = lax.rem(lax.axis_index(ALL), split) * rows
    entering = pl.pallas_call(
        lambda *refs: chain_kernel(*refs, rows=rows, reverse=reverse),
        grid_spec=pltpu.PrefetchScalarGridSpec(
            num_scalar_prefetch=1,
            grid=(1,),
            in_specs=[pl.BlockSpec(packed.shape, lambda i, c: (0, 0, 0))],
            out_specs=pl.BlockSpec((count, rows, LANES), lambda i, c: (0, 0, 0)),
            scratch_shapes=[pltpu.VMEM((count, rows, LANES), F32)],
        ),
        out_shape=jax.ShapeDtypeStruct((count, rows, LANES), BF16),
        compiler_params=pltpu.CompilerParams(vmem_limit_bytes=40 << 20),
        name="chain",
    )(first.astype(jnp.int32).reshape(1), packed)
    return lax.all_to_all(entering, ALL, 0, 0, tiled=True).reshape(state.shape)


def norm_forward(values, gain, bias):
    mean = jnp.mean(values, -1, keepdims=True)
    centered = values - mean
    rstd = lax.rsqrt(jnp.mean(centered * centered, -1, keepdims=True) + 1e-05)
    hat = centered * rstd
    return hat * gain + bias, hat, rstd


def norm_backward(grad, hat, rstd, gain):
    d = grad * gain
    back = rstd * (
        d - jnp.mean(d, -1, keepdims=True) - hat * jnp.mean(d * hat, -1, keepdims=True)
    )
    return back, jnp.sum(grad * hat, 0), jnp.sum(grad, 0)


def prior_of(values, seqs):
    shaped = values.reshape(seqs, -1, values.shape[-1])
    incoming = along(shaped[:, -1], 1)
    return jnp.concatenate([incoming[:, None], shaped[:, :-1]], 1).reshape(values.shape)


def prior_back(grad, seqs):
    shaped = grad.reshape(seqs, -1, grad.shape[-1])
    incoming = along(shaped[:, 0], -1)
    return jnp.concatenate([shaped[:, 1:], incoming[:, None]], 1).reshape(grad.shape)


def stack_nn(value, shards, which, tile=512):
    devices, _, rows, cols = shards.shape

    def kernel(a_ref, w_ref, o_ref):
        w = w_ref[...].reshape(devices * rows, tile)
        o_ref[...] = jnp.dot(a_ref[...], w, preferred_element_type=F32)

    return pl.pallas_call(
        kernel,
        grid=(cols // tile,),
        out_shape=jax.ShapeDtypeStruct((value.shape[0], cols), F32),
        in_specs=[
            pl.BlockSpec(value.shape, lambda j: (0, 0)),
            pl.BlockSpec((devices, 1, rows, tile), lambda j: (0, which, 0, j)),
        ],
        out_specs=pl.BlockSpec((value.shape[0], tile), lambda j: (0, j)),
        compiler_params=pltpu.CompilerParams(vmem_limit_bytes=40 << 20),
        cost_estimate=pl.CostEstimate(
            flops=2 * value.size * cols, transcendentals=0,
            bytes_accessed=2 * value.size + 2 * devices * rows * cols + 4 * value.shape[0] * cols,
        ),
        name="stack_nn",
    )(value, shards)


def stack_nt(value, shards, which, tile=512):
    devices, _, rows, cols = shards.shape
    group = tile // rows

    def kernel(a_ref, w_ref, o_ref):
        w = w_ref[...].reshape(tile, cols)
        o_ref[...] = lax.dot_general(
            a_ref[...], w, (((1,), (1,)), ((), ())), preferred_element_type=F32
        )

    return pl.pallas_call(
        kernel,
        grid=(devices // group,),
        out_shape=jax.ShapeDtypeStruct((value.shape[0], devices * rows), F32),
        in_specs=[
            pl.BlockSpec(value.shape, lambda j: (0, 0)),
            pl.BlockSpec((group, 1, rows, cols), lambda j: (j, which, 0, 0)),
        ],
        out_specs=pl.BlockSpec((value.shape[0], tile), lambda j: (0, j)),
        compiler_params=pltpu.CompilerParams(vmem_limit_bytes=40 << 20),
        cost_estimate=pl.CostEstimate(
            flops=2 * value.size * devices * rows, transcendentals=0,
            bytes_accessed=2 * value.size + 2 * devices * rows * cols
            + 4 * value.shape[0] * devices * rows,
        ),
        name="stack_nt",
    )(value, shards)


TILE = 256


def pack_blocks(shard):
    rows, cols = shard.shape
    return jnp.swapaxes(shard.reshape(rows, cols // TILE, TILE), 0, 1).reshape(-1, TILE)


def ffn_call(kernel, core, grid, ins, specs, outs, out_specs, flops, scratch=(), name=None):
    moved = sum(a.size * a.dtype.itemsize for a in ins[:1] + outs) + flops // 1024
    return pl.pallas_call(
        kernel,
        grid_spec=pltpu.PrefetchScalarGridSpec(
            num_scalar_prefetch=1, grid=grid, in_specs=specs, out_specs=out_specs, scratch_shapes=scratch
        ),
        out_shape=outs,
        compiler_params=pltpu.CompilerParams(vmem_limit_bytes=56 << 20),
        cost_estimate=pl.CostEstimate(flops=flops, transcendentals=0, bytes_accessed=moved),
        name=name,
    )(core.reshape(1), *ins)


class PackedWeights:
    def __init__(self, packed, core, ff, width, half, chips):
        self.packed, self.core = packed, core
        self.devices = packed.shape[0]
        self.rows = width // self.devices
        self.quarter, self.width, self.half, self.chips = ff // 4, width, half, chips
        self.blocks = self.quarter // TILE
        self.fast = half % 16 == 0 and self.rows % 16 == 0 and self.rows == 128

    def _plain(self, start, rows, count):
        part = self.packed[:, start : start + rows * count]
        return part.reshape(-1, count, rows, TILE)

    def plain_key(self):
        start = self.half * (self.width // TILE)
        part = self._plain(start, self.rows, 2 * self.blocks)
        part = piece(part, self.core, self.blocks, 1)
        return jnp.swapaxes(part, 1, 2).reshape(self.width, self.quarter)

    def plain_value(self):
        part = self._plain(0, self.half, self.width // TILE)
        part = lax.dynamic_index_in_dim(
            part.reshape(self.chips, 2, *part.shape[1:]), self.core, 1, False
        )
        return jnp.swapaxes(part, 1, 2).reshape(self.quarter, self.width)

    def plain_rec(self):
        start = self.half * (self.width // TILE) + self.rows * 2 * self.blocks
        part = self._plain(start, self.rows, self.width // TILE)
        return jnp.swapaxes(part, 1, 2).reshape(self.width, self.width)

    def key_forward(self, mix):
        if not self.fast:
            relu = low(jnp.maximum(nn(mix, self.plain_key()), 0.0))
            return relu, low(relu.astype(F32) * relu.astype(F32))
        tokens = mix.shape[0]
        first = self.half * (self.width // TILE) // self.rows

        def kernel(c_ref, a_ref, w_ref, relu_ref, sq_ref):
            w = w_ref[...].reshape(self.width, TILE)
            relu = jnp.maximum(jnp.dot(a_ref[...], w, preferred_element_type=F32), 0.0)
            relu_ref[...] = low(relu)
            sq_ref[...] = low(relu * relu)

        out = jax.ShapeDtypeStruct((tokens, self.quarter), BF16)
        spec = pl.BlockSpec((tokens, TILE), lambda n, c: (0, n))
        return ffn_call(
            kernel, self.core, (self.blocks,), [mix, self.packed],
            [pl.BlockSpec(mix.shape, lambda n, c: (0, 0)),
             pl.BlockSpec((self.devices, self.rows, TILE),
                          lambda n, c: (0, first + c[0] * self.blocks + n, 0))],
            [out, out], [spec, spec], 2 * mix.size * self.quarter, name="key_forward",
        )

    def value_forward(self, squared):
        if not self.fast:
            return low(nn(squared, self.plain_value()))
        tokens = squared.shape[0]
        view = self.packed.reshape(self.chips, 2, *self.packed.shape[1:])

        def kernel(c_ref, a_ref, w_ref, o_ref):
            w = w_ref[...].reshape(self.quarter, TILE)
            o_ref[...] = low(jnp.dot(a_ref[...], w, preferred_element_type=F32))

        return ffn_call(
            kernel, self.core, (self.width // TILE,), [squared, view],
            [pl.BlockSpec(squared.shape, lambda m, c: (0, 0)),
             pl.BlockSpec((self.chips, 1, self.half, TILE), lambda m, c: (0, c[0], m, 0))],
            [jax.ShapeDtypeStruct((tokens, self.width), BF16)],
            [pl.BlockSpec((tokens, TILE), lambda m, c: (0, m))],
            2 * squared.size * self.width, name="value_forward",
        )[0]

    def rec_forward(self, mix):
        if not self.fast:
            return jax.nn.sigmoid(nn(mix, self.plain_rec()))
        tokens = mix.shape[0]
        first = self.packed.shape[1] // self.rows - self.width // TILE

        def kernel(c_ref, a_ref, w_ref, o_ref):
            w = w_ref[...].reshape(self.width, TILE)
            o_ref[...] = jax.nn.sigmoid(jnp.dot(a_ref[...], w, preferred_element_type=F32))

        return ffn_call(
            kernel, self.core, (self.width // TILE,), [mix, self.packed],
            [pl.BlockSpec(mix.shape, lambda m, c: (0, 0)),
             pl.BlockSpec((self.devices, self.rows, TILE), lambda m, c: (0, first + m, 0))],
            [jax.ShapeDtypeStruct((tokens, self.width), F32)],
            [pl.BlockSpec((tokens, TILE), lambda m, c: (0, m))],
            2 * mix.size * self.width, name="rec_forward",
        )[0]

    def value_backward(self, grad, relu):
        if not self.fast:
            return low(nt(grad, self.plain_value()) * 2.0 * relu.astype(F32))
        tokens = grad.shape[0]
        view = self.packed.reshape(self.chips, 2, *self.packed.shape[1:])
        count = self.width // TILE
        part = self.chips // 2

        def kernel(c_ref, a_ref, r_ref, w_ref, o_ref, flat):
            w = w_ref[...].reshape(part, count, self.half, TILE)
            for m in range(count):
                flat[:, m * TILE : (m + 1) * TILE] = w[:, m].reshape(part * self.half, TILE)
            back = lax.dot_general(
                a_ref[...], flat[...], (((1,), (1,)), ((), ())), preferred_element_type=F32
            )
            o_ref[...] = low(back * 2.0 * r_ref[...].astype(F32))

        wide = part * self.half
        return ffn_call(
            kernel, self.core, (2,), [grad, relu, view],
            [pl.BlockSpec(grad.shape, lambda i, c: (0, 0)),
             pl.BlockSpec((tokens, wide), lambda i, c: (0, i)),
             pl.BlockSpec((part, 1, count * self.half, TILE), lambda i, c: (i, c[0], 0, 0))],
            [jax.ShapeDtypeStruct((tokens, self.quarter), BF16)],
            [pl.BlockSpec((tokens, wide), lambda i, c: (0, i))],
            2 * grad.size * self.quarter,
            scratch=(pltpu.VMEM((wide, self.width), BF16),), name="value_backward",
        )[0]

    def key_backward(self, grad):
        if not self.fast:
            return low(nt(grad, self.plain_key()))
        tokens = grad.shape[0]
        part = 4
        rows = self.blocks * self.rows
        first = self.half * (self.width // TILE) // rows

        def kernel(c_ref, a_ref, w_ref, o_ref, flat):
            w = w_ref[...].reshape(part, self.blocks, self.rows, TILE)
            for n in range(self.blocks):
                flat[:, n * TILE : (n + 1) * TILE] = w[:, n].reshape(part * self.rows, TILE)
            o_ref[...] = low(lax.dot_general(
                a_ref[...], flat[...], (((1,), (1,)), ((), ())), preferred_element_type=F32
            ))

        wide = part * self.rows
        return ffn_call(
            kernel, self.core, (self.devices // part,), [grad, self.packed],
            [pl.BlockSpec(grad.shape, lambda i, c: (0, 0)),
             pl.BlockSpec((part, rows, TILE), lambda i, c: (i, first + c[0], 0))],
            [jax.ShapeDtypeStruct((tokens, self.width), BF16)],
            [pl.BlockSpec((tokens, wide), lambda i, c: (0, i))],
            2 * grad.size * self.width,
            scratch=(pltpu.VMEM((wide, self.quarter), BF16),), name="key_backward",
        )[0]

    def rec_backward(self, grad):
        if not self.fast:
            return nt(grad, self.plain_rec())
        tokens = grad.shape[0]
        part, count = 4, self.width // TILE
        rows = count * self.rows // 2
        first = self.packed.shape[1] // rows - 2

        def kernel(c_ref, a_ref, w_ref, v_ref, o_ref, flat):
            for k, ref in enumerate((w_ref, v_ref)):
                w = ref[...].reshape(part, count // 2, self.rows, TILE)
                for n in range(count // 2):
                    m = k * (count // 2) + n
                    flat[:, m * TILE : (m + 1) * TILE] = w[:, n].reshape(part * self.rows, TILE)
            o_ref[...] = lax.dot_general(
                a_ref[...], flat[...], (((1,), (1,)), ((), ())), preferred_element_type=F32
            )

        wide = part * self.rows
        return ffn_call(
            kernel, self.core, (self.devices // part,), [grad, self.packed, self.packed],
            [pl.BlockSpec(grad.shape, lambda i, c: (0, 0)),
             pl.BlockSpec((part, rows, TILE), lambda i, c: (i, first, 0)),
             pl.BlockSpec((part, rows, TILE), lambda i, c: (i, first + 1, 0))],
            [jax.ShapeDtypeStruct((tokens, self.width), F32)],
            [pl.BlockSpec((tokens, wide), lambda i, c: (0, i))],
            2 * grad.size * self.width,
            scratch=(pltpu.VMEM((wide, self.width), BF16),), name="rec_backward",
        )[0]


def body(tokens, att_w, down_w, up_w, key_w, value_w, rec_w, vectors, out_grad):
    seqs, length, width = tokens.shape
    total = seqs * length
    y, core = lax.axis_index("y"), lax.axis_index("core")
    zs = lax.axis_size("z")
    ff = key_w.shape[1]
    share = value_w.shape[0]
    half = share // 2
    quarter = ff // 4

    def rows(v):
        return v.reshape(total, width)

    def columns(shard):
        gathered = lax.all_gather(shard, WIDE, axis=0)
        return jnp.swapaxes(gathered, 0, 1).reshape(shard.shape[0], width)

    cols = up_w.shape[0]
    up_vec = columns(jnp.concatenate([vectors, up_w], 0))
    vec, up = up_vec[:16].astype(F32), up_vec[16:]
    down_t = columns(down_w.T)
    w_rkv = lax.all_gather(att_w[:3], WIDE, axis=0)
    w_go = lax.all_gather(att_w[3:], WIDE, axis=0)
    key_sh = key_w.reshape(-1, zs, 2, 2, 2, half)
    key_sh = lax.dynamic_index_in_dim(key_sh, y, 4, False)
    key_sh = key_sh.transpose(0, 3, 1, 2, 4).reshape(-1, 2 * quarter)
    packed = jnp.concatenate(
        [pack_blocks(piece(value_w, y, half, 0)), pack_blocks(key_sh), pack_blocks(rec_w)], 0
    )
    packed = lax.all_gather(packed, WIDE, axis=0)

    x = rows(tokens.astype(F32))
    normed, hat, rstd = norm_forward(x, vec[0], vec[1])
    delta = prior_of(normed, seqs) - normed
    mix_low = low(normed + delta * vec[2])
    tanh_mix = jnp.tanh(nt(mix_low, down_t[:MIXCOLS]))
    hidden = low(tanh_mix)
    hid = [hidden[:, i * RANK : (i + 1) * RANK] for i in range(5)]
    ups = [up[i * RANK : (i + 1) * RANK] for i in range(5)]
    mixed = [low(normed + delta * (vec[3 + i] + nn(hid[i], ups[i]))) for i in range(5)]
    decay_in, key_in, value_in, rec_in, gate_in = mixed
    tanh_decay = jnp.tanh(nt(decay_in, down_t[MIXCOLS:]))
    hidden_decay = low(tanh_decay)
    logdecay = -jnp.exp(vec[8] + nn(hidden_decay, up[MIXCOLS:]))
    keys = stack_nn(key_in, w_rkv, 1)
    values = stack_nn(value_in, w_rkv, 2)
    shaped = jax.ShapeDtypeStruct
    flat, flat_low = shaped((total, width), F32), shaped((total, width), BF16)
    states = shaped((seqs, width // LANES, HEAD, LANES), BF16)
    finals = shaped((seqs, width // LANES, 16, LANES), BF16)
    sums = shaped((seqs, 8, width), F32)
    unit = 2 * total * width
    inclusive, state, final = wkv_call(
        state_kernel, seqs, [keys, values, logdecay], [flat, states, finals], "wkv_state", unit * 512
    )
    carried = chain(state, final, False)
    recept = stack_nn(rec_in, w_rkv, 0)
    gate_pre = stack_nn(gate_in, w_go, 0)
    wkv, gated = wkv_call(
        wkv_kernel, seqs, [recept, keys, values, inclusive, carried, gate_pre, vec], [flat, flat_low],
        "wkv_forward", unit * 1536,
    )
    first_sum = x + stack_nn(gated, w_go, 1)

    normed_two, hat_two, rstd_two = norm_forward(first_sum, vec[12], vec[13])
    delta_two = prior_of(normed_two, seqs) - normed_two
    key_mix = low(normed_two + delta_two * vec[14])
    rec_mix = low(normed_two + delta_two * vec[15])
    key_all, rec_all = group_many([key_mix, rec_mix])
    gated_all = group_many([gated])[0]
    mix_all = group_many([rec_in, key_in, value_in, gate_in])
    packed, key_all, rec_all, gated_all, mix_all = lax.optimization_barrier(
        (packed, key_all, rec_all, gated_all, mix_all)
    )
    ffn = PackedWeights(packed, core, ff, width, half, 2 * zs)
    relu, squared = ffn.key_forward(key_all)
    value_out = group_sum(ffn.value_forward(squared))
    rec_gate = ffn.rec_forward(rec_mix)
    block_out = low(first_sum + rec_gate * value_out).reshape(tokens.shape)

    g = rows(out_grad.astype(F32))
    grad_value = low(g * rec_gate)
    grad_gate_in = low(g * value_out * rec_gate * (1.0 - rec_gate))
    value_all = group_many([grad_value])[0]
    grad_key_pre = ffn.value_backward(value_all, relu)
    g_key_mix = group_sum(ffn.key_backward(grad_key_pre))
    g_rec_mix = ffn.rec_backward(grad_gate_in)
    value_part = low(tn(squared, value_all)).reshape(-1, half, width)
    value_part = lax.psum_scatter(value_part, ("z", "x"), scatter_dimension=0, tiled=True)[0]
    other = swap(value_part, "y")
    first = y == 0
    value_share = jnp.concatenate(
        [jnp.where(first, value_part, other), jnp.where(first, other, value_part)], 0
    ).astype(F32)
    part = low(tn(key_all, grad_key_pre))
    part = lax.psum_scatter(part, ("z", "x"), scatter_dimension=0, tiled=True)
    key_share = spread_cols(part[:, None])[0].reshape(-1, 2, 2, zs, 2, half)
    key_share = key_share.transpose(0, 3, 4, 2, 1, 5).reshape(-1, ff)

    g_prior = prior_back(g_key_mix * vec[14] + g_rec_mix * vec[15], seqs)
    g_normed_two = g_key_mix * (1.0 - vec[14]) + g_rec_mix * (1.0 - vec[15]) + g_prior
    g_maa_key = jnp.sum(g_key_mix * delta_two, 0)
    g_maa_rec = jnp.sum(g_rec_mix * delta_two, 0)
    back_two, g_gain_two, g_bias_two = norm_backward(g_normed_two, hat_two, rstd_two, vec[12])
    grad_first = g + back_two

    grad_att = low(grad_first)
    g_wkv, g_gate_low, g_state, gate_sums = wkv_call(
        gate_back_kernel, seqs,
        [stack_nt(grad_att, w_go, 1), wkv, gate_pre, recept, inclusive, vec],
        [flat_low, flat_low, states, sums], "gate_backward", unit * 1536,
    )
    g_state_out = chain(g_state, final, True)
    g_rec, g_key, g_val, g_decay_low, wkv_sums = wkv_call(
        wkv_back_kernel, seqs,
        [recept, keys, values, inclusive, logdecay, carried, g_state_out, g_wkv, vec],
        [flat_low, flat_low, flat_low, flat_low, sums], "wkv_backward", unit * 4096,
        scratch=[pltpu.VMEM((length, SPAN), F32)] * 3,
    )
    gate_sums, wkv_sums = jnp.sum(gate_sums, 0), jnp.sum(wkv_sums, 0)
    projs = [g_rec, g_key, g_val, g_gate_low]
    early = quad_grads([rec_all, gated_all, mix_all[3]], [grad_gate_in, grad_att, projs[3]])
    late = quad_grads(mix_all[:3], projs[:3])
    rec_share = early[0]
    att_share = jnp.concatenate([late, early[2:], early[1:2]], 0)

    decay_up_grad = tn(hidden_decay, g_decay_low)
    g_pre_decay = low(nt(g_decay_low, up[MIXCOLS:]) * (1.0 - tanh_decay * tanh_decay))
    decay_down_grad = tn(g_pre_decay, decay_in)
    g_mixed = [
        nn(g_pre_decay, down_t[MIXCOLS:]),
        stack_nt(projs[1], w_rkv, 1),
        stack_nt(projs[2], w_rkv, 2),
        stack_nt(projs[0], w_rkv, 0),
        stack_nt(projs[3], w_go, 0),
    ]
    g_normed = g_prior_sum = None
    maa_rows, up_grads, hid_grads = [], [], []
    for i in range(5):
        offset = vec[3 + i] + nn(hid[i], ups[i])
        g_off = g_mixed[i] * delta
        maa_rows.append(jnp.sum(g_off, 0))
        off_low = low(g_off)
        up_grads.append(tn(hid[i], off_low))
        hid_grads.append(nt(off_low, ups[i]))
        here = g_mixed[i] * (1.0 - offset)
        back = g_mixed[i] * offset
        g_normed = here if g_normed is None else g_normed + here
        g_prior_sum = back if g_prior_sum is None else g_prior_sum + back
    g_pre_mix = low(jnp.concatenate(hid_grads, 1) * (1.0 - tanh_mix * tanh_mix))
    mix_down_grad = tn(g_pre_mix, mix_low)
    g_first_mix = nn(g_pre_mix, down_t[:MIXCOLS])
    maa_first = jnp.sum(g_first_mix * delta, 0)
    g_prior_sum = g_prior_sum + g_first_mix * vec[2]
    g_normed = g_normed + g_first_mix * (1.0 - vec[2]) + prior_back(g_prior_sum, seqs)
    back_one, g_gain, g_bias = norm_backward(g_normed, hat, rstd, vec[0])
    input_grad = (grad_first + back_one).reshape(tokens.shape)

    vec_rows = jnp.stack(
        [g_gain, g_bias, maa_first] + maa_rows
        + [wkv_sums[1], wkv_sums[0], gate_sums[0], gate_sums[1], g_gain_two, g_bias_two,
           g_maa_key, g_maa_rec], 0,
    )
    packed = jnp.concatenate(up_grads + [decay_up_grad, mix_down_grad, decay_down_grad, vec_rows], 0)
    packed = small_sum(packed)
    return (
        block_out, input_grad, att_share, packed[cols : 2 * cols].T, packed[:cols],
        key_share, value_share, rec_share, packed[2 * cols :],
    )


def solution(mesh):
    seq, wide = mesh.devices.shape
    fine = Mesh(mesh.devices.reshape(seq, wide // 4, 2, 2), ALL)
    token = P(None, ALL, None)
    by_row, by_col, stacked = P(WIDE, None), P(None, WIDE), P(None, WIDE, None)
    return jax.shard_map(
        body,
        mesh=fine,
        in_specs=(token, stacked, by_row, by_col, by_row, by_row, by_row, by_col, token),
        out_specs=(token, token, stacked, by_row, by_col, by_row, by_row, by_row, by_col),
        check_vma=False,
    )
```

time: 1900 us -> 1240 us (0.65)
  waiting for transfers between devices: 755 us -> 465 us
  matrix products: 319 us -> 68.8 us
  starting transfers between devices: 290 us -> 60.7 us
  Pallas kernels: 5.56 us -> 198 us
  other arithmetic: 211 us -> 120 us
  blocking collectives: 55.6 us -> 138 us
  local copies, waits for them, and re-layouts: 234 us -> 159 us
    all_gather x9 -> x3, waiting for transfers between devices: 396 us -> 182 us  [the longest x1 83 us: body(): w_go = lax.all_gather(att_w[3:], WIDE, axis=0)]
    pallas_call x2 -> x22, Pallas kernels: 5.56 us -> 198 us  [the longest x6 68.9 us: ffn_call(): pl.pallas_call(kernel, grid_spec=pltpu.PrefetchScalarGridSpec(num_scalar_...]
    all_to_all x1 -> x0, starting transfers between devices: 117 us -> none  [chain(): packed = lax.all_to_all(packed, ALL, 0, 0, tiled=True)]
    dot_general x12 -> x0, matrix products: 93.1 us -> none  [the longest x3 31.4 us: wkv_local(): scores = jnp.einsum('sthi,suhi->shtu', query, key_side, precision=exact)]
    ppermute x24 -> x3, starting transfers between devices: 95.6 us -> 12.9 us  [line_sum(): lax.ppermute(low(right), 'z', [(i, i + 1) for i in range(count - 1) if i...]
    ppermute x24 -> x3, waiting for transfers between devices: 90.1 us -> 10.9 us  [line_sum(): lax.ppermute(low(right), 'z', [(i, i + 1) for i in range(count - 1) if i...]
    dot_general x16 -> x8, matrix products: 81.6 us -> 12.3 us  [nn(): return jnp.dot(a, b, preferred_element_type=F32)]
    dot_general x16 -> x8, matrix products: 71.3 us -> 4.1 us  [nt(): lax.dot_general(a, b, (((1,), (1,)), ((), ())), preferred_element_type=F32)]
  transfers between devices with their start and end apart: 113 -> 49, of which waited for: 44 -> 26; matrix products, arithmetic and copies ran while one was open for 39% -> 22% of each run, Pallas kernels for 0% -> 13%
where the time goes in v2:
time: 1240 us; the launch traced here: 1230 us
  waiting for transfers between devices  465 us (38%)
  Pallas kernels  198 us (16%)
  local copies, waits for them, and re-layouts  159 us (13%)
  blocking collectives  138 us (11%)
  other arithmetic  120 us (10%)
  matrix products  68.8 us (6%)
  starting transfers between devices  60.7 us (5%)
  between operations  16.9 us (1%)
    ppermute x30, waiting for transfers between devices, swap(): return lax.ppermute(value, axis, [(0, 1), (1, 0)])  242 us
    all_gather x1, waiting for transfers between devices, body(): w_go = lax.all_gather(att_w[3:], WIDE, axis=0)  83 us
    all_to_all x2, blocking collectives, chain(): packed = lax.all_to_all(packed, ALL, 0, 0, tiled=True)  80.4 us
    pallas_call x6, Pallas kernels, ffn_call(): pl.pallas_call(kernel, grid_spec=pltpu.PrefetchScalarGridSpec(num_scalar_...  68.9 us
    pallas_call x4, Pallas kernels, wkv_call(): pl.pallas_call(kernel, grid=(seqs, width // SPAN), in_specs=[spec(a) for...  64.1 us
    all_gather x1, waiting for transfers between devices, body(): w_rkv = lax.all_gather(att_w[:3], WIDE, axis=0)  60.3 us
    all_gather x2, blocking collectives, columns(): gathered = lax.all_gather(shard, WIDE, axis=0)  57.5 us
    unnamed x358, local copies, waits for them, and re-layouts  52.6 us
  transfers between devices with their start and end apart: 49, of which 26 were waited for; matrix products, arithmetic and copies ran while one was open for 22% of the time, Pallas kernels for 13%

profile of v2, /device:TPU:0, one launch (start us, length us, event | category | flops | bytes accessed | tf_op | source)
XLA Modules:
  0.0 1225.7 jit_solution(14818964832569882484)
XLA Ops:
  20.0 31.5 %all-gather = bf16[3840,128]{1,0:T(8,128)(2,1)S(1)} all-gather(bf16[240,128]{1,0:T(8,128)(2,1)S(1)} %pad_maximum_fusion.27), channel_id=2, replica_groups=mesh['y'=2,'z'=4,'x'=2,'core'=2] {'z','x','core'}, dimensions={0}, use_global_device_ids=true | all-gather | bytes 1044480 | tf_op jit(solution)/shard_map/all_gather | solution.py:725
  55.9 25.9 %all-gather.1 = bf16[3584,128]{1,0:T(8,128)(2,1)S(1)} all-gather(bf16[224,128]{1,0:T(8,128)(2,1)S(1)} %bitcast.638), channel_id=3, replica_groups=mesh['y'=2,'z'=4,'x'=2,'core'=2] {'z','x','core'}, dimensions={0}, use_global_device_ids=true | all-gather | bytes 974848 | tf_op jit(solution)/shard_map/all_gather | solution.py:725
  98.9 60.3 %all-gather.9.cloned.1.call-done = bf16[48,128,2048]{2,1,0:T(8,128)(2,1)} async-done(((bf16[3,128,2048]{2,1,0:T(8,128)(2,1)}), bf16[48,128,2048]{2,1,0:T(8,128)(2,1)}) %all-gather.9.cloned.1.call-update) | async-done | bytes 25165840 | tf_op jit(solution)/shard_map/all_gather | solution.py:732
  183.6 38.8 %all_to_all.20.refs_1_ = bf16[32,80,128]{2,1,0:T(8,128)(2,1)S(1)} all-to-all(bf16[32,80,128]{2,1,0:T(8,128)(2,1)S(1)} %pad_maximum_fusion.24), channel_id=1, replica_groups=mesh['y'=2,'z'=4,'x'=2,'core'=2] {'y','z','x','core'}, dimensions={0} | all-to-all | bytes 1310720 | tf_op jit(solution)/shard_map/all_to_all | solution.py:410
  228.3 83.0 %all-gather.11.cloned.1.call-done = bf16[32,128,2048]{2,1,0:T(8,128)(2,1)} async-done(((bf16[2,128,2048]{2,1,0:T(8,128)(2,1)}), bf16[32,128,2048]{2,1,0:T(8,128)(2,1)}) %all-gather.11.cloned.1.call-update) | async-done | bytes 16777232 | tf_op jit(solution)/shard_map/all_gather | solution.py:733
  333.8 17.2 %wkv_forward.1 = (f32[256,2048]{1,0:T(8,128)S(1)}, bf16[256,2048]{1,0:T(8,128)(2,1)S(1)}) custom-call(f32[256,2048]{1,0:T(8,128)S(1)} %copy-done.13, f32[256,2048]{1,0:T(8,128)S(1)} %copy-done.10, f32[256,2048]{1,0:T(8,128)S(1)} %stack_nn.7.value_ref, f32[256,2048]{1,0:T(8,128)S(1)} %copy-done.30, bf16[2,16,64,128]{3,2,1,0:T(8,128)(2,1)} %bitcast.22.state_ref, ...), custom_call_target="tpu_custom_call" | custom-call | flops 1610612736 | bytes 14286848 | tf_op jit(solution)/shard_map/wkv_forward/pallas_call | solution.py:366
  385.6 55.9 %collective-permute-done.6 = bf16[1,256,2048]{2,1,0:T(8,128)(2,1)} collective-permute-done((bf16[1,256,2048]{2,1,0:T(8,128)(2,1)S(1)}, bf16[1,256,2048]{2,1,0:T(8,128)(2,1)}, u32[]{:S(2)}, u32[]{:S(2)}) %collective-permute-start.6) | collective-permute-done | bytes 1048608 | tf_op jit(solution)/shard_map/ppermute | solution.py:35
  461.8 38.5 %all-gather.13.cloned.1.call-done = bf16[73728,256]{1,0:T(8,128)(2,1)} async-done(((bf16[4608,256]{1,0:T(8,128)(2,1)}), bf16[73728,256]{1,0:T(8,128)(2,1)}) %all-gather.13.cloned.1.call-update) | async-done | bytes 37748752 | tf_op jit(solution)/shard_map/all_gather | solution.py:740
  500.2 13.4 %key_forward.1 = (bf16[1024,1792]{1,0:T(8,128)(2,1)}, bf16[1024,1792]{1,0:T(8,128)(2,1)}) custom-call(s32[1]{0:T(128)} %bitcast.25.c_ref, bf16[1024,2048]{1,0:T(8,128)(2,1)} %get-tuple-element.38.a_ref, bf16[16,4608,256]{2,1,0:T(8,128)(2,1)} %bitcast.534), custom_call_target="tpu_custom_call" | custom-call | flops 7516192768 | bytes 18874368 | tf_op jit(solution)/shard_map/key_forward/pallas_call | solution.py:520
  513.6 13.1 %value_forward.1 = bf16[1024,2048]{1,0:T(8,128)(2,1)} custom-call(s32[1]{0:T(128)} %bitcast.25.c_ref, bf16[1024,1792]{1,0:T(8,128)(2,1)} %get-tuple-element.39.a_ref, bf16[8,2,4608,256]{3,2,1,0:T(8,128)(2,1)} %bitcast.535), custom_call_target="tpu_custom_call" | custom-call | flops 7516192768 | bytes 15204352 | tf_op jit(solution)/shard_map/value_forward/pallas_call | solution.py:520
  545.9 15.2 %collective-permute-done.12 = bf16[256,2048]{1,0:T(8,128)(2,1)} collective-permute-done((bf16[256,2048]{1,0:T(8,128)(2,1)}, bf16[256,2048]{1,0:T(8,128)(2,1)}, u32[]{:S(2)}, u32[]{:S(2)}) %collective-permute-start.12) | collective-permute-done | bytes 1048608 | tf_op jit(solution)/shard_map/ppermute | solution.py:35
  567.4 23.0 %collective-permute-done.14 = bf16[1,256,2048]{2,1,0:T(8,128)(2,1)S(1)} collective-permute-done((bf16[1,256,2048]{2,1,0:T(8,128)(2,1)S(1)}, bf16[1,256,2048]{2,1,0:T(8,128)(2,1)S(1)}, u32[]{:S(2)}, u32[]{:S(2)}) %collective-permute-start.14) | collective-permute-done | bytes 1048608 | tf_op jit(solution)/shard_map/ppermute | solution.py:35
  595.4 14.4 %value_backward.1.a_ref = bf16[1024,1792]{1,0:T(8,128)(2,1)} custom-call(s32[1]{0:T(128)} %bitcast.25.c_ref, bf16[1024,2048]{1,0:T(8,128)(2,1)} %pad_maximum_fusion.11.a_ref, bf16[1024,1792]{1,0:T(8,128)(2,1)} %get-tuple-element.40.r_ref, bf16[8,2,4608,256]{3,2,1,0:T(8,128)(2,1)} %bitcast.537), custom_call_target="tpu_custom_call" | custom-call | flops 7516192768 | bytes 15204352 | tf_op jit(solution)/shard_map/value_backward/pallas_call | solution.py:520
  665.3 17.0 %collective-permute-done.17 = bf16[256,2048]{1,0:T(8,128)(2,1)S(1)} collective-permute-done((bf16[256,2048]{1,0:T(8,128)(2,1)}, bf16[256,2048]{1,0:T(8,128)(2,1)S(1)}, u32[]{:S(2)}, u32[]{:S(2)}) %collective-permute-start.17) | collective-permute-done | bytes 1048608 | tf_op jit(solution)/shard_map/ppermute | solution.py:35
  706.4 13.4 %gate_backward.1 = (bf16[256,2048]{1,0:T(8,128)(2,1)S(1)}, bf16[256,2048]{1,0:T(8,128)(2,1)S(1)}, bf16[2,16,64,128]{3,2,1,0:T(8,128)(2,1)S(1)}, f32[2,8,2048]{2,1,0:T(8,128)S(1)}) custom-call(f32[256,2048]{1,0:T(8,128)S(1)} %stack_nt.5.grad_ref, f32[256,2048]{1,0:T(8,128)S(1)} %copy-done.36, f32[256,2048]{1,0:T(8,128)S(1)} %copy-done.18, ...), custom_call_target="tpu_custom_call" | custom-call | flops 1610612736 | bytes 13369344 | tf_op jit(solution)/shard_map/gate_backward/pallas_call | solution.py:366
  727.6 33.8 %collective-permute-done.24 = bf16[256,3,1024]{2,0,1:T(8,128)(2,1)} collective-permute-done((bf16[256,3,1024]{2,0,1:T(8,128)(2,1)}, bf16[256,3,1024]{2,0,1:T(8,128)(2,1)}, u32[]{:S(2)}, u32[]{:S(2)}) %collective-permute-start.24) | collective-permute-done | bytes 1572896 | tf_op jit(solution)/shard_map/ppermute | solution.py:35
  789.5 41.6 %all_to_all.21.refs_1_ = bf16[32,80,128]{2,1,0:T(8,128)(2,1)S(1)} all-to-all(bf16[32,80,128]{2,1,0:T(8,128)(2,1)S(1)} %pad_maximum_fusion.23), channel_id=1, replica_groups=mesh['y'=2,'z'=4,'x'=2,'core'=2] {'y','z','x','core'}, dimensions={0} | all-to-all | bytes 1310720 | tf_op jit(solution)/shard_map/all_to_all | solution.py:410
  859.2 24.9 %wkv_backward.1 = (bf16[256,2048]{1,0:T(8,128)(2,1)S(1)}, bf16[256,2048]{1,0:T(8,128)(2,1)S(1)}, bf16[256,2048]{1,0:T(8,128)(2,1)S(1)}, bf16[256,2048]{1,0:T(8,128)(2,1)S(1)}, f32[2,8,2048]{2,1,0:T(8,128)S(1)}) custom-call(f32[256,2048]{1,0:T(8,128)S(1)} %copy-done.15, f32[256,2048]{1,0:T(8,128)S(1)} %copy-done.11, f32[256,2048]{1,0:T(8,128)S(1)} %copy-done.8, ...), custom_call_target="tpu_custom_call" | custom-call | flops 4294967296 | bytes 17039360 | tf_op jit(solution)/shard_map/wkv_backward/pallas_call | solution.py:366
  910.2 13.0 %collective-permute-done.20 = bf16[256,3,1024]{2,0,1:T(8,128)(2,1)} collective-permute-done((bf16[256,3,1024]{2,0,1:T(8,128)(2,1)}, bf16[256,3,1024]{2,0,1:T(8,128)(2,1)}, u32[]{:S(2)}, u32[]{:S(2)}) %collective-permute-start.20) | collective-permute-done | bytes 1572896 | tf_op jit(solution)/shard_map/ppermute | solution.py:35
  999.8 16.3 %concatenate.170 = f32[464,8,2,128]{3,0,2,1:T(8,128)} concatenate(f32[32,8,2,128]{3,0,2,1:T(8,128)S(1)} %copy-done.123, f32[32,8,2,128]{3,0,2,1:T(8,128)} %copy.149, f32[32,8,2,128]{3,0,2,1:T(8,128)} %copy.150, f32[32,8,2,128]{3,0,2,1:T(8,128)} %copy.151, f32[32,8,2,128]{3,0,2,1:T(8,128)} %copy.152, f32[64,8,2,128]{3,0,2,1:T(8,128)} %copy.153, f32[160,8,2,128]{3,0,2,1:T(8,128)} %fusion.81, ...), dimensions={0} | concatenate | bytes 7602176 | tf_op jit(solution)/shard_map/concatenate | solution.py:874
  1038.7 18.9 %collective-permute-done.29 = bf16[464,512]{1,0:T(8,128)(2,1)S(1)} collective-permute-done((bf16[464,512]{1,0:T(8,128)(2,1)S(1)}, bf16[464,512]{1,0:T(8,128)(2,1)S(1)}, u32[]{:S(2)}, u32[]{:S(2)}) %collective-permute-start.29) | collective-permute-done | bytes 475168 | tf_op jit(solution)/shard_map/ppermute | solution.py:35
  1108.4 19.2 %collective-permute-done.39 = bf16[224,2048]{1,0:T(8,128)(2,1)S(1)} collective-permute-done((bf16[224,2048]{1,0:T(8,128)(2,1)}, bf16[224,2048]{1,0:T(8,128)(2,1)S(1)}, u32[]{:S(2)}, u32[]{:S(2)}) %collective-permute-start.39) | collective-permute-done | bytes 917536 | tf_op jit(solution)/shard_map/ppermute | solution.py:35
  1131.2 15.3 %collective-permute-done.38 = bf16[2,128,1,1792]{3,1,0,2:T(8,128)(2,1)S(1)} collective-permute-done((bf16[2,128,1,1792]{3,1,0,2:T(8,128)(2,1)S(1)}, bf16[2,128,1,1792]{3,1,0,2:T(8,128)(2,1)S(1)}, u32[]{:S(2)}, u32[]{:S(2)}) %collective-permute-start.38) | collective-permute-done | bytes 917536 | tf_op jit(solution)/shard_map/ppermute | solution.py:35
  1189.7 13.1 %collective-permute-done.23 = bf16[2,128,3,512]{1,3,2,0:T(8,128)(2,1)} collective-permute-done((bf16[2,128,3,512]{1,3,2,0:T(8,128)(2,1)}, bf16[2,128,3,512]{1,3,2,0:T(8,128)(2,1)}, u32[]{:S(2)}, u32[]{:S(2)}) %collective-permute-start.23) | collective-permute-done | bytes 786464 | tf_op jit(solution)/shard_map/ppermute | solution.py:35
  (652 shorter events, 552.0 us)
Async XLA Ops:
  7.2 152.1 %all-gather.9.cloned.1.call-start = ((), (), s32[]{:S(2)}) async-start(), calls=%async_computation.12 | async-start | bytes 26738688 | tf_op jit(solution)/shard_map/all_gather | solution.py:732
  10.1 301.2 %all-gather.11.cloned.1.call-start = ((), (), s32[]{:S(2)}) async-start(), calls=%async_computation.13 | async-start | bytes 17825792 | tf_op jit(solution)/shard_map/all_gather | solution.py:733
  12.5 487.7 %all-gather.13.cloned.1.call-start = ((), (), s32[]{:S(2)}) async-start(), calls=%async_computation.14 | async-start | bytes 40108032 | tf_op jit(solution)/shard_map/all_gather | solution.py:740
  53.6 28.9 %collective-permute-start = (f32[2,2048]{1,0:T(2,128)S(1)}, f32[2,2048]{1,0:T(2,128)S(1)}, u32[]{:S(2)}, u32[]{:S(2)}) collective-permute-start(f32[2,2048]{1,0:T(2,128)S(1)} %bitcast.655), channel_id=1, source_target_pairs={{0,1},{1,2},{2,3},{3,4},{4,5},{5,6},{6,7},{7,8},{8,9},{9,10},{10,1... | collective-permute-start | bytes 49160 | tf_op jit(solution)/shard_map/ppermute | solution.py:44
  94.7 133.1 %collective-permute-start.9 = (bf16[4,256,2048]{2,1,0:T(8,128)(2,1)}, bf16[4,256,2048]{2,1,0:T(8,128)(2,1)}, u32[]{:S(2)}, u32[]{:S(2)}) collective-permute-start(bf16[4,256,2048]{2,1,0:T(8,128)(2,1)} %pad_maximum_fusion.6), channel_id=1, source_target_pairs={{0,16},{16,0},{1,17},{17,1},{2,18},{18,2},{3,19},{19,3},{4,20},{20... | collective-permute-start | bytes 12582920 | tf_op jit(solution)/shard_map/ppermute | solution.py:35
  223.9 103.5 %all-to-all-start.1 = ((bf16[32,64,128]{2,1,0:T(8,128)(2,1)}), bf16[32,64,128]{2,1,0:T(8,128)(2,1)}, u32[]{:S(2)}, u32[]{:S(2)}) async-start(bf16[32,64,128]{2,1,0:T(8,128)(2,1)} %copy-done.34), calls=%async_computation.1 | async-start | bytes 1048576 | tf_op jit(solution)/shard_map/all_to_all | solution.py:425
  227.7 868.8 %reduce-scatter.9.cloned.1.call-start = ((), (), s32[]{:S(2)}) async-start(), calls=%async_computation.10 | async-start | bytes 8257536 | tf_op jit(solution)/shard_map/reduce_scatter | solution.py:806
  227.8 152.0 %collective-permute-start.8 = (bf16[4,256,2048]{2,1,0:T(8,128)(2,1)}, bf16[4,256,2048]{2,1,0:T(8,128)(2,1)}, u32[]{:S(2)}, u32[]{:S(2)}) collective-permute-start(bf16[4,256,2048]{2,1,0:T(8,128)(2,1)} %pad_maximum_fusion.6), channel_id=1, source_target_pairs={{0,1},{1,0},{2,3},{3,2},{4,5},{5,4},{6,7},{7,6},{8,9},{9,8},{10,11... | collective-permute-start | bytes 12582920 | tf_op jit(solution)/shard_map/ppermute | solution.py:35
  227.9 154.5 %collective-permute-start.10 = (bf16[4,256,2048]{2,1,0:T(8,128)(2,1)}, bf16[4,256,2048]{2,1,0:T(8,128)(2,1)}, u32[]{:S(2)}, u32[]{:S(2)}) collective-permute-start(bf16[4,256,2048]{2,1,0:T(8,128)(2,1)} %collective-permute-done.9), channel_id=1, source_target_pairs={{0,1},{1,0},{2,3},{3,2},{4,5},{5,4},{6,7},{7,6},{8,9},{9,8},{10,11... | collective-permute-start | bytes 12582920 | tf_op jit(solution)/shard_map/ppermute | solution.py:35
  369.4 76.4 %collective-permute-start.3 = (bf16[2,256,2048]{2,1,0:T(8,128)(2,1)}, bf16[2,256,2048]{2,1,0:T(8,128)(2,1)}, u32[]{:S(2)}, u32[]{:S(2)}) collective-permute-start(bf16[2,256,2048]{2,1,0:T(8,128)(2,1)} %pad_maximum_fusion.19), channel_id=1, source_target_pairs={{0,16},{16,0},{1,17},{17,1},{2,18},{18,2},{3,19},{19,3},{4,20},{20... | collective-permute-start | bytes 6291464 | tf_op jit(solution)/shard_map/ppermute | solution.py:35
  379.6 61.9 %collective-permute-start.6 = (bf16[1,256,2048]{2,1,0:T(8,128)(2,1)S(1)}, bf16[1,256,2048]{2,1,0:T(8,128)(2,1)}, u32[]{:S(2)}, u32[]{:S(2)}) collective-permute-start(bf16[1,256,2048]{2,1,0:T(8,128)(2,1)S(1)} %bitcast.525), channel_id=1, source_target_pairs={{0,16},{16,0},{1,17},{17,1},{2,18},{18,2},{3,19},{19,3},{4,20},{20... | collective-permute-start | bytes 3145736 | tf_op jit(solution)/shard_map/ppermute | solution.py:35
  385.0 65.3 %collective-permute-start.5 = (bf16[1,256,2048]{2,1,0:T(8,128)(2,1)S(1)}, bf16[1,256,2048]{2,1,0:T(8,128)(2,1)}, u32[]{:S(2)}, u32[]{:S(2)}) collective-permute-start(bf16[1,256,2048]{2,1,0:T(8,128)(2,1)S(1)} %bitcast.526), channel_id=1, source_target_pairs={{0,1},{1,0},{2,3},{3,2},{4,5},{5,4},{6,7},{7,6},{8,9},{9,8},{10,11... | collective-permute-start | bytes 3145736 | tf_op jit(solution)/shard_map/ppermute | solution.py:35
  385.1 70.7 %collective-permute-start.2 = (bf16[2,256,2048]{2,1,0:T(8,128)(2,1)}, bf16[2,256,2048]{2,1,0:T(8,128)(2,1)}, u32[]{:S(2)}, u32[]{:S(2)}) collective-permute-start(bf16[2,256,2048]{2,1,0:T(8,128)(2,1)} %pad_maximum_fusion.19), channel_id=1, source_target_pairs={{0,1},{1,0},{2,3},{3,2},{4,5},{5,4},{6,7},{7,6},{8,9},{9,8},{10,11... | collective-permute-start | bytes 6291464 | tf_op jit(solution)/shard_map/ppermute | solution.py:35
  535.5 25.6 %collective-permute-start.12 = (bf16[256,2048]{1,0:T(8,128)(2,1)}, bf16[256,2048]{1,0:T(8,128)(2,1)}, u32[]{:S(2)}, u32[]{:S(2)}) collective-permute-start(bf16[256,2048]{1,0:T(8,128)(2,1)} %fusion.8), channel_id=1, source_target_pairs={{0,16},{16,0},{1,17},{17,1},{2,18},{18,2},{3,19},{19,3},{4,20},{20... | collective-permute-start | bytes 3145736 | tf_op jit(solution)/shard_map/ppermute | solution.py:35
  565.9 24.5 %collective-permute-start.14 = (bf16[1,256,2048]{2,1,0:T(8,128)(2,1)S(1)}, bf16[1,256,2048]{2,1,0:T(8,128)(2,1)S(1)}, u32[]{:S(2)}, u32[]{:S(2)}) collective-permute-start(bf16[1,256,2048]{2,1,0:T(8,128)(2,1)S(1)} %bitcast.578), channel_id=1, source_target_pairs={{0,16},{16,0},{1,17},{17,1},{2,18},{18,2},{3,19},{19,3},{4,20},{20... | collective-permute-start | bytes 3145736 | tf_op jit(solution)/shard_map/ppermute | solution.py:35
  622.1 482.1 %reduce-scatter.11.cloned.1.call-start = ((), (), s32[]{:S(2)}) async-start(), calls=%async_computation.11 | async-start | bytes 8257536 | tf_op jit(solution)/shard_map/reduce_scatter | solution.py:799
  635.8 494.2 %reduce-scatter.7.cloned.1.call-start = ((), (), s32[]{:S(2)}) async-start(), calls=%async_computation.9 | async-start | bytes 7077888 | tf_op jit(solution)/shard_map/reduce_scatter | solution.py:119
  656.8 25.4 %collective-permute-start.17 = (bf16[256,2048]{1,0:T(8,128)(2,1)}, bf16[256,2048]{1,0:T(8,128)(2,1)S(1)}, u32[]{:S(2)}, u32[]{:S(2)}) collective-permute-start(bf16[256,2048]{1,0:T(8,128)(2,1)} %fusion.6), channel_id=1, source_target_pairs={{0,16},{16,0},{1,17},{17,1},{2,18},{18,2},{3,19},{19,3},{4,20},{20... | collective-permute-start | bytes 3145736 | tf_op jit(solution)/shard_map/ppermute | solution.py:35
  722.8 38.6 %collective-permute-start.24 = (bf16[256,3,1024]{2,0,1:T(8,128)(2,1)}, bf16[256,3,1024]{2,0,1:T(8,128)(2,1)}, u32[]{:S(2)}, u32[]{:S(2)}) collective-permute-start(bf16[256,3,1024]{2,0,1:T(8,128)(2,1)} %get-tuple-element.153), channel_id=1, source_target_pairs={{0,16},{16,0},{1,17},{17,1},{2,18},{18,2},{3,19},{19,3},{4,20},{20... | collective-permute-start | bytes 4718600 | tf_op jit(solution)/shard_map/ppermute | solution.py:35
  835.9 325.1 %reduce-scatter.5.cloned.1.call-start = ((), (), s32[]{:S(2)}) async-start(), calls=%async_computation.8 | async-start | bytes 7077888 | tf_op jit(solution)/shard_map/reduce_scatter | solution.py:119
  886.6 36.6 %collective-permute-start.20 = (bf16[256,3,1024]{2,0,1:T(8,128)(2,1)}, bf16[256,3,1024]{2,0,1:T(8,128)(2,1)}, u32[]{:S(2)}, u32[]{:S(2)}) collective-permute-start(bf16[256,3,1024]{2,0,1:T(8,128)(2,1)} %get-tuple-element.149), channel_id=1, source_target_pairs={{0,16},{16,0},{1,17},{17,1},{2,18},{18,2},{3,19},{19,3},{4,20},{20... | collective-permute-start | bytes 4718600 | tf_op jit(solution)/shard_map/ppermute | solution.py:35
  959.5 27.3 %collective-permute-start.19 = (f32[2,2048]{1,0:T(2,128)}, f32[2,2048]{1,0:T(2,128)}, u32[]{:S(2)}, u32[]{:S(2)}) collective-permute-start(f32[2,2048]{1,0:T(2,128)} %bitcast.510), channel_id=1, source_target_pairs={{1,0},{2,1},{3,2},{4,3},{5,4},{6,5},{7,6},{8,7},{9,8},{10,9},{11,1... | collective-permute-start | bytes 49160 | tf_op jit(solution)/shard_map/ppermute | solution.py:44
  1107.7 38.8 %collective-permute-start.38 = (bf16[2,128,1,1792]{3,1,0,2:T(8,128)(2,1)S(1)}, bf16[2,128,1,1792]{3,1,0,2:T(8,128)(2,1)S(1)}, u32[]{:S(2)}, u32[]{:S(2)}) collective-permute-start(bf16[2,128,1,1792]{3,1,0,2:T(8,128)(2,1)S(1)} %fusion.47), channel_id=1, source_target_pairs={{0,16},{16,0},{1,17},{17,1},{2,18},{18,2},{3,19},{19,3},{4,20},{20... | collective-permute-start | bytes 2752520 | tf_op jit(solution)/shard_map/ppermute | solution.py:35
  1147.8 36.2 %collective-permute-start.27 = (bf16[2,128,3,512]{1,3,2,0:T(8,128)(2,1)}, bf16[2,128,3,512]{1,3,2,0:T(8,128)(2,1)}, u32[]{:S(2)}, u32[]{:S(2)}) collective-permute-start(bf16[2,128,3,512]{1,3,2,0:T(8,128)(2,1)} %pad_maximum_fusion.26), channel_id=1, source_target_pairs={{0,16},{16,0},{1,17},{17,1},{2,18},{18,2},{3,19},{19,3},{4,20},{20... | collective-permute-start | bytes 2359304 | tf_op jit(solution)/shard_map/ppermute | solution.py:35
  (198 other events, 2864.8 us)
Sparse Core Ops, SparseCore 0:
  10.2 148.9 all-gather.8
  161.4 149.8 all-gather.10
  313.5 186.7 all-gather.12
  622.2 132.7 reduce-scatter.8
  758.5 152.0 reduce-scatter.10
  914.0 117.4 reduce-scatter.6
  1035.1 125.8 reduce-scatter.4

commit v3 on v2

--- a/solution.py
+++ b/solution.py
@@ -52,80 +52,201 @@
     return lax.dynamic_slice(value, start, shape)
 
 
+def line_own(block, index):
+    count = lax.axis_size("z")
+    return lax.dynamic_index_in_dim(block, jnp.clip(index, 0, count - 1), 0, False).astype(F32)
+
+
+def line_step(block, t, moving):
+    count, place = lax.axis_size("z"), lax.axis_index("z")
+    right = line_own(block, count - t + place)
+    left = line_own(block, place + t - count)
+    if moving is not None:
+        right, left = right + moving[0].astype(F32), left + moving[1].astype(F32)
+    up = lax.ppermute(low(right), "z", [(i, i + 1) for i in range(count - 1) if i <= t - 1])
+    down = lax.ppermute(
+        low(left), "z", [(i, i - 1) for i in range(1, count) if count - 1 - i <= t - 1]
+    )
+    return up, down
+
+
+def line_end(block, moving):
+    own = line_own(block, lax.axis_index("z"))
+    return own + moving[0].astype(F32) + moving[1].astype(F32)
+
+
 def line_sum(block):
-    count = lax.axis_size("z")
-    place = lax.axis_index("z")
-
-    def own(index):
-        return lax.dynamic_index_in_dim(block, jnp.clip(index, 0, count - 1), 0, False).astype(F32)
-
-    up = down = None
-    for t in range(1, count):
-        right = own(count - t + place)
-        left = own(place + t - count)
-        if up is not None:
-            right = right + up.astype(F32)
-            left = left + down.astype(F32)
-        up = lax.ppermute(low(right), "z", [(i, i + 1) for i in range(count - 1) if i <= t - 1])
-        down = lax.ppermute(
-            low(left), "z", [(i, i - 1) for i in range(1, count) if count - 1 - i <= t - 1]
-        )
-    return own(place) + up.astype(F32) + down.astype(F32)
+    moving = None
+    for t in range(1, lax.axis_size("z")):
+        moving = line_step(block, t, moving)
+    return line_end(block, moving)
+
+
+def pack_columns(parts):
+    width = parts[0].shape[1]
+    counts = [p.shape[0] for p in parts]
+    rows = sum(counts)
+    block = LANES
+
+    def kernel(*refs):
+        out = refs[-1]
+        start = 0
+        while start < len(counts):
+            take, n = [], 0
+            while n == 0 or n % 8:
+                take.append(refs[start][...])
+                n += counts[start]
+                start += 1
+            first = sum(counts[: start - len(take)])
+            out[0, first : first + n] = take[0] if len(take) == 1 else jnp.concatenate(take, 0)
+
+    return pl.pallas_call(
+        kernel,
+        grid=(width // block,),
+        in_specs=[pl.BlockSpec((c, block), lambda j: (0, j)) for c in counts],
+        out_specs=pl.BlockSpec((1, rows, block), lambda j: (j, 0, 0)),
+        out_shape=jax.ShapeDtypeStruct((width // block, rows, block), F32),
+        name="pack_columns",
+    )(*parts)
+
+
+def small_core(value):
+    z, rows = lax.axis_size("z"), value.shape[1]
+    share = 16 * LANES // (4 * z)
+    if share != LANES:
+        value = value.reshape(16, rows, LANES // share, share).swapaxes(1, 2).reshape(-1, rows, share)
+    core = lax.axis_index("core")
+    value = value.reshape(2 * z, 2, rows, share)
+    give = low(lax.dynamic_index_in_dim(value, 1 - core, 1, False))
+    value = lax.dynamic_index_in_dim(value, core, 1, False) + swap(give, "core").astype(F32)
+    return value.reshape(z, 2, rows, share)
 
 
 def small_sum(value):
-    z, rows = lax.axis_size("z"), value.shape[0]
-    for axis in ("core", "x"):
-        place = lax.axis_index(axis)
-        parts = value.reshape(rows, z, 2, -1) if axis == "x" else value.reshape(rows, 2 * z, 2, -1)
-        give = lax.dynamic_index_in_dim(parts, 1 - place, 2, False).reshape(rows, -1)
-        keep = lax.dynamic_index_in_dim(parts, place, 2, False).reshape(rows, -1)
-        value = keep + swap(give if axis == "core" else low(give), axis).astype(F32)
-    value = line_sum(jnp.swapaxes(value.reshape(rows, z, -1), 0, 1))
+    x = lax.axis_index("x")
+    give = low(lax.dynamic_index_in_dim(value, 1 - x, 1, False))
+    value = line_sum(lax.dynamic_index_in_dim(value, x, 1, False) + swap(give, "x").astype(F32))
     return value + swap(value, "y")
 
 
-def quarter_cols(right):
-    y, core = lax.axis_index("y"), lax.axis_index("core")
+def tie(*values):
+    return lax.optimization_barrier(values)
+
+
+def half_cols(right):
+    y = lax.axis_index("y")
     half = right.shape[2] // 2
-    near = piece(right, y, half, 2)
-    across = swap(piece(right, 1 - y, half, 2), "y")
-    both = jnp.concatenate([near, across], 0)
-    mine = piece(both, core, half // 2, 2)
-    other = swap(piece(both, 1 - core, half // 2, 2), "core")
-    rows = right.shape[0]
-    return jnp.concatenate([mine[:rows], other[:rows], mine[rows:], other[rows:]], 0)
+    return piece(right, y, half, 2), swap(piece(right, 1 - y, half, 2), "y")
+
+
+def quarter_cols(near, across):
+    core = lax.axis_index("core")
+    both = jnp.stack([near, across], 1)
+    quarter = near.shape[2] // 2
+    mine = piece(both, core, quarter, 3)
+    other = swap(piece(both, 1 - core, quarter, 3), "core")
+    both = jnp.stack([mine, other], 2)
+    return both.reshape(near.shape[0], -1, quarter)
 
 
 def spread_cols(part):
     y, core = lax.axis_index("y"), lax.axis_index("core")
     rows = part.shape[0] // 2
     keep = piece(part, core, rows, 0)
-    give = swap(piece(part, 1 - core, rows, 0), "core")
-    first = core == 0
-    part = jnp.stack([jnp.where(first, keep, give), jnp.where(first, give, keep)], 0)
-    other = swap(part, "y")
-    first = y == 0
-    part = jnp.stack([jnp.where(first, part, other), jnp.where(first, other, part)], 0)
-    part = part.transpose(3, 2, 0, 1, 4)
-    return part.reshape(part.shape[0], rows, -1).astype(F32)
-
-
-def quad_grads(lefts, rights):
-    right = quarter_cols(jnp.stack(rights, 1))
-    quarter = right.shape[2]
-    parts = [low(tn(a, right[:, i])) for i, a in enumerate(lefts)]
-    part = jnp.concatenate(parts, 1)
-    part = lax.psum_scatter(part, ("z", "x"), scatter_dimension=0, tiled=True)
-    return spread_cols(part.reshape(part.shape[0], len(lefts), quarter))
-
-
-def group_many(values):
+    give = piece(part, 1 - core, rows, 0)
+    near, across = swap(give, "core"), swap(keep, "y")
+    far = lax.ppermute(give, ("y", "core"), [(0, 3), (1, 2), (2, 1), (3, 0)])
+    quarters = []
+    for q in range(4):
+        this, that = jnp.where(core == q % 2, keep, near), jnp.where(core == q % 2, across, far)
+        quarters.append(jnp.where(y == q // 2, this, that))
+    outs = [
+        jnp.concatenate([a[:, i].astype(F32) for a in quarters], 1) for i in range(part.shape[1])
+    ]
+    return outs
+
+
+def x_parts(part):
+    x, z = lax.axis_index("x"), lax.axis_size("z")
+    view = part.reshape(z, 2, -1, part.shape[1])
+    give = lax.dynamic_index_in_dim(view, 1 - x, 1, False)
+    keep = lax.dynamic_index_in_dim(view, x, 1, False)
+    return give.reshape(-1, part.shape[1]), keep.reshape(-1, part.shape[1])
+
+
+def z_sum(keep, got):
+    part = low(keep.astype(F32) + got.astype(F32))
+    return lax.psum_scatter(part, "z", scatter_dimension=0, tiled=True)
+
+
+def grad_call(lefts, rights, block, count, place):
+    total, tokens, q = rights.shape
+    bounds = [0]
+    for _, _, many in lefts:
+        bounds.append(bounds[-1] + many)
+
+    def left_spec(k):
+        low_end, high_end, first = bounds[k], bounds[k + 1], lefts[k][1]
+
+        def index(i, j, x):
+            inside = jnp.logical_and(i >= low_end, i < high_end)
+            which = jnp.clip(i, low_end, high_end - 1) - low_end + first
+            at = jnp.where(inside, place(j, x[0]), place(jnp.where(i < low_end, 0, count - 1), x[0]))
+            return which, 0, at
+
+        return pl.BlockSpec((1, tokens, block), index)
+
+    def kernel(x_ref, *refs):
+        *a_refs, b_ref, o_ref = refs
+        i = pl.program_id(0)
+        for k, a_ref in enumerate(a_refs):
+
+            @pl.when(jnp.logical_and(i >= bounds[k], i < bounds[k + 1]))
+            def _(a_ref=a_ref):
+                o_ref[...] = low(tn(a_ref[0], b_ref[0]))
+
+    return pl.pallas_call(
+        kernel,
+        grid_spec=pltpu.PrefetchScalarGridSpec(
+            num_scalar_prefetch=1,
+            grid=(total, count),
+            in_specs=[left_spec(k) for k in range(len(lefts))]
+            + [pl.BlockSpec((1, tokens, q), lambda i, j, x: (i, 0, 0))],
+            out_specs=pl.BlockSpec((block, q), lambda i, j, x: (j, i)),
+        ),
+        out_shape=jax.ShapeDtypeStruct((count * block, total * q), BF16),
+        compiler_params=pltpu.CompilerParams(vmem_limit_bytes=40 << 20),
+        cost_estimate=pl.CostEstimate(
+            flops=2 * rights.size * count * block, transcendentals=0,
+            bytes_accessed=2 * (tokens * total * count * block + rights.size + count * block * total * q),
+        ),
+        name="weight_grad",
+    )(lax.axis_index("x").astype(jnp.int32).reshape(1), *[a for a, _, _ in lefts], rights)
+
+
+def all_rows(lefts, rights):
+    return grad_call(lefts, rights, 512, lefts[0][0].shape[2] // 512, lambda j, x: j)
+
+
+def x_rows(lefts, rights):
+    z = lax.axis_size("z")
+    block = lefts[0][0].shape[2] // (2 * z)
+    if block % LANES:
+        return x_parts(all_rows(lefts, rights))
+    give = grad_call(lefts, rights, block, z, lambda j, x: 2 * j + 1 - x)
+    return give, grad_call(lefts, rights, block, z, lambda j, x: 2 * j + x)
+
+
+def group_pieces(values):
     value = jnp.stack(values, 0)
     near = swap(value, "core")
     across = swap(value, "y")
     far = swap(across, "core")
-    return [jnp.concatenate([v[i] for v in (value, near, across, far)], 0) for i in range(len(values))]
+    return value, near, across, far
+
+
+def group_many(values):
+    return jnp.concatenate(group_pieces(values), 1)
 
 
 def group_sum(value):
@@ -438,7 +559,7 @@
     back = rstd * (
         d - jnp.mean(d, -1, keepdims=True) - hat * jnp.mean(d * hat, -1, keepdims=True)
     )
-    return back, jnp.sum(grad * hat, 0), jnp.sum(grad, 0)
+    return back, jnp.sum(grad * hat, 0, keepdims=True), jnp.sum(grad, 0, keepdims=True)
 
 
 def prior_of(values, seqs):
@@ -729,8 +850,7 @@
     up_vec = columns(jnp.concatenate([vectors, up_w], 0))
     vec, up = up_vec[:16].astype(F32), up_vec[16:]
     down_t = columns(down_w.T)
-    w_rkv = lax.all_gather(att_w[:3], WIDE, axis=0)
-    w_go = lax.all_gather(att_w[3:], WIDE, axis=0)
+    w_att = lax.all_gather(att_w, WIDE, axis=0)
     key_sh = key_w.reshape(-1, zs, 2, 2, 2, half)
     key_sh = lax.dynamic_index_in_dim(key_sh, y, 4, False)
     key_sh = key_sh.transpose(0, 3, 1, 2, 4).reshape(-1, 2 * quarter)
@@ -752,8 +872,10 @@
     tanh_decay = jnp.tanh(nt(decay_in, down_t[MIXCOLS:]))
     hidden_decay = low(tanh_decay)
     logdecay = -jnp.exp(vec[8] + nn(hidden_decay, up[MIXCOLS:]))
-    keys = stack_nn(key_in, w_rkv, 1)
-    values = stack_nn(value_in, w_rkv, 2)
+    mix_all = group_many([gate_in, rec_in, key_in, value_in])
+    w_att, mix_all = tie(w_att, mix_all)
+    keys = stack_nn(key_in, w_att, 1)
+    values = stack_nn(value_in, w_att, 2)
     shaped = jax.ShapeDtypeStruct
     flat, flat_low = shaped((total, width), F32), shaped((total, width), BF16)
     states = shaped((seqs, width // LANES, HEAD, LANES), BF16)
@@ -764,26 +886,24 @@
         state_kernel, seqs, [keys, values, logdecay], [flat, states, finals], "wkv_state", unit * 512
     )
     carried = chain(state, final, False)
-    recept = stack_nn(rec_in, w_rkv, 0)
-    gate_pre = stack_nn(gate_in, w_go, 0)
+    recept = stack_nn(rec_in, w_att, 0)
+    gate_pre = stack_nn(gate_in, w_att, 3)
     wkv, gated = wkv_call(
         wkv_kernel, seqs, [recept, keys, values, inclusive, carried, gate_pre, vec], [flat, flat_low],
         "wkv_forward", unit * 1536,
     )
-    first_sum = x + stack_nn(gated, w_go, 1)
+    first_sum = x + stack_nn(gated, w_att, 4)
 
     normed_two, hat_two, rstd_two = norm_forward(first_sum, vec[12], vec[13])
     delta_two = prior_of(normed_two, seqs) - normed_two
     key_mix = low(normed_two + delta_two * vec[14])
     rec_mix = low(normed_two + delta_two * vec[15])
-    key_all, rec_all = group_many([key_mix, rec_mix])
-    gated_all = group_many([gated])[0]
-    mix_all = group_many([rec_in, key_in, value_in, gate_in])
-    packed, key_all, rec_all, gated_all, mix_all = lax.optimization_barrier(
-        (packed, key_all, rec_all, gated_all, mix_all)
-    )
+    key_all = group_many([key_mix])[0]
+    key_all, rec_low, gated_low = tie(key_all, rec_mix, gated)
+    side_all = group_pieces([rec_low, gated_low])
     ffn = PackedWeights(packed, core, ff, width, half, 2 * zs)
     relu, squared = ffn.key_forward(key_all)
+    squared, side_all = tie(squared, side_all)
     value_out = group_sum(ffn.value_forward(squared))
     rec_gate = ffn.rec_forward(rec_mix)
     block_out = low(first_sum + rec_gate * value_out).reshape(tokens.shape)
@@ -792,35 +912,35 @@
     grad_value = low(g * rec_gate)
     grad_gate_in = low(g * value_out * rec_gate * (1.0 - rec_gate))
     value_all = group_many([grad_value])[0]
+    value_part = low(tn(squared, value_all)).reshape(-1, half, width)
+    value_part, value_all = tie(value_part, value_all)
+    value_part = lax.psum_scatter(value_part, ("z", "x"), scatter_dimension=0, tiled=True)[0]
     grad_key_pre = ffn.value_backward(value_all, relu)
-    g_key_mix = group_sum(ffn.key_backward(grad_key_pre))
+    g_key_mix = ffn.key_backward(grad_key_pre)
+    grad_key_pre, g_key_mix = tie(grad_key_pre, g_key_mix)
+    key_part = low(tn(key_all, grad_key_pre))
+    key_part = lax.psum_scatter(key_part, ("z", "x"), scatter_dimension=0, tiled=True)
+    g_key_mix = group_sum(g_key_mix)
     g_rec_mix = ffn.rec_backward(grad_gate_in)
-    value_part = low(tn(squared, value_all)).reshape(-1, half, width)
-    value_part = lax.psum_scatter(value_part, ("z", "x"), scatter_dimension=0, tiled=True)[0]
-    other = swap(value_part, "y")
-    first = y == 0
-    value_share = jnp.concatenate(
-        [jnp.where(first, value_part, other), jnp.where(first, other, value_part)], 0
-    ).astype(F32)
-    part = low(tn(key_all, grad_key_pre))
-    part = lax.psum_scatter(part, ("z", "x"), scatter_dimension=0, tiled=True)
-    key_share = spread_cols(part[:, None])[0].reshape(-1, 2, 2, zs, 2, half)
-    key_share = key_share.transpose(0, 3, 4, 2, 1, 5).reshape(-1, ff)
 
     g_prior = prior_back(g_key_mix * vec[14] + g_rec_mix * vec[15], seqs)
     g_normed_two = g_key_mix * (1.0 - vec[14]) + g_rec_mix * (1.0 - vec[15]) + g_prior
-    g_maa_key = jnp.sum(g_key_mix * delta_two, 0)
-    g_maa_rec = jnp.sum(g_rec_mix * delta_two, 0)
+    g_maa_key = jnp.sum(g_key_mix * delta_two, 0, keepdims=True)
+    g_maa_rec = jnp.sum(g_rec_mix * delta_two, 0, keepdims=True)
     back_two, g_gain_two, g_bias_two = norm_backward(g_normed_two, hat_two, rstd_two, vec[12])
     grad_first = g + back_two
 
     grad_att = low(grad_first)
     g_wkv, g_gate_low, g_state, gate_sums = wkv_call(
         gate_back_kernel, seqs,
-        [stack_nt(grad_att, w_go, 1), wkv, gate_pre, recept, inclusive, vec],
+        [stack_nt(grad_att, w_att, 4), wkv, gate_pre, recept, inclusive, vec],
         [flat_low, flat_low, states, sums], "gate_backward", unit * 1536,
     )
     g_state_out = chain(g_state, final, True)
+    g_state_out, grad_gate_in, grad_att, g_gate_low, value_part = tie(
+        g_state_out, grad_gate_in, grad_att, g_gate_low, value_part
+    )
+    side_near, side_across = half_cols(jnp.stack([grad_gate_in, grad_att, g_gate_low], 0))
     g_rec, g_key, g_val, g_decay_low, wkv_sums = wkv_call(
         wkv_back_kernel, seqs,
         [recept, keys, values, inclusive, logdecay, carried, g_state_out, g_wkv, vec],
@@ -829,27 +949,35 @@
     )
     gate_sums, wkv_sums = jnp.sum(gate_sums, 0), jnp.sum(wkv_sums, 0)
     projs = [g_rec, g_key, g_val, g_gate_low]
-    early = quad_grads([rec_all, gated_all, mix_all[3]], [grad_gate_in, grad_att, projs[3]])
-    late = quad_grads(mix_all[:3], projs[:3])
-    rec_share = early[0]
-    att_share = jnp.concatenate([late, early[2:], early[1:2]], 0)
+    main_near, main_across = half_cols(jnp.stack([g_rec, g_key, g_val], 0))
+    main_near, side_across = tie(main_near, side_across)
+    side_lefts = [(jnp.concatenate(side_all, 1), 0, 2), (mix_all, 0, 1)]
+    side_give, side_keep = x_rows(side_lefts, quarter_cols(side_near, side_across))
+    side_got = swap(side_give, "x")
+    main_across, side_keep = tie(main_across, side_keep)
+    main = all_rows([(mix_all, 1, 3)], quarter_cols(main_near, main_across))
+    main, g_rec, g_key, g_val, g_gate_low, g_decay_low, key_part = tie(
+        main, g_rec, g_key, g_val, g_gate_low, g_decay_low, key_part
+    )
+    main = lax.psum_scatter(main, ("z", "x"), scatter_dimension=0, tiled=True)
+    projs = [g_rec, g_key, g_val, g_gate_low]
 
     decay_up_grad = tn(hidden_decay, g_decay_low)
     g_pre_decay = low(nt(g_decay_low, up[MIXCOLS:]) * (1.0 - tanh_decay * tanh_decay))
     decay_down_grad = tn(g_pre_decay, decay_in)
     g_mixed = [
         nn(g_pre_decay, down_t[MIXCOLS:]),
-        stack_nt(projs[1], w_rkv, 1),
-        stack_nt(projs[2], w_rkv, 2),
-        stack_nt(projs[0], w_rkv, 0),
-        stack_nt(projs[3], w_go, 0),
+        stack_nt(projs[1], w_att, 1),
+        stack_nt(projs[2], w_att, 2),
+        stack_nt(projs[0], w_att, 0),
+        stack_nt(projs[3], w_att, 3),
     ]
     g_normed = g_prior_sum = None
     maa_rows, up_grads, hid_grads = [], [], []
     for i in range(5):
         offset = vec[3 + i] + nn(hid[i], ups[i])
         g_off = g_mixed[i] * delta
-        maa_rows.append(jnp.sum(g_off, 0))
+        maa_rows.append(jnp.sum(g_off, 0, keepdims=True))
         off_low = low(g_off)
         up_grads.append(tn(hid[i], off_low))
         hid_grads.append(nt(off_low, ups[i]))
@@ -858,21 +986,41 @@
         g_normed = here if g_normed is None else g_normed + here
         g_prior_sum = back if g_prior_sum is None else g_prior_sum + back
     g_pre_mix = low(jnp.concatenate(hid_grads, 1) * (1.0 - tanh_mix * tanh_mix))
+    g_pre_mix, value_part, key_part, side_got = tie(g_pre_mix, value_part, key_part, side_got)
+    side = low(side_keep.astype(F32) + side_got.astype(F32))
+    side = side.reshape(zs, -1, side.shape[1])
+    moving = line_step(side, 1, None)
     mix_down_grad = tn(g_pre_mix, mix_low)
     g_first_mix = nn(g_pre_mix, down_t[:MIXCOLS])
-    maa_first = jnp.sum(g_first_mix * delta, 0)
+    maa_first = jnp.sum(g_first_mix * delta, 0, keepdims=True)
     g_prior_sum = g_prior_sum + g_first_mix * vec[2]
     g_normed = g_normed + g_first_mix * (1.0 - vec[2]) + prior_back(g_prior_sum, seqs)
     back_one, g_gain, g_bias = norm_backward(g_normed, hat, rstd, vec[0])
     input_grad = (grad_first + back_one).reshape(tokens.shape)
 
-    vec_rows = jnp.stack(
+    vec_rows = (
         [g_gain, g_bias, maa_first] + maa_rows
-        + [wkv_sums[1], wkv_sums[0], gate_sums[0], gate_sums[1], g_gain_two, g_bias_two,
-           g_maa_key, g_maa_rec], 0,
-    )
-    packed = jnp.concatenate(up_grads + [decay_up_grad, mix_down_grad, decay_down_grad, vec_rows], 0)
+        + [wkv_sums[1:2], wkv_sums[0:1], gate_sums[0:1], gate_sums[1:2], g_gain_two, g_bias_two,
+           g_maa_key, g_maa_rec]
+    )
+    packed = pack_columns(up_grads + [decay_up_grad, mix_down_grad, decay_down_grad] + vec_rows)
+    first = y == 0
+    other = swap(value_part, "y")
+    value_share = jnp.concatenate(
+        [jnp.where(first, value_part, other), jnp.where(first, other, value_part)], 0
+    ).astype(F32)
+    key_share = spread_cols(key_part[:, None])[0].reshape(-1, 2, 2, zs, 2, half)
+    key_share = key_share.transpose(0, 3, 4, 2, 1, 5).reshape(-1, ff)
+    packed, key_share, value_share, moving = tie(packed, key_share, value_share, moving)
+    for t in range(2, zs - 1):
+        moving = line_step(side, t, moving)
+    packed, main, moving = tie(small_core(packed), main, moving)
+    side = low(line_end(side, line_step(side, zs - 1, moving)))
+    late = spread_cols(main.reshape(main.shape[0], 3, -1))
+    early = spread_cols(side.reshape(side.shape[0], 3, -1))
     packed = small_sum(packed)
+    rec_share = early[0]
+    att_share = jnp.stack(late + [early[2], early[1]], 0)
     return (
         block_out, input_grad, att_share, packed[cols : 2 * cols].T, packed[:cols],
         key_share, value_share, rec_share, packed[2 * cols :],

time: 1240 us -> 1130 us (0.911)
  waiting for transfers between devices: 465 us -> 383 us
  local copies, waits for them, and re-layouts: 159 us -> 112 us
  Pallas kernels: 198 us -> 242 us
  starting transfers between devices: 60.7 us -> 94.7 us
  other arithmetic: 120 us -> 88.1 us
  matrix products: 68.8 us -> 47.3 us
    all_gather x2 -> x1, waiting for transfers between devices: 143 us -> 38.8 us  [body(): w_att = lax.all_gather(att_w, WIDE, axis=0)]
    pallas_call x0 -> x4, Pallas kernels: none -> 46.2 us  [the longest x3 35.3 us: grad_call(): pl.pallas_call(kernel, grid_spec=pltpu.PrefetchScalarGridSpec(num_scalar_...]
    concatenate x12 -> x2, other arithmetic: 52.4 us -> 8.62 us  [the longest x1 7.51 us: group_many(): return jnp.concatenate(group_pieces(values), 1)]
    ppermute x6 -> x15, starting transfers between devices: 15.7 us -> 56.3 us  [the longest x6 46.4 us: line_step(): lax.ppermute(low(right), 'z', [(i, i + 1) for i in range(count - 1) if i...]
    ppermute x30 -> x31, waiting for transfers between devices: 242 us -> 280 us  [swap(): return lax.ppermute(value, axis, [(0, 1), (1, 0)])]
    all_gather x1, waiting for transfers between devices: 38.5 us -> 9.64 us  [body(): packed = lax.all_gather(packed, WIDE, axis=0)]
    concatenate x15 -> x1, local copies, waits for them, and re-layouts: 28 us -> 1.94 us  [body(): side_lefts = [(jnp.concatenate(side_all, 1), 0, 2), (mix_all, 0, 1)]]
    dot_general x16 -> x10, matrix products: 52.4 us -> 28.6 us  [tn(): lax.dot_general(a, b, (((0,), (0,)), ((), ())), preferred_element_type=F32)]
  transfers between devices with their start and end apart: 49 -> 57, of which waited for: 26 -> 27; matrix products, arithmetic and copies ran while one was open for 22% -> 16% of each run, Pallas kernels for 13% -> 20%
where the time goes in v3:
time: 1130 us; the launch traced here: 1120 us
  waiting for transfers between devices  383 us (34%)
  Pallas kernels  242 us (21%)
  blocking collectives  135 us (12%)
  local copies, waits for them, and re-layouts  112 us (10%)
  starting transfers between devices  94.7 us (8%)
  other arithmetic  88.1 us (8%)
  matrix products  47.3 us (4%)
  between operations  16.2 us (1%)
    ppermute x31, waiting for transfers between devices, swap(): return lax.ppermute(value, axis, [(0, 1), (1, 0)])  280 us
    all_to_all x2, blocking collectives, chain(): packed = lax.all_to_all(packed, ALL, 0, 0, tiled=True)  77.1 us
    pallas_call x6, Pallas kernels, ffn_call(): pl.pallas_call(kernel, grid_spec=pltpu.PrefetchScalarGridSpec(num_scalar_...  69.2 us
    unnamed x280, local copies, waits for them, and re-layouts  68.7 us
    pallas_call x4, Pallas kernels, wkv_call(): pl.pallas_call(kernel, grid=(seqs, width // SPAN), in_specs=[spec(a) for...  64.1 us
    all_gather x2, blocking collectives, columns(): gathered = lax.all_gather(shard, WIDE, axis=0)  57.4 us
    ppermute x6, starting transfers between devices, line_step(): lax.ppermute(low(right), 'z', [(i, i + 1) for i in range(count - 1) if i...  46.4 us
    all_gather x1, waiting for transfers between devices, body(): w_att = lax.all_gather(att_w, WIDE, axis=0)  38.8 us
  transfers between devices with their start and end apart: 57, of which 27 were waited for; matrix products, arithmetic and copies ran while one was open for 16% of the time, Pallas kernels for 20%

profile of v3, /device:TPU:0, one launch (start us, length us, event | category | flops | bytes accessed | tf_op | source)
XLA Modules:
  0.0 1116.9 jit_solution(8349831695770619812)
XLA Ops:
  19.0 31.5 %all-gather = bf16[3840,128]{1,0:T(8,128)(2,1)S(1)} all-gather(bf16[240,128]{1,0:T(8,128)(2,1)S(1)} %pad_maximum_fusion.14), channel_id=2, replica_groups=mesh['y'=2,'z'=4,'x'=2,'core'=2] {'z','x','core'}, dimensions={0}, use_global_device_ids=true | all-gather | bytes 1044480 | tf_op jit(solution)/shard_map/all_gather | solution.py:846
  54.8 25.9 %all-gather.1 = bf16[3584,128]{1,0:T(8,128)(2,1)S(1)} all-gather(bf16[224,128]{1,0:T(8,128)(2,1)S(1)} %bitcast.617), channel_id=3, replica_groups=mesh['y'=2,'z'=4,'x'=2,'core'=2] {'z','x','core'}, dimensions={0}, use_global_device_ids=true | all-gather | bytes 974848 | tf_op jit(solution)/shard_map/all_gather | solution.py:846
  92.5 91.5 %collective-permute-done.2 = bf16[4,256,2048]{2,1,0:T(8,128)(2,1)S(1)} collective-permute-done((bf16[4,256,2048]{2,1,0:T(8,128)(2,1)S(1)}, bf16[4,256,2048]{2,1,0:T(8,128)(2,1)S(1)}, u32[]{:S(2)}, u32[]{:S(2)}) %collective-permute-start.2) | collective-permute-done | bytes 4194336 | tf_op jit(solution)/shard_map/ppermute | solution.py:35
  198.7 38.8 %all-gather.7.cloned.1.call-done = bf16[80,128,2048]{2,1,0:T(8,128)(2,1)} async-done(((bf16[5,128,2048]{2,1,0:T(8,128)(2,1)}), bf16[80,128,2048]{2,1,0:T(8,128)(2,1)}) %all-gather.7.cloned.1.call-update) | async-done | bytes 41943056 | tf_op jit(solution)/shard_map/all_gather | solution.py:853
  261.7 31.7 %all_to_all.20.refs_1_ = bf16[32,80,128]{2,1,0:T(8,128)(2,1)S(1)} all-to-all(bf16[32,80,128]{2,1,0:T(8,128)(2,1)S(1)} %pad_maximum_fusion.13), channel_id=1, replica_groups=mesh['y'=2,'z'=4,'x'=2,'core'=2] {'y','z','x','core'}, dimensions={0} | all-to-all | bytes 1310720 | tf_op jit(solution)/shard_map/all_to_all | solution.py:531
  327.1 17.2 %wkv_forward.1 = (f32[256,2048]{1,0:T(8,128)S(1)}, bf16[256,2048]{1,0:T(8,128)(2,1)S(1)}) custom-call(f32[256,2048]{1,0:T(8,128)S(1)} %copy-done.15, f32[256,2048]{1,0:T(8,128)S(1)} %stack_nn.6.key_ref, f32[256,2048]{1,0:T(8,128)S(1)} %copy-done.12, f32[256,2048]{1,0:T(8,128)S(1)} %copy-done.31, bf16[2,16,64,128]{3,2,1,0:T(8,128)(2,1)} %bitcast.27.state_ref, ...), custom_call_target="tpu_custom_call" | custom-call | flops 1610612736 | bytes 14286848 | tf_op jit(solution)/shard_map/wkv_forward/pallas_call | solution.py:487
  362.7 20.1 %collective-permute-done.6 = bf16[1,256,2048]{2,1,0:T(8,128)(2,1)S(1)} collective-permute-done((bf16[1,256,2048]{2,1,0:T(8,128)(2,1)S(1)}, bf16[1,256,2048]{2,1,0:T(8,128)(2,1)S(1)}, u32[]{:S(2)}, u32[]{:S(2)}) %collective-permute-start.6) | collective-permute-done | bytes 1048608 | tf_op jit(solution)/shard_map/ppermute | solution.py:35
  389.9 47.4 %collective-permute-done.9 = bf16[2,256,2048]{2,1,0:T(8,128)(2,1)} collective-permute-done((bf16[2,256,2048]{2,1,0:T(8,128)(2,1)}, bf16[2,256,2048]{2,1,0:T(8,128)(2,1)}, u32[]{:S(2)}, u32[]{:S(2)}) %collective-permute-start.9) | collective-permute-done | bytes 2097184 | tf_op jit(solution)/shard_map/ppermute | solution.py:35
  446.9 13.4 %key_forward.1 = (bf16[1024,1792]{1,0:T(8,128)(2,1)}, bf16[1024,1792]{1,0:T(8,128)(2,1)}) custom-call(s32[1]{0:T(128)} %bitcast.28.c_ref, bf16[1024,2048]{1,0:T(8,128)(2,1)} %maximum_bitcast_fusion.a_ref, bf16[16,4608,256]{2,1,0:T(8,128)(2,1)} %bitcast.544), custom_call_target="tpu_custom_call" | custom-call | flops 7516192768 | bytes 18874368 | tf_op jit(solution)/shard_map/key_forward/pallas_call | solution.py:641
  460.4 13.2 %value_forward.1 = bf16[1024,2048]{1,0:T(8,128)(2,1)} custom-call(s32[1]{0:T(128)} %bitcast.28.c_ref, bf16[1024,1792]{1,0:T(8,128)(2,1)} %get-tuple-element.77.a_ref, bf16[8,2,4608,256]{3,2,1,0:T(8,128)(2,1)} %bitcast.545), custom_call_target="tpu_custom_call" | custom-call | flops 7516192768 | bytes 15204352 | tf_op jit(solution)/shard_map/value_forward/pallas_call | solution.py:641
  492.9 14.9 %collective-permute-done.12 = bf16[256,2048]{1,0:T(8,128)(2,1)S(1)} collective-permute-done((bf16[256,2048]{1,0:T(8,128)(2,1)S(1)}, bf16[256,2048]{1,0:T(8,128)(2,1)S(1)}, u32[]{:S(2)}, u32[]{:S(2)}) %collective-permute-start.12) | collective-permute-done | bytes 1048608 | tf_op jit(solution)/shard_map/ppermute | solution.py:35
  514.3 23.0 %collective-permute-done.14 = bf16[1,256,2048]{2,1,0:T(8,128)(2,1)S(1)} collective-permute-done((bf16[1,256,2048]{2,1,0:T(8,128)(2,1)S(1)}, bf16[1,256,2048]{2,1,0:T(8,128)(2,1)S(1)}, u32[]{:S(2)}, u32[]{:S(2)}) %collective-permute-start.14) | collective-permute-done | bytes 1048608 | tf_op jit(solution)/shard_map/ppermute | solution.py:35
  552.5 14.2 %value_backward.1.a_ref = bf16[1024,1792]{1,0:T(8,128)(2,1)} custom-call(s32[1]{0:T(128)} %bitcast.28.c_ref, bf16[1024,2048]{1,0:T(8,128)(2,1)} %maximum_bitcast_fusion.1.a_ref, bf16[1024,1792]{1,0:T(8,128)(2,1)} %get-tuple-element.79.r_ref, bf16[8,2,4608,256]{3,2,1,0:T(8,128)(2,1)} %bitcast.547), custom_call_target="tpu_custom_call" | custom-call | flops 7516192768 | bytes 15204352 | tf_op jit(solution)/shard_map/value_backward/pallas_call | solution.py:641
  566.7 12.2 %key_backward.1 = bf16[1024,2048]{1,0:T(8,128)(2,1)} custom-call(s32[1]{0:T(128)} %bitcast.28.c_ref, bf16[1024,1792]{1,0:T(8,128)(2,1)} %value_backward.1.a_ref, bf16[16,4608,256]{2,1,0:T(8,128)(2,1)} %bitcast.548), custom_call_target="tpu_custom_call" | custom-call | flops 7516192768 | bytes 15204352 | tf_op jit(solution)/shard_map/key_backward/pallas_call | solution.py:641
  604.2 16.9 %collective-permute-done.17 = bf16[256,2048]{1,0:T(8,128)(2,1)S(1)} collective-permute-done((bf16[256,2048]{1,0:T(8,128)(2,1)}, bf16[256,2048]{1,0:T(8,128)(2,1)S(1)}, u32[]{:S(2)}, u32[]{:S(2)}) %collective-permute-start.17) | collective-permute-done | bytes 1048608 | tf_op jit(solution)/shard_map/ppermute | solution.py:35
  643.8 13.4 %gate_backward.1 = (bf16[256,2048]{1,0:T(8,128)(2,1)S(1)}, bf16[256,2048]{1,0:T(8,128)(2,1)S(1)}, bf16[2,16,64,128]{3,2,1,0:T(8,128)(2,1)S(1)}, f32[2,8,2048]{2,1,0:T(8,128)S(1)}) custom-call(f32[256,2048]{1,0:T(8,128)S(1)} %stack_nt.5.grad_ref, f32[256,2048]{1,0:T(8,128)S(1)} %copy-done.46, f32[256,2048]{1,0:T(8,128)S(1)} %copy-done.20, ...), custom_call_target="tpu_custom_call" | custom-call | flops 1610612736 | bytes 13369344 | tf_op jit(solution)/shard_map/gate_backward/pallas_call | solution.py:487
  659.2 45.4 %all_to_all.21.refs_1_ = bf16[32,80,128]{2,1,0:T(8,128)(2,1)S(1)} all-to-all(bf16[32,80,128]{2,1,0:T(8,128)(2,1)S(1)} %pad_maximum_fusion.12), channel_id=1, replica_groups=mesh['y'=2,'z'=4,'x'=2,'core'=2] {'y','z','x','core'}, dimensions={0} | all-to-all | bytes 1310720 | tf_op jit(solution)/shard_map/all_to_all | solution.py:531
  709.4 25.8 %all-to-all-done.3 = bf16[32,64,128]{2,1,0:T(8,128)(2,1)} async-done(((bf16[32,64,128]{2,1,0:T(8,128)(2,1)}), bf16[32,64,128]{2,1,0:T(8,128)(2,1)}, u32[]{:S(2)}, u32[]{:S(2)}) %all-to-all-start.3) | async-done | bytes 524320 | tf_op jit(solution)/shard_map/all_to_all | solution.py:546
  743.0 24.9 %wkv_backward.1 = (bf16[256,2048]{1,0:T(8,128)(2,1)S(1)}, bf16[256,2048]{1,0:T(8,128)(2,1)S(1)}, bf16[256,2048]{1,0:T(8,128)(2,1)S(1)}, bf16[256,2048]{1,0:T(8,128)(2,1)S(1)}, f32[2,8,2048]{2,1,0:T(8,128)S(1)}) custom-call(f32[256,2048]{1,0:T(8,128)S(1)} %copy-done.17, f32[256,2048]{1,0:T(8,128)S(1)} %stack_nn.6.key_ref, f32[256,2048]{1,0:T(8,128)S(1)} %copy-done.13, ...), custom_call_target="tpu_custom_call" | custom-call | flops 4294967296 | bytes 17039360 | tf_op jit(solution)/shard_map/wkv_backward/pallas_call | solution.py:487
  798.7 14.3 %collective-permute-done.20 = bf16[3,256,1024]{2,1,0:T(8,128)(2,1)S(1)} collective-permute-done((bf16[3,256,1024]{2,1,0:T(8,128)(2,1)}, bf16[3,256,1024]{2,1,0:T(8,128)(2,1)S(1)}, u32[]{:S(2)}, u32[]{:S(2)}) %collective-permute-start.20) | collective-permute-done | bytes 1572896 | tf_op jit(solution)/shard_map/ppermute | solution.py:35
  816.3 11.4 %weight_grad.5 = bf16[1024,1536]{1,0:T(8,128)(2,1)} custom-call(s32[1]{0:T(128)} %bitcast.75.x_ref, bf16[2,1024,2048]{2,1,0:T(8,128)(2,1)} %copy-done.57, bf16[4,1024,2048]{2,1,0:T(8,128)(2,1)} %pad_maximum_fusion.refs_1_.refs_0_, bf16[3,1024,512]{2,1,0:T(8,128)(2,1)S(1)} %bitcast.511), custom_call_target="tpu_custom_call" | custom-call | flops 3221225472 | bytes 12582912 | tf_op jit(solution)/shard_map/weight_grad/pallas_call | solution.py:208
  829.9 13.5 %weight_grad.4 = bf16[2048,1536]{1,0:T(8,128)(2,1)S(1)} custom-call(s32[1]{0:T(128)} %bitcast.75.x_ref, bf16[4,1024,2048]{2,1,0:T(8,128)(2,1)} %pad_maximum_fusion.refs_1_.refs_0_, bf16[3,1024,512]{2,1,0:T(8,128)(2,1)S(1)} %bitcast.520), custom_call_target="tpu_custom_call" | custom-call | flops 6442450944 | bytes 22020096 | tf_op jit(solution)/shard_map/weight_grad/pallas_call | solution.py:208
  891.2 15.7 %collective-permute-done.23 = bf16[1024,1536]{1,0:T(8,128)(2,1)} collective-permute-done((bf16[1024,1536]{1,0:T(8,128)(2,1)}, bf16[1024,1536]{1,0:T(8,128)(2,1)}, u32[]{:S(2)}, u32[]{:S(2)}) %collective-permute-start.23) | collective-permute-done | bytes 3145760 | tf_op jit(solution)/shard_map/ppermute | solution.py:35
  1019.6 28.9 %collective-permute-start.37 = (bf16[256,1536]{0,1:T(8,128)(2,1)S(1)}, bf16[256,1536]{0,1:T(8,128)(2,1)S(1)}, u32[]{:S(2)}, u32[]{:S(2)}) collective-permute-start(bf16[256,1536]{0,1:T(8,128)(2,1)S(1)} %fusion.45), channel_id=1, source_target_pairs={{0,4},{4,8},{8,12},{1,5},{5,9},{9,13},{2,6},{6,10},{10,14},{3,7},{... | collective-permute-start | bytes 2359304 | tf_op jit(solution)/shard_map/ppermute | solution.py:66
  (557 shorter events, 495.5 us)
Async XLA Ops:
  7.2 230.3 %all-gather.7.cloned.1.call-start = ((), (), s32[]{:S(2)}) async-start(), calls=%async_computation.10 | async-start | bytes 44564480 | tf_op jit(solution)/shard_map/all_gather | solution.py:853
  7.9 439.0 %all-gather.9.cloned.1.call-start = ((), (), s32[]{:S(2)}) async-start(), calls=%async_computation.11 | async-start | bytes 40108032 | tf_op jit(solution)/shard_map/all_gather | solution.py:860
  52.5 28.9 %collective-permute-start = (f32[2,2048]{1,0:T(2,128)S(1)}, f32[2,2048]{1,0:T(2,128)S(1)}, u32[]{:S(2)}, u32[]{:S(2)}) collective-permute-start(f32[2,2048]{1,0:T(2,128)S(1)} %bitcast.632), channel_id=1, source_target_pairs={{0,1},{1,2},{2,3},{3,4},{4,5},{5,6},{6,7},{7,8},{8,9},{9,10},{10,1... | collective-permute-start | bytes 49160 | tf_op jit(solution)/shard_map/ppermute | solution.py:44
  91.3 92.7 %collective-permute-start.2 = (bf16[4,256,2048]{2,1,0:T(8,128)(2,1)S(1)}, bf16[4,256,2048]{2,1,0:T(8,128)(2,1)S(1)}, u32[]{:S(2)}, u32[]{:S(2)}) collective-permute-start(bf16[4,256,2048]{2,1,0:T(8,128)(2,1)S(1)} %pad_maximum_fusion.1), channel_id=1, source_target_pairs={{0,16},{16,0},{1,17},{17,1},{2,18},{18,2},{3,19},{19,3},{4,20},{20... | collective-permute-start | bytes 12582920 | tf_op jit(solution)/shard_map/ppermute | solution.py:35
  92.4 94.0 %collective-permute-start.1 = (bf16[4,256,2048]{2,1,0:T(8,128)(2,1)S(1)}, bf16[4,256,2048]{2,1,0:T(8,128)(2,1)S(1)}, u32[]{:S(2)}, u32[]{:S(2)}) collective-permute-start(bf16[4,256,2048]{2,1,0:T(8,128)(2,1)S(1)} %pad_maximum_fusion.1), channel_id=1, source_target_pairs={{0,1},{1,0},{2,3},{3,2},{4,5},{5,4},{6,7},{7,6},{8,9},{9,8},{10,11... | collective-permute-start | bytes 12582920 | tf_op jit(solution)/shard_map/ppermute | solution.py:35
  298.2 437.0 %reduce-scatter.4.cloned.1.call-start = ((), (), s32[]{:S(2)}) async-start(), calls=%async_computation.7 | async-start | bytes 8257536 | tf_op jit(solution)/shard_map/reduce_scatter | solution.py:917
  389.3 48.0 %collective-permute-start.9 = (bf16[2,256,2048]{2,1,0:T(8,128)(2,1)}, bf16[2,256,2048]{2,1,0:T(8,128)(2,1)}, u32[]{:S(2)}, u32[]{:S(2)}) collective-permute-start(bf16[2,256,2048]{2,1,0:T(8,128)(2,1)} %pad_maximum_fusion.9), channel_id=1, source_target_pairs={{0,16},{16,0},{1,17},{17,1},{2,18},{18,2},{3,19},{19,3},{4,20},{20... | collective-permute-start | bytes 6291464 | tf_op jit(solution)/shard_map/ppermute | solution.py:35
  389.9 70.4 %collective-permute-start.8 = (bf16[2,256,2048]{2,1,0:T(8,128)(2,1)}, bf16[2,256,2048]{2,1,0:T(8,128)(2,1)}, u32[]{:S(2)}, u32[]{:S(2)}) collective-permute-start(bf16[2,256,2048]{2,1,0:T(8,128)(2,1)} %pad_maximum_fusion.9), channel_id=1, source_target_pairs={{0,1},{1,0},{2,3},{3,2},{4,5},{5,4},{6,7},{7,6},{8,9},{9,8},{10,11... | collective-permute-start | bytes 6291464 | tf_op jit(solution)/shard_map/ppermute | solution.py:35
  552.3 295.8 %reduce-scatter.6.cloned.1.call-start = ((), (), s32[]{:S(2)}) async-start(), calls=%async_computation.8 | async-start | bytes 8257536 | tf_op jit(solution)/shard_map/reduce_scatter | solution.py:922
  706.0 29.2 %all-to-all-start.3 = ((bf16[32,64,128]{2,1,0:T(8,128)(2,1)}), bf16[32,64,128]{2,1,0:T(8,128)(2,1)}, u32[]{:S(2)}, u32[]{:S(2)}) async-start(bf16[32,64,128]{2,1,0:T(8,128)(2,1)} %copy-done.43), calls=%async_computation.3 | async-start | bytes 1048576 | tf_op jit(solution)/shard_map/all_to_all | solution.py:546
  709.4 302.4 %reduce-scatter.8.cloned.1.call-start = ((), (), s32[]{:S(2)}) async-start(), calls=%async_computation.9 | async-start | bytes 7077888 | tf_op jit(solution)/shard_map/reduce_scatter | solution.py:962
  739.2 33.9 %collective-permute-start.19 = (bf16[3,256,1024]{2,1,0:T(8,128)(2,1)}, bf16[3,256,1024]{2,1,0:T(8,128)(2,1)}, u32[]{:S(2)}, u32[]{:S(2)}) collective-permute-start(bf16[3,256,1024]{2,1,0:T(8,128)(2,1)} %get-tuple-element.203), channel_id=1, source_target_pairs={{0,16},{16,0},{1,17},{17,1},{2,18},{18,2},{3,19},{19,3},{4,20},{20... | collective-permute-start | bytes 4718600 | tf_op jit(solution)/shard_map/ppermute | solution.py:35
  776.0 37.0 %collective-permute-start.20 = (bf16[3,256,1024]{2,1,0:T(8,128)(2,1)}, bf16[3,256,1024]{2,1,0:T(8,128)(2,1)S(1)}, u32[]{:S(2)}, u32[]{:S(2)}) collective-permute-start(bf16[3,256,1024]{2,1,0:T(8,128)(2,1)} %get-tuple-element.204), channel_id=1, source_target_pairs={{0,16},{16,0},{1,17},{17,1},{2,18},{18,2},{3,19},{19,3},{4,20},{20... | collective-permute-start | bytes 4718600 | tf_op jit(solution)/shard_map/ppermute | solution.py:35
  827.7 79.3 %collective-permute-start.23 = (bf16[1024,1536]{1,0:T(8,128)(2,1)}, bf16[1024,1536]{1,0:T(8,128)(2,1)}, u32[]{:S(2)}, u32[]{:S(2)}) collective-permute-start(bf16[1024,1536]{1,0:T(8,128)(2,1)} %weight_grad.5), channel_id=1, source_target_pairs={{0,2},{2,0},{1,3},{3,1},{4,6},{6,4},{5,7},{7,5},{8,10},{10,8},{9,1... | collective-permute-start | bytes 9437192 | tf_op jit(solution)/shard_map/ppermute | solution.py:35
  913.4 54.7 %collective-permute-start.25 = (bf16[128,1,1792]{2,0,1:T(8,128)(2,1)}, bf16[128,1,1792]{2,0,1:T(8,128)(2,1)}, u32[]{:S(2)}, u32[]{:S(2)}) collective-permute-start(bf16[128,1,1792]{2,0,1:T(8,128)(2,1)} %get-tuple-element.235), channel_id=1, source_target_pairs={{0,1},{1,0},{2,3},{3,2},{4,5},{5,4},{6,7},{7,6},{8,9},{9,8},{10,11... | collective-permute-start | bytes 1376264 | tf_op jit(solution)/shard_map/ppermute | solution.py:35
  913.4 55.5 %collective-permute-start.27 = (bf16[128,1,1792]{2,0,1:T(8,128)(2,1)}, bf16[128,1,1792]{2,0,1:T(8,128)(2,1)}, u32[]{:S(2)}, u32[]{:S(2)}) collective-permute-start(bf16[128,1,1792]{2,0,1:T(8,128)(2,1)} %get-tuple-element.235), channel_id=1, source_target_pairs={{0,17},{1,16},{16,1},{17,0},{2,19},{3,18},{18,3},{19,2},{4,21},{5,... | collective-permute-start | bytes 1376264 | tf_op jit(solution)/shard_map/ppermute | solution.py:158
  916.1 52.8 %collective-permute-start.26 = (bf16[128,1,1792]{2,0,1:T(8,128)(2,1)}, bf16[128,1,1792]{2,0,1:T(8,128)(2,1)}, u32[]{:S(2)}, u32[]{:S(2)}) collective-permute-start(bf16[128,1,1792]{2,0,1:T(8,128)(2,1)} %get-tuple-element.236), channel_id=1, source_target_pairs={{0,16},{16,0},{1,17},{17,1},{2,18},{18,2},{3,19},{19,3},{4,20},{20... | collective-permute-start | bytes 1376264 | tf_op jit(solution)/shard_map/ppermute | solution.py:35
  921.0 61.7 %collective-permute-start.28 = (bf16[224,2048]{1,0:T(8,128)(2,1)}, bf16[224,2048]{1,0:T(8,128)(2,1)}, u32[]{:S(2)}, u32[]{:S(2)}) collective-permute-start(bf16[224,2048]{1,0:T(8,128)(2,1)} %bitcast.78), channel_id=1, source_target_pairs={{0,16},{16,0},{1,17},{17,1},{2,18},{18,2},{3,19},{19,3},{4,20},{20... | collective-permute-start | bytes 2752520 | tf_op jit(solution)/shard_map/ppermute | solution.py:35
  942.7 43.9 %collective-permute-start.29 = (bf16[256,1536]{0,1:T(8,128)(2,1)}, bf16[256,1536]{0,1:T(8,128)(2,1)}, u32[]{:S(2)}, u32[]{:S(2)}) collective-permute-start(bf16[256,1536]{0,1:T(8,128)(2,1)} %bitcast.615), channel_id=1, source_target_pairs={{0,4},{1,5},{2,6},{3,7},{16,20},{17,21},{18,22},{19,23}} | collective-permute-start | bytes 2359304 | tf_op jit(solution)/shard_map/ppermute | solution.py:66
  1013.4 35.2 %collective-permute-start.34 = (bf16[128,3,512]{0,2,1:T(8,128)(2,1)S(1)}, bf16[128,3,512]{0,2,1:T(8,128)(2,1)S(1)}, u32[]{:S(2)}, u32[]{:S(2)}) collective-permute-start(bf16[128,3,512]{0,2,1:T(8,128)(2,1)S(1)} %get-tuple-element.239), channel_id=1, source_target_pairs={{0,1},{1,0},{2,3},{3,2},{4,5},{5,4},{6,7},{7,6},{8,9},{9,8},{10,11... | collective-permute-start | bytes 1179656 | tf_op jit(solution)/shard_map/ppermute | solution.py:35
  1013.4 36.0 %collective-permute-start.36 = (bf16[128,3,512]{0,2,1:T(8,128)(2,1)S(1)}, bf16[128,3,512]{0,2,1:T(8,128)(2,1)S(1)}, u32[]{:S(2)}, u32[]{:S(2)}) collective-permute-start(bf16[128,3,512]{0,2,1:T(8,128)(2,1)S(1)} %get-tuple-element.239), channel_id=1, source_target_pairs={{0,17},{1,16},{16,1},{17,0},{2,19},{3,18},{18,3},{19,2},{4,21},{5,... | collective-permute-start | bytes 1179656 | tf_op jit(solution)/shard_map/ppermute | solution.py:158
  1015.3 34.1 %collective-permute-start.35 = (bf16[128,3,512]{0,2,1:T(8,128)(2,1)S(1)}, bf16[128,3,512]{0,2,1:T(8,128)(2,1)S(1)}, u32[]{:S(2)}, u32[]{:S(2)}) collective-permute-start(bf16[128,3,512]{0,2,1:T(8,128)(2,1)S(1)} %get-tuple-element.240), channel_id=1, source_target_pairs={{0,16},{16,0},{1,17},{17,1},{2,18},{18,2},{3,19},{19,3},{4,20},{20... | collective-permute-start | bytes 1179656 | tf_op jit(solution)/shard_map/ppermute | solution.py:35
  1016.9 63.3 %collective-permute-start.38 = (bf16[256,1536]{0,1:T(8,128)(2,1)S(1)}, bf16[256,1536]{0,1:T(8,128)(2,1)S(1)}, u32[]{:S(2)}, u32[]{:S(2)}) collective-permute-start(bf16[256,1536]{0,1:T(8,128)(2,1)S(1)} %fusion.44), channel_id=1, source_target_pairs={{4,0},{8,4},{12,8},{5,1},{9,5},{13,9},{6,2},{10,6},{14,10},{7,3},{... | collective-permute-start | bytes 2359304 | tf_op jit(solution)/shard_map/ppermute | solution.py:67
  1019.6 60.6 %collective-permute-start.37 = (bf16[256,1536]{0,1:T(8,128)(2,1)S(1)}, bf16[256,1536]{0,1:T(8,128)(2,1)S(1)}, u32[]{:S(2)}, u32[]{:S(2)}) collective-permute-start(bf16[256,1536]{0,1:T(8,128)(2,1)S(1)} %fusion.45), channel_id=1, source_target_pairs={{0,4},{4,8},{8,12},{1,5},{5,9},{9,13},{2,6},{6,10},{10,14},{3,7},{... | collective-permute-start | bytes 2359304 | tf_op jit(solution)/shard_map/ppermute | solution.py:66
  (164 other events, 2003.9 us)
Sparse Core Ops, SparseCore 0:
  9.6 227.8 all-gather.6
  239.7 207.2 all-gather.8
  552.4 152.4 reduce-scatter.3
  708.4 139.7 reduce-scatter.5
  876.1 135.6 reduce-scatter.7

commit v4 on v3

--- a/solution.py
+++ b/solution.py
@@ -122,10 +122,14 @@
     return value.reshape(z, 2, rows, share)
 
 
-def small_sum(value):
+def small_cross(value):
     x = lax.axis_index("x")
     give = low(lax.dynamic_index_in_dim(value, 1 - x, 1, False))
-    value = line_sum(lax.dynamic_index_in_dim(value, x, 1, False) + swap(give, "x").astype(F32))
+    return lax.dynamic_index_in_dim(value, x, 1, False) + swap(give, "x").astype(F32)
+
+
+def small_sum(value):
+    value = line_sum(value)
     return value + swap(value, "y")
 
 
@@ -181,37 +185,39 @@
 
 def grad_call(lefts, rights, block, count, place):
     total, tokens, q = rights.shape
-    bounds = [0]
-    for _, _, many in lefts:
-        bounds.append(bounds[-1] + many)
-
-    def left_spec(k):
-        low_end, high_end, first = bounds[k], bounds[k + 1], lefts[k][1]
-
+    bounds, arrays, specs = [0], [], []
+
+    def left_spec(low_end, high_end, first, rows):
         def index(i, j, x):
             inside = jnp.logical_and(i >= low_end, i < high_end)
             which = jnp.clip(i, low_end, high_end - 1) - low_end + first
             at = jnp.where(inside, place(j, x[0]), place(jnp.where(i < low_end, 0, count - 1), x[0]))
             return which, 0, at
 
-        return pl.BlockSpec((1, tokens, block), index)
+        return pl.BlockSpec((1, rows, block), index)
+
+    for pieces, first, many in lefts:
+        bounds.append(bounds[-1] + many)
+        arrays.extend(pieces)
+        specs.extend(left_spec(bounds[-2], bounds[-1], first, p.shape[1]) for p in pieces)
 
     def kernel(x_ref, *refs):
         *a_refs, b_ref, o_ref = refs
         i = pl.program_id(0)
-        for k, a_ref in enumerate(a_refs):
+        parts = len(lefts[0][0])
+        for k in range(len(lefts)):
 
             @pl.when(jnp.logical_and(i >= bounds[k], i < bounds[k + 1]))
-            def _(a_ref=a_ref):
-                o_ref[...] = low(tn(a_ref[0], b_ref[0]))
+            def _(mine=a_refs[k * parts : (k + 1) * parts]):
+                left = jnp.concatenate([a[0] for a in mine], 0)
+                o_ref[...] = low(tn(left, b_ref[0]))
 
     return pl.pallas_call(
         kernel,
         grid_spec=pltpu.PrefetchScalarGridSpec(
             num_scalar_prefetch=1,
             grid=(total, count),
-            in_specs=[left_spec(k) for k in range(len(lefts))]
-            + [pl.BlockSpec((1, tokens, q), lambda i, j, x: (i, 0, 0))],
+            in_specs=specs + [pl.BlockSpec((1, tokens, q), lambda i, j, x: (i, 0, 0))],
             out_specs=pl.BlockSpec((block, q), lambda i, j, x: (j, i)),
         ),
         out_shape=jax.ShapeDtypeStruct((count * block, total * q), BF16),
@@ -221,16 +227,16 @@
             bytes_accessed=2 * (tokens * total * count * block + rights.size + count * block * total * q),
         ),
         name="weight_grad",
-    )(lax.axis_index("x").astype(jnp.int32).reshape(1), *[a for a, _, _ in lefts], rights)
+    )(lax.axis_index("x").astype(jnp.int32).reshape(1), *arrays, rights)
 
 
 def all_rows(lefts, rights):
-    return grad_call(lefts, rights, 512, lefts[0][0].shape[2] // 512, lambda j, x: j)
+    return grad_call(lefts, rights, 512, lefts[0][0][0].shape[2] // 512, lambda j, x: j)
 
 
 def x_rows(lefts, rights):
     z = lax.axis_size("z")
-    block = lefts[0][0].shape[2] // (2 * z)
+    block = lefts[0][0][0].shape[2] // (2 * z)
     if block % LANES:
         return x_parts(all_rows(lefts, rights))
     give = grad_call(lefts, rights, block, z, lambda j, x: 2 * j + 1 - x)
@@ -519,7 +525,7 @@
     lax.fori_loop(0, count, one, jnp.zeros((rows, LANES), F32))
 
 
-def chain(state, finals, reverse):
+def chain(state, finals, reverse, beside=None):
     count = lax.axis_size(ALL)
     pairs = state.shape[0] * state.shape[1]
     split = count // pairs
@@ -529,6 +535,7 @@
         logs = jnp.repeat(logs, split, axis=0)
     packed = jnp.concatenate([state.reshape(count, rows, LANES), logs], 1)
     packed = lax.all_to_all(packed, ALL, 0, 0, tiled=True)
+    packed, beside = tie(packed, beside)
     first = lax.rem(lax.axis_index(ALL), split) * rows
     entering = pl.pallas_call(
         lambda *refs: chain_kernel(*refs, rows=rows, reverse=reverse),
@@ -543,7 +550,7 @@
         compiler_params=pltpu.CompilerParams(vmem_limit_bytes=40 << 20),
         name="chain",
     )(first.astype(jnp.int32).reshape(1), packed)
-    return lax.all_to_all(entering, ALL, 0, 0, tiled=True).reshape(state.shape)
+    return lax.all_to_all(entering, ALL, 0, 0, tiled=True).reshape(state.shape), beside
 
 
 def norm_forward(values, gain, bias):
@@ -628,6 +635,104 @@
     )(value, shards)
 
 
+def other_half(shards, which):
+    core = lax.axis_index("core")
+    devices, n, rows, cols = shards.shape
+    quarter = cols // 4
+    own = lax.dynamic_slice(
+        shards, (0, n - 1, 0, (2 * which + core) * quarter), (devices, 1, rows, quarter)
+    )
+    return swap(own.reshape(devices, rows, quarter), "y")
+
+
+def places():
+    return jnp.stack([lax.axis_index("y"), lax.axis_index("core")]).astype(jnp.int32)
+
+
+def half_nn(value, shards, which, got, near):
+    devices, n, rows, cols = shards.shape
+    tile = cols // 4
+
+    def kernel(p_ref, a_ref, w_ref, g_ref, n_ref, o_ref):
+        t = pl.program_id(0)
+
+        def put(w):
+            w = w.reshape(devices * rows, tile)
+            o_ref[...] = jnp.dot(a_ref[...], w, preferred_element_type=F32)
+
+        pl.when(t < 2)(lambda: put(w_ref[...]))
+        pl.when(t == 2)(lambda: put(g_ref[...]))
+        pl.when(t == 3)(lambda: put(n_ref[...]))
+
+    def out_at(t, p):
+        other = 2 * (1 - p[0]) + jnp.where(t == 2, p[1], 1 - p[1])
+        return 0, jnp.where(t < 2, 2 * p[0] + t, other)
+
+    whole = pl.BlockSpec(got.shape, lambda t, p: (0, 0, 0))
+    return pl.pallas_call(
+        kernel,
+        grid_spec=pltpu.PrefetchScalarGridSpec(
+            num_scalar_prefetch=1,
+            grid=(4,),
+            in_specs=[
+                pl.BlockSpec(value.shape, lambda t, p: (0, 0)),
+                pl.BlockSpec(
+                    (devices, 1, rows, tile),
+                    lambda t, p: (0, n - 1, 0, 2 * which + jnp.minimum(t, 1)),
+                ),
+                whole,
+                whole,
+            ],
+            out_specs=pl.BlockSpec((value.shape[0], tile), out_at),
+        ),
+        out_shape=jax.ShapeDtypeStruct((value.shape[0], cols), F32),
+        compiler_params=pltpu.CompilerParams(vmem_limit_bytes=48 << 20),
+        cost_estimate=pl.CostEstimate(
+            flops=2 * value.size * cols, transcendentals=0,
+            bytes_accessed=2 * value.size + 2 * devices * rows * cols + 4 * value.shape[0] * cols,
+        ),
+        name="half_nn",
+    )(places(), value, shards, got, near)
+
+
+def half_nt(value, shards, which, got, near):
+    devices, n, rows, cols = shards.shape
+    wide = 512
+    group = wide // rows
+    tile = cols // 4
+    tokens = value.shape[0]
+
+    def kernel(p_ref, a_ref, b_ref, c_ref, w_ref, g_ref, n_ref, o_ref):
+        total = nt(a_ref[...], w_ref[...].reshape(wide, 2 * tile))
+        total = total + nt(b_ref[...], g_ref[...].reshape(wide, tile))
+        o_ref[...] = total + nt(c_ref[...], n_ref[...].reshape(wide, tile))
+
+    part = pl.BlockSpec((group, rows, tile), lambda j, p: (j, 0, 0))
+    return pl.pallas_call(
+        kernel,
+        grid_spec=pltpu.PrefetchScalarGridSpec(
+            num_scalar_prefetch=1,
+            grid=(devices // group,),
+            in_specs=[
+                pl.BlockSpec((tokens, 2 * tile), lambda j, p: (0, p[0])),
+                pl.BlockSpec((tokens, tile), lambda j, p: (0, 2 * (1 - p[0]) + p[1])),
+                pl.BlockSpec((tokens, tile), lambda j, p: (0, 2 * (1 - p[0]) + 1 - p[1])),
+                pl.BlockSpec((group, 1, rows, 2 * tile), lambda j, p: (j, n - 1, 0, which)),
+                part,
+                part,
+            ],
+            out_specs=pl.BlockSpec((tokens, wide), lambda j, p: (0, j)),
+        ),
+        out_shape=jax.ShapeDtypeStruct((tokens, devices * rows), F32),
+        compiler_params=pltpu.CompilerParams(vmem_limit_bytes=40 << 20),
+        cost_estimate=pl.CostEstimate(
+            flops=2 * value.size * devices * rows, transcendentals=0,
+            bytes_accessed=2 * value.size + 2 * devices * rows * cols + 4 * tokens * devices * rows,
+        ),
+        name="half_nt",
+    )(places(), value, value, value, shards, got, near)
+
+
 TILE = 256
 
 
@@ -850,7 +955,9 @@
     up_vec = columns(jnp.concatenate([vectors, up_w], 0))
     vec, up = up_vec[:16].astype(F32), up_vec[16:]
     down_t = columns(down_w.T)
-    w_att = lax.all_gather(att_w, WIDE, axis=0)
+    halves = [piece(att_w[i], y, width // 2, 1) for i in (3, 4)]
+    w_att = jnp.concatenate([att_w[:3], jnp.concatenate(halves, 1)[None]], 0)
+    w_att = lax.all_gather(w_att, WIDE, axis=0)
     key_sh = key_w.reshape(-1, zs, 2, 2, 2, half)
     key_sh = lax.dynamic_index_in_dim(key_sh, y, 4, False)
     key_sh = key_sh.transpose(0, 3, 1, 2, 4).reshape(-1, 2 * quarter)
@@ -872,8 +979,10 @@
     tanh_decay = jnp.tanh(nt(decay_in, down_t[MIXCOLS:]))
     hidden_decay = low(tanh_decay)
     logdecay = -jnp.exp(vec[8] + nn(hidden_decay, up[MIXCOLS:]))
-    mix_all = group_many([gate_in, rec_in, key_in, value_in])
+    mix_all = group_pieces([gate_in, rec_in, key_in, value_in])
     w_att, mix_all = tie(w_att, mix_all)
+    gate_other = other_half(w_att, 0)
+    out_other = other_half(w_att, 1)
     keys = stack_nn(key_in, w_att, 1)
     values = stack_nn(value_in, w_att, 2)
     shaped = jax.ShapeDtypeStruct
@@ -885,25 +994,27 @@
     inclusive, state, final = wkv_call(
         state_kernel, seqs, [keys, values, logdecay], [flat, states, finals], "wkv_state", unit * 512
     )
-    carried = chain(state, final, False)
+    carried, gate_other = chain(state, final, False, gate_other)
+    gate_other = (gate_other, swap(gate_other, "core"))
+    carried, out_other = tie(carried, out_other)
+    out_other = (out_other, swap(out_other, "core"))
     recept = stack_nn(rec_in, w_att, 0)
-    gate_pre = stack_nn(gate_in, w_att, 3)
+    gate_pre = half_nn(gate_in, w_att, 0, *gate_other)
     wkv, gated = wkv_call(
         wkv_kernel, seqs, [recept, keys, values, inclusive, carried, gate_pre, vec], [flat, flat_low],
         "wkv_forward", unit * 1536,
     )
-    first_sum = x + stack_nn(gated, w_att, 4)
+    first_sum = x + half_nn(gated, w_att, 1, *out_other)
 
     normed_two, hat_two, rstd_two = norm_forward(first_sum, vec[12], vec[13])
     delta_two = prior_of(normed_two, seqs) - normed_two
     key_mix = low(normed_two + delta_two * vec[14])
     rec_mix = low(normed_two + delta_two * vec[15])
     key_all = group_many([key_mix])[0]
-    key_all, rec_low, gated_low = tie(key_all, rec_mix, gated)
-    side_all = group_pieces([rec_low, gated_low])
+    gated_all = group_pieces([gated])
+    packed, key_all, gated_all = tie(packed, key_all, gated_all)
     ffn = PackedWeights(packed, core, ff, width, half, 2 * zs)
     relu, squared = ffn.key_forward(key_all)
-    squared, side_all = tie(squared, side_all)
     value_out = group_sum(ffn.value_forward(squared))
     rec_gate = ffn.rec_forward(rec_mix)
     block_out = low(first_sum + rec_gate * value_out).reshape(tokens.shape)
@@ -933,14 +1044,15 @@
     grad_att = low(grad_first)
     g_wkv, g_gate_low, g_state, gate_sums = wkv_call(
         gate_back_kernel, seqs,
-        [stack_nt(grad_att, w_att, 4), wkv, gate_pre, recept, inclusive, vec],
+        [half_nt(grad_att, w_att, 1, *out_other), wkv, gate_pre, recept, inclusive, vec],
         [flat_low, flat_low, states, sums], "gate_backward", unit * 1536,
     )
-    g_state_out = chain(g_state, final, True)
-    g_state_out, grad_gate_in, grad_att, g_gate_low, value_part = tie(
-        g_state_out, grad_gate_in, grad_att, g_gate_low, value_part
-    )
-    side_near, side_across = half_cols(jnp.stack([grad_gate_in, grad_att, g_gate_low], 0))
+    g_state_out, (rights, rec_low) = chain(
+        g_state, final, True, ([grad_gate_in, grad_att, g_gate_low], rec_mix)
+    )
+    side_near, side_across = half_cols(jnp.stack(rights, 0))
+    rec_all = group_pieces([rec_low])
+    g_state_out, value_part = tie(g_state_out, value_part)
     g_rec, g_key, g_val, g_decay_low, wkv_sums = wkv_call(
         wkv_back_kernel, seqs,
         [recept, keys, values, inclusive, logdecay, carried, g_state_out, g_wkv, vec],
@@ -950,8 +1062,8 @@
     gate_sums, wkv_sums = jnp.sum(gate_sums, 0), jnp.sum(wkv_sums, 0)
     projs = [g_rec, g_key, g_val, g_gate_low]
     main_near, main_across = half_cols(jnp.stack([g_rec, g_key, g_val], 0))
-    main_near, side_across = tie(main_near, side_across)
-    side_lefts = [(jnp.concatenate(side_all, 1), 0, 2), (mix_all, 0, 1)]
+    main_near, side_across, rec_all = tie(main_near, side_across, rec_all)
+    side_lefts = [(rec_all, 0, 1), (gated_all, 0, 1), (mix_all, 0, 1)]
     side_give, side_keep = x_rows(side_lefts, quarter_cols(side_near, side_across))
     side_got = swap(side_give, "x")
     main_across, side_keep = tie(main_across, side_keep)
@@ -970,7 +1082,7 @@
         stack_nt(projs[1], w_att, 1),
         stack_nt(projs[2], w_att, 2),
         stack_nt(projs[0], w_att, 0),
-        stack_nt(projs[3], w_att, 3),
+        half_nt(projs[3], w_att, 0, *gate_other),
     ]
     g_normed = g_prior_sum = None
     maa_rows, up_grads, hid_grads = [], [], []
@@ -986,10 +1098,7 @@
         g_normed = here if g_normed is None else g_normed + here
         g_prior_sum = back if g_prior_sum is None else g_prior_sum + back
     g_pre_mix = low(jnp.concatenate(hid_grads, 1) * (1.0 - tanh_mix * tanh_mix))
-    g_pre_mix, value_part, key_part, side_got = tie(g_pre_mix, value_part, key_part, side_got)
-    side = low(side_keep.astype(F32) + side_got.astype(F32))
-    side = side.reshape(zs, -1, side.shape[1])
-    moving = line_step(side, 1, None)
+    g_pre_mix, value_part, key_part = tie(g_pre_mix, value_part, key_part)
     mix_down_grad = tn(g_pre_mix, mix_low)
     g_first_mix = nn(g_pre_mix, down_t[:MIXCOLS])
     maa_first = jnp.sum(g_first_mix * delta, 0, keepdims=True)
@@ -1011,10 +1120,14 @@
     ).astype(F32)
     key_share = spread_cols(key_part[:, None])[0].reshape(-1, 2, 2, zs, 2, half)
     key_share = key_share.transpose(0, 3, 4, 2, 1, 5).reshape(-1, ff)
-    packed, key_share, value_share, moving = tie(packed, key_share, value_share, moving)
+    packed, key_share, value_share, side_got = tie(packed, key_share, value_share, side_got)
+    side = low(side_keep.astype(F32) + side_got.astype(F32))
+    side = side.reshape(zs, -1, side.shape[1])
+    moving = line_step(side, 1, None)
+    packed, moving, main = tie(small_core(packed), moving, main)
     for t in range(2, zs - 1):
         moving = line_step(side, t, moving)
-    packed, main, moving = tie(small_core(packed), main, moving)
+    packed, moving = tie(small_cross(packed), moving)
     side = low(line_end(side, line_step(side, zs - 1, moving)))
     late = spread_cols(main.reshape(main.shape[0], 3, -1))
     early = spread_cols(side.reshape(side.shape[0], 3, -1))

time: 1130 us -> 1080 us (0.956)
  blocking collectives: 135 us -> 100 us
  waiting for transfers between devices: 383 us -> 361 us
    all_gather x1, waiting for transfers between devices: 38.8 us -> 0.82 us  [body(): w_att = lax.all_gather(w_att, WIDE, axis=0)]
    all_to_all x2 -> x1, blocking collectives: 77.1 us -> 42.4 us  [chain(): packed = lax.all_to_all(packed, ALL, 0, 0, tiled=True)]
    pallas_call x0 -> x4, Pallas kernels: none -> 27.9 us  [the longest x2 14.5 us: half_nn(): pl.pallas_call(kernel, grid_spec=pltpu.PrefetchScalarGridSpec(num_scalar_...]
    ppermute x31 -> x38, waiting for transfers between devices: 280 us -> 303 us  [swap(): return lax.ppermute(value, axis, [(0, 1), (1, 0)])]
    ppermute x31 -> x38, starting transfers between devices: 22.8 us -> 42.5 us  [swap(): return lax.ppermute(value, axis, [(0, 1), (1, 0)])]
    ppermute x6, starting transfers between devices: 46.4 us -> 29.7 us  [line_step(): lax.ppermute(low(right), 'z', [(i, i + 1) for i in range(count - 1) if i...]
    pallas_call x5 -> x3, Pallas kernels: 30.5 us -> 17.3 us  [stack_nt(): pl.pallas_call(kernel, grid=(devices // group,), out_shape=jax.ShapeDtype...]
    unnamed x280 -> x301, local copies, waits for them, and re-layouts: 68.7 us -> 56.1 us
  transfers between devices with their start and end apart: 57 -> 65, of which waited for: 27 -> 29; matrix products, arithmetic and copies ran while one was open for 16% -> 16% of each run, Pallas kernels for 20% -> 21%
where the time goes in v4:
time: 1080 us; the launch traced here: 1070 us
  waiting for transfers between devices  361 us (33%)
  Pallas kernels  251 us (23%)
  local copies, waits for them, and re-layouts  113 us (10%)
  starting transfers between devices  101 us (9%)
  blocking collectives  100 us (9%)
  other arithmetic  83.9 us (8%)
  matrix products  44.6 us (4%)
  between operations  16.3 us (2%)
    ppermute x38, waiting for transfers between devices, swap(): return lax.ppermute(value, axis, [(0, 1), (1, 0)])  303 us
    pallas_call x6, Pallas kernels, ffn_call(): pl.pallas_call(kernel, grid_spec=pltpu.PrefetchScalarGridSpec(num_scalar_...  69 us
    pallas_call x4, Pallas kernels, wkv_call(): pl.pallas_call(kernel, grid=(seqs, width // SPAN), in_specs=[spec(a) for...  64.5 us
    all_gather x2, blocking collectives, columns(): gathered = lax.all_gather(shard, WIDE, axis=0)  57.6 us
    unnamed x301, local copies, waits for them, and re-layouts  56.1 us
    ppermute x38, starting transfers between devices, swap(): return lax.ppermute(value, axis, [(0, 1), (1, 0)])  42.5 us
    all_to_all x1, blocking collectives, chain(): packed = lax.all_to_all(packed, ALL, 0, 0, tiled=True)  42.4 us
    pallas_call x3, Pallas kernels, grad_call(): pl.pallas_call(kernel, grid_spec=pltpu.PrefetchScalarGridSpec(num_scalar_...  39.6 us
  transfers between devices with their start and end apart: 65, of which 29 were waited for; matrix products, arithmetic and copies ran while one was open for 16% of the time, Pallas kernels for 21%

profile of v4, /device:TPU:0, one launch (start us, length us, event | category | flops | bytes accessed | tf_op | source)
XLA Modules:
  0.0 1071.0 jit_solution(18208809662346937705)
XLA Ops:
  24.3 31.5 %all-gather = bf16[3840,128]{1,0:T(8,128)(2,1)S(1)} all-gather(bf16[240,128]{1,0:T(8,128)(2,1)S(1)} %pad_maximum_fusion.13), channel_id=2, replica_groups=mesh['y'=2,'z'=4,'x'=2,'core'=2] {'z','x','core'}, dimensions={0}, use_global_device_ids=true | all-gather | bytes 1044480 | tf_op jit(solution)/shard_map/all_gather | solution.py:951
  60.2 26.1 %all-gather.1 = bf16[3584,128]{1,0:T(8,128)(2,1)S(1)} all-gather(bf16[224,128]{1,0:T(8,128)(2,1)S(1)} %bitcast.629), channel_id=3, replica_groups=mesh['y'=2,'z'=4,'x'=2,'core'=2] {'z','x','core'}, dimensions={0}, use_global_device_ids=true | all-gather | bytes 974848 | tf_op jit(solution)/shard_map/all_gather | solution.py:951
  101.1 91.8 %collective-permute-done.2.refs_10_.refs_2_ = bf16[4,256,2048]{2,1,0:T(8,128)(2,1)} collective-permute-done((bf16[4,256,2048]{2,1,0:T(8,128)(2,1)}, bf16[4,256,2048]{2,1,0:T(8,128)(2,1)}, u32[]{:S(2)}, u32[]{:S(2)}) %collective-permute-start.2) | collective-permute-done | bytes 4194336 | tf_op jit(solution)/shard_map/ppermute | solution.py:35
  239.3 24.7 %all-to-all-done.refs_1_ = bf16[32,80,128]{2,1,0:T(8,128)(2,1)} async-done(((bf16[32,80,128]{2,1,0:T(8,128)(2,1)}), bf16[32,80,128]{2,1,0:T(8,128)(2,1)}, u32[]{:S(2)}, u32[]{:S(2)}) %all-to-all-start) | async-done | bytes 655392 | tf_op jit(solution)/shard_map/all_to_all | solution.py:537
  271.4 40.1 %collective-permute-done.5.g_ref = bf16[16,128,512]{2,1,0:T(8,128)(2,1)} collective-permute-done((bf16[16,128,512]{2,1,0:T(8,128)(2,1)}, bf16[16,128,512]{2,1,0:T(8,128)(2,1)}, u32[]{:S(2)}, u32[]{:S(2)}) %collective-permute-start.5) | collective-permute-done | bytes 2097184 | tf_op jit(solution)/shard_map/ppermute | solution.py:35
  329.2 17.2 %wkv_forward.1 = (f32[256,2048]{1,0:T(8,128)S(1)}, bf16[256,2048]{1,0:T(8,128)(2,1)S(1)}) custom-call(f32[256,2048]{1,0:T(8,128)S(1)} %stack_nn.3.rec_ref, f32[256,2048]{1,0:T(8,128)S(1)} %stack_nn.4.key_ref, f32[256,2048]{1,0:T(8,128)S(1)} %copy-done.7, f32[256,2048]{1,0:T(8,128)S(1)} %copy-done.29, bf16[2,16,64,128]{3,2,1,0:T(8,128)(2,1)} %bitcast.33.state_ref, ...), custom_call_target="tpu_custom_call" | custom-call | flops 1610612736 | bytes 14286848 | tf_op jit(solution)/shard_map/wkv_forward/pallas_call | solution.py:493
  369.2 24.0 %collective-permute-done.10 = bf16[1,256,2048]{2,1,0:T(8,128)(2,1)S(1)} collective-permute-done((bf16[1,256,2048]{2,1,0:T(8,128)(2,1)S(1)}, bf16[1,256,2048]{2,1,0:T(8,128)(2,1)S(1)}, u32[]{:S(2)}, u32[]{:S(2)}) %collective-permute-start.10) | collective-permute-done | bytes 1048608 | tf_op jit(solution)/shard_map/ppermute | solution.py:35
  393.7 17.6 %collective-permute-done.13.refs_6_ = bf16[1,256,2048]{2,1,0:T(8,128)(2,1)S(1)} collective-permute-done((bf16[1,256,2048]{2,1,0:T(8,128)(2,1)S(1)}, bf16[1,256,2048]{2,1,0:T(8,128)(2,1)S(1)}, u32[]{:S(2)}, u32[]{:S(2)}) %collective-permute-start.13) | collective-permute-done | bytes 1048608 | tf_op jit(solution)/shard_map/ppermute | solution.py:35
  415.7 13.4 %key_forward.1 = (bf16[1024,1792]{1,0:T(8,128)(2,1)}, bf16[1024,1792]{1,0:T(8,128)(2,1)}) custom-call(s32[1]{0:T(128)} %bitcast.2.c_ref, bf16[1024,2048]{1,0:T(8,128)(2,1)} %maximum_bitcast_fusion.a_ref, bf16[16,4608,256]{2,1,0:T(8,128)(2,1)} %bitcast.557), custom_call_target="tpu_custom_call" | custom-call | flops 7516192768 | bytes 18874368 | tf_op jit(solution)/shard_map/key_forward/pallas_call | solution.py:746
  429.1 13.1 %value_forward.1 = bf16[1024,2048]{1,0:T(8,128)(2,1)} custom-call(s32[1]{0:T(128)} %bitcast.2.c_ref, bf16[1024,1792]{1,0:T(8,128)(2,1)} %get-tuple-element.91.a_ref, bf16[8,2,4608,256]{3,2,1,0:T(8,128)(2,1)} %bitcast.558), custom_call_target="tpu_custom_call" | custom-call | flops 7516192768 | bytes 15204352 | tf_op jit(solution)/shard_map/value_forward/pallas_call | solution.py:746
  462.7 14.0 %collective-permute-done.16 = bf16[256,2048]{1,0:T(8,128)(2,1)} collective-permute-done((bf16[256,2048]{1,0:T(8,128)(2,1)}, bf16[256,2048]{1,0:T(8,128)(2,1)}, u32[]{:S(2)}, u32[]{:S(2)}) %collective-permute-start.16) | collective-permute-done | bytes 1048608 | tf_op jit(solution)/shard_map/ppermute | solution.py:35
  482.6 23.6 %collective-permute-done.18 = bf16[1,256,2048]{2,1,0:T(8,128)(2,1)S(1)} collective-permute-done((bf16[1,256,2048]{2,1,0:T(8,128)(2,1)S(1)}, bf16[1,256,2048]{2,1,0:T(8,128)(2,1)S(1)}, u32[]{:S(2)}, u32[]{:S(2)}) %collective-permute-start.18) | collective-permute-done | bytes 1048608 | tf_op jit(solution)/shard_map/ppermute | solution.py:35
  521.3 14.2 %value_backward.1.a_ref = bf16[1024,1792]{1,0:T(8,128)(2,1)} custom-call(s32[1]{0:T(128)} %bitcast.2.c_ref, bf16[1024,2048]{1,0:T(8,128)(2,1)} %maximum_bitcast_fusion.1.a_ref, bf16[1024,1792]{1,0:T(8,128)(2,1)} %get-tuple-element.93.r_ref, bf16[8,2,4608,256]{3,2,1,0:T(8,128)(2,1)} %bitcast.560), custom_call_target="tpu_custom_call" | custom-call | flops 7516192768 | bytes 15204352 | tf_op jit(solution)/shard_map/value_backward/pallas_call | solution.py:746
  535.5 12.3 %key_backward.1 = bf16[1024,2048]{1,0:T(8,128)(2,1)} custom-call(s32[1]{0:T(128)} %bitcast.2.c_ref, bf16[1024,1792]{1,0:T(8,128)(2,1)} %value_backward.1.a_ref, bf16[16,4608,256]{2,1,0:T(8,128)(2,1)} %bitcast.561), custom_call_target="tpu_custom_call" | custom-call | flops 7516192768 | bytes 15204352 | tf_op jit(solution)/shard_map/key_backward/pallas_call | solution.py:746
  572.6 17.5 %collective-permute-done.21 = bf16[256,2048]{1,0:T(8,128)(2,1)S(1)} collective-permute-done((bf16[256,2048]{1,0:T(8,128)(2,1)}, bf16[256,2048]{1,0:T(8,128)(2,1)S(1)}, u32[]{:S(2)}, u32[]{:S(2)}) %collective-permute-start.21) | collective-permute-done | bytes 1048608 | tf_op jit(solution)/shard_map/ppermute | solution.py:35
  612.1 13.4 %gate_backward.1 = (bf16[256,2048]{1,0:T(8,128)(2,1)S(1)}, bf16[256,2048]{1,0:T(8,128)(2,1)S(1)}, bf16[2,16,64,128]{3,2,1,0:T(8,128)(2,1)S(1)}, f32[2,8,2048]{2,1,0:T(8,128)S(1)}) custom-call(f32[256,2048]{1,0:T(8,128)S(1)} %half_nt.2.grad_ref, f32[256,2048]{1,0:T(8,128)S(1)} %copy-done.51, f32[256,2048]{1,0:T(8,128)S(1)} %copy-done.13, ...), custom_call_target="tpu_custom_call" | custom-call | flops 1610612736 | bytes 13369344 | tf_op jit(solution)/shard_map/gate_backward/pallas_call | solution.py:493
  625.5 42.4 %all_to_all.20.refs_1_ = bf16[32,80,128]{2,1,0:T(8,128)(2,1)} all-to-all(bf16[32,80,128]{2,1,0:T(8,128)(2,1)S(1)} %pad_maximum_fusion.11), channel_id=1, replica_groups=mesh['y'=2,'z'=4,'x'=2,'core'=2] {'y','z','x','core'}, dimensions={0} | all-to-all | bytes 1310720 | tf_op jit(solution)/shard_map/all_to_all | solution.py:537
  680.6 18.0 %collective-permute-done.25.refs_2_ = bf16[1,256,2048]{2,1,0:T(8,128)(2,1)} collective-permute-done((bf16[1,256,2048]{2,1,0:T(8,128)(2,1)S(1)}, bf16[1,256,2048]{2,1,0:T(8,128)(2,1)}, u32[]{:S(2)}, u32[]{:S(2)}) %collective-permute-start.25) | collective-permute-done | bytes 1048608 | tf_op jit(solution)/shard_map/ppermute | solution.py:35
  706.3 25.3 %wkv_backward.1 = (bf16[256,2048]{1,0:T(8,128)(2,1)S(1)}, bf16[256,2048]{1,0:T(8,128)(2,1)S(1)}, bf16[256,2048]{1,0:T(8,128)(2,1)S(1)}, bf16[256,2048]{1,0:T(8,128)(2,1)S(1)}, f32[2,8,2048]{2,1,0:T(8,128)S(1)}) custom-call(f32[256,2048]{1,0:T(8,128)S(1)} %copy-done.11, f32[256,2048]{1,0:T(8,128)S(1)} %copy-done.5, f32[256,2048]{1,0:T(8,128)S(1)} %copy-done.8, ...), custom_call_target="tpu_custom_call" | custom-call | flops 4294967296 | bytes 17039360 | tf_op jit(solution)/shard_map/wkv_backward/pallas_call | solution.py:493
  747.4 12.1 %weight_grad.3 = bf16[1024,1536]{1,0:T(8,128)(2,1)S(1)} custom-call(s32[1]{0:T(128)} %bitcast.80.x_ref, bf16[1,256,2048]{2,1,0:T(8,128)(2,1)S(1)} %bitcast.524, bf16[1,256,2048]{2,1,0:T(8,128)(2,1)} %collective-permute-done.24.refs_1_, bf16[1,256,2048]{2,1,0:T(8,128)(2,1)} %collective-permute-done.25.refs_2_, ...), custom_call_target="tpu_custom_call" | custom-call | flops 3221225472 | bytes 12582912 | tf_op jit(solution)/shard_map/weight_grad/pallas_call | solution.py:215
  759.5 16.1 %collective-permute-done.27 = bf16[3,256,1024]{2,1,0:T(8,128)(2,1)} collective-permute-done((bf16[3,256,1024]{2,1,0:T(8,128)(2,1)}, bf16[3,256,1024]{2,1,0:T(8,128)(2,1)}, u32[]{:S(2)}, u32[]{:S(2)}) %collective-permute-start.27) | collective-permute-done | bytes 1572896 | tf_op jit(solution)/shard_map/ppermute | solution.py:35
  783.0 12.6 %weight_grad.5 = bf16[1024,1536]{1,0:T(8,128)(2,1)} custom-call(s32[1]{0:T(128)} %bitcast.80.x_ref, bf16[1,256,2048]{2,1,0:T(8,128)(2,1)S(1)} %bitcast.525, bf16[1,256,2048]{2,1,0:T(8,128)(2,1)} %collective-permute-done.24.refs_1_, bf16[1,256,2048]{2,1,0:T(8,128)(2,1)} %collective-permute-done.25.refs_2_, ...), custom_call_target="tpu_custom_call" | custom-call | flops 3221225472 | bytes 12582912 | tf_op jit(solution)/shard_map/weight_grad/pallas_call | solution.py:215
  799.1 14.9 %weight_grad.4 = bf16[2048,1536]{1,0:T(8,128)(2,1)} custom-call(s32[1]{0:T(128)} %bitcast.80.x_ref, bf16[4,256,2048]{2,1,0:T(8,128)(2,1)} %pad_maximum_fusion.refs_8_.refs_0_, bf16[4,256,2048]{2,1,0:T(8,128)(2,1)} %collective-permute-done.1.refs_9_.refs_1_, bf16[4,256,2048]{2,1,0:T(8,128)(2,1)} %collective-permute-done.2.refs_10_.refs_2_, ...), custom_call_target="tpu_custom_call" | custom-call | flops 6442450944 | bytes 22020096 | tf_op jit(solution)/shard_map/weight_grad/pallas_call | solution.py:215
  1041.4 14.5 %collective-permute-done.48 = bf16[128,3,512]{0,2,1:T(8,128)(2,1)S(1)} collective-permute-done((bf16[128,3,512]{0,2,1:T(8,128)(2,1)S(1)}, bf16[128,3,512]{0,2,1:T(8,128)(2,1)S(1)}, u32[]{:S(2)}, u32[]{:S(2)}) %collective-permute-start.48) | collective-permute-done | bytes 393248 | tf_op jit(solution)/shard_map/ppermute | solution.py:35
  (599 shorter events, 504.2 us)
Async XLA Ops:
  7.2 194.2 %all-gather.7.cloned.1.call-start = ((), (), s32[]{:S(2)}) async-start(), calls=%async_computation.10 | async-start | bytes 35651584 | tf_op jit(solution)/shard_map/all_gather | solution.py:960
  12.7 402.9 %all-gather.9.cloned.1.call-start = ((), (), s32[]{:S(2)}) async-start(), calls=%async_computation.11 | async-start | bytes 40108032 | tf_op jit(solution)/shard_map/all_gather | solution.py:967
  100.0 93.0 %collective-permute-start.2 = (bf16[4,256,2048]{2,1,0:T(8,128)(2,1)}, bf16[4,256,2048]{2,1,0:T(8,128)(2,1)}, u32[]{:S(2)}, u32[]{:S(2)}) collective-permute-start(bf16[4,256,2048]{2,1,0:T(8,128)(2,1)} %pad_maximum_fusion.refs_8_.refs_0_), channel_id=1, source_target_pairs={{0,16},{16,0},{1,17},{17,1},{2,18},{18,2},{3,19},{19,3},{4,20},{20... | collective-permute-start | bytes 12582920 | tf_op jit(solution)/shard_map/ppermute | solution.py:35
  101.1 93.5 %collective-permute-start.1 = (bf16[4,256,2048]{2,1,0:T(8,128)(2,1)}, bf16[4,256,2048]{2,1,0:T(8,128)(2,1)}, u32[]{:S(2)}, u32[]{:S(2)}) collective-permute-start(bf16[4,256,2048]{2,1,0:T(8,128)(2,1)} %pad_maximum_fusion.refs_8_.refs_0_), channel_id=1, source_target_pairs={{0,1},{1,0},{2,3},{3,2},{4,5},{5,4},{6,7},{7,6},{8,9},{9,8},{10,11... | collective-permute-start | bytes 12582920 | tf_op jit(solution)/shard_map/ppermute | solution.py:35
  206.2 57.8 %collective-permute-start.4 = (bf16[16,128,512]{2,1,0:T(8,128)(2,1)}, bf16[16,128,512]{2,1,0:T(8,128)(2,1)}, u32[]{:S(2)}, u32[]{:S(2)}) collective-permute-start(bf16[16,128,512]{2,1,0:T(8,128)(2,1)} %get-tuple-element.207), channel_id=1, source_target_pairs={{0,16},{16,0},{1,17},{17,1},{2,18},{18,2},{3,19},{19,3},{4,20},{20... | collective-permute-start | bytes 6291464 | tf_op jit(solution)/shard_map/ppermute | solution.py:35
  237.5 74.0 %collective-permute-start.5 = (bf16[16,128,512]{2,1,0:T(8,128)(2,1)}, bf16[16,128,512]{2,1,0:T(8,128)(2,1)}, u32[]{:S(2)}, u32[]{:S(2)}) collective-permute-start(bf16[16,128,512]{2,1,0:T(8,128)(2,1)} %get-tuple-element.206), channel_id=1, source_target_pairs={{0,16},{16,0},{1,17},{17,1},{2,18},{18,2},{3,19},{19,3},{4,20},{20... | collective-permute-start | bytes 6291464 | tf_op jit(solution)/shard_map/ppermute | solution.py:35
  266.5 45.3 %all-to-all-start.1 = ((bf16[32,64,128]{2,1,0:T(8,128)(2,1)}), bf16[32,64,128]{2,1,0:T(8,128)(2,1)}, u32[]{:S(2)}, u32[]{:S(2)}) async-start(bf16[32,64,128]{2,1,0:T(8,128)(2,1)} %copy-done.49), calls=%async_computation.1 | async-start | bytes 1048576 | tf_op jit(solution)/shard_map/all_to_all | solution.py:553
  269.9 432.0 %reduce-scatter.4.cloned.1.call-start = ((), (), s32[]{:S(2)}) async-start(), calls=%async_computation.7 | async-start | bytes 8257536 | tf_op jit(solution)/shard_map/reduce_scatter | solution.py:1028
  270.3 48.8 %collective-permute-start.6 = (bf16[16,128,512]{2,1,0:T(8,128)(2,1)}, bf16[16,128,512]{2,1,0:T(8,128)(2,1)}, u32[]{:S(2)}, u32[]{:S(2)}) collective-permute-start(bf16[16,128,512]{2,1,0:T(8,128)(2,1)} %collective-permute-done.4.g_ref), channel_id=1, source_target_pairs={{0,1},{1,0},{2,3},{3,2},{4,5},{5,4},{6,7},{7,6},{8,9},{9,8},{10,11... | collective-permute-start | bytes 6291464 | tf_op jit(solution)/shard_map/ppermute | solution.py:35
  311.8 36.0 %collective-permute-start.7 = (bf16[16,128,512]{2,1,0:T(8,128)(2,1)}, bf16[16,128,512]{2,1,0:T(8,128)(2,1)}, u32[]{:S(2)}, u32[]{:S(2)}) collective-permute-start(bf16[16,128,512]{2,1,0:T(8,128)(2,1)} %collective-permute-done.5.g_ref), channel_id=1, source_target_pairs={{0,1},{1,0},{2,3},{3,2},{4,5},{5,4},{6,7},{7,6},{8,9},{9,8},{10,11... | collective-permute-start | bytes 6291464 | tf_op jit(solution)/shard_map/ppermute | solution.py:35
  369.1 42.2 %collective-permute-start.13 = (bf16[1,256,2048]{2,1,0:T(8,128)(2,1)S(1)}, bf16[1,256,2048]{2,1,0:T(8,128)(2,1)S(1)}, u32[]{:S(2)}, u32[]{:S(2)}) collective-permute-start(bf16[1,256,2048]{2,1,0:T(8,128)(2,1)S(1)} %bitcast.528), channel_id=1, source_target_pairs={{0,16},{16,0},{1,17},{17,1},{2,18},{18,2},{3,19},{19,3},{4,20},{20... | collective-permute-start | bytes 3145736 | tf_op jit(solution)/shard_map/ppermute | solution.py:35
  369.1 42.2 %collective-permute-start.9 = (bf16[1,256,2048]{2,1,0:T(8,128)(2,1)S(1)}, bf16[1,256,2048]{2,1,0:T(8,128)(2,1)S(1)}, u32[]{:S(2)}, u32[]{:S(2)}) collective-permute-start(bf16[1,256,2048]{2,1,0:T(8,128)(2,1)S(1)} %get-tuple-element.200), channel_id=1, source_target_pairs={{0,1},{1,0},{2,3},{3,2},{4,5},{5,4},{6,7},{7,6},{8,9},{9,8},{10,11... | collective-permute-start | bytes 3145736 | tf_op jit(solution)/shard_map/ppermute | solution.py:35
  521.1 293.3 %reduce-scatter.6.cloned.1.call-start = ((), (), s32[]{:S(2)}) async-start(), calls=%async_computation.8 | async-start | bytes 8257536 | tf_op jit(solution)/shard_map/reduce_scatter | solution.py:1033
  675.3 287.3 %reduce-scatter.8.cloned.1.call-start = ((), (), s32[]{:S(2)}) async-start(), calls=%async_computation.9 | async-start | bytes 7077888 | tf_op jit(solution)/shard_map/reduce_scatter | solution.py:1074
  679.0 56.6 %collective-permute-start.23 = (bf16[3,256,1024]{2,1,0:T(8,128)(2,1)}, bf16[3,256,1024]{2,1,0:T(8,128)(2,1)}, u32[]{:S(2)}, u32[]{:S(2)}) collective-permute-start(bf16[3,256,1024]{2,1,0:T(8,128)(2,1)} %get-tuple-element.229), channel_id=1, source_target_pairs={{0,16},{16,0},{1,17},{17,1},{2,18},{18,2},{3,19},{19,3},{4,20},{20... | collective-permute-start | bytes 4718600 | tf_op jit(solution)/shard_map/ppermute | solution.py:35
  680.6 55.0 %collective-permute-start.24 = (bf16[1,256,2048]{2,1,0:T(8,128)(2,1)S(1)}, bf16[1,256,2048]{2,1,0:T(8,128)(2,1)}, u32[]{:S(2)}, u32[]{:S(2)}) collective-permute-start(bf16[1,256,2048]{2,1,0:T(8,128)(2,1)S(1)} %bitcast.523), channel_id=1, source_target_pairs={{0,1},{1,0},{2,3},{3,2},{4,5},{5,4},{6,7},{7,6},{8,9},{9,8},{10,11... | collective-permute-start | bytes 3145736 | tf_op jit(solution)/shard_map/ppermute | solution.py:35
  698.7 37.0 %collective-permute-start.26 = (bf16[1,256,2048]{2,1,0:T(8,128)(2,1)}, bf16[1,256,2048]{2,1,0:T(8,128)(2,1)}, u32[]{:S(2)}, u32[]{:S(2)}) collective-permute-start(bf16[1,256,2048]{2,1,0:T(8,128)(2,1)} %collective-permute-done.25.refs_2_), channel_id=1, source_target_pairs={{0,1},{1,0},{2,3},{3,2},{4,5},{5,4},{6,7},{7,6},{8,9},{9,8},{10,11... | collective-permute-start | bytes 3145736 | tf_op jit(solution)/shard_map/ppermute | solution.py:35
  738.5 37.1 %collective-permute-start.27 = (bf16[3,256,1024]{2,1,0:T(8,128)(2,1)}, bf16[3,256,1024]{2,1,0:T(8,128)(2,1)}, u32[]{:S(2)}, u32[]{:S(2)}) collective-permute-start(bf16[3,256,1024]{2,1,0:T(8,128)(2,1)} %get-tuple-element.230), channel_id=1, source_target_pairs={{0,16},{16,0},{1,17},{17,1},{2,18},{18,2},{3,19},{19,3},{4,20},{20... | collective-permute-start | bytes 4718600 | tf_op jit(solution)/shard_map/ppermute | solution.py:35
  795.6 113.9 %collective-permute-start.35 = (bf16[1024,1536]{1,0:T(8,128)(2,1)}, bf16[1024,1536]{1,0:T(8,128)(2,1)}, u32[]{:S(2)}, u32[]{:S(2)}) collective-permute-start(bf16[1024,1536]{1,0:T(8,128)(2,1)} %weight_grad.5), channel_id=1, source_target_pairs={{0,2},{2,0},{1,3},{3,1},{4,6},{6,4},{5,7},{7,5},{8,10},{10,8},{9,1... | collective-permute-start | bytes 9437192 | tf_op jit(solution)/shard_map/ppermute | solution.py:35
  856.6 35.6 %collective-permute-start.31 = (bf16[128,1,1792]{2,0,1:T(8,128)(2,1)}, bf16[128,1,1792]{2,0,1:T(8,128)(2,1)}, u32[]{:S(2)}, u32[]{:S(2)}) collective-permute-start(bf16[128,1,1792]{2,0,1:T(8,128)(2,1)} %get-tuple-element.263), channel_id=1, source_target_pairs={{0,1},{1,0},{2,3},{3,2},{4,5},{5,4},{6,7},{7,6},{8,9},{9,8},{10,11... | collective-permute-start | bytes 1376264 | tf_op jit(solution)/shard_map/ppermute | solution.py:35
  856.6 35.6 %collective-permute-start.33 = (bf16[128,1,1792]{2,0,1:T(8,128)(2,1)}, bf16[128,1,1792]{2,0,1:T(8,128)(2,1)}, u32[]{:S(2)}, u32[]{:S(2)}) collective-permute-start(bf16[128,1,1792]{2,0,1:T(8,128)(2,1)} %get-tuple-element.263), channel_id=1, source_target_pairs={{0,17},{1,16},{16,1},{17,0},{2,19},{3,18},{18,3},{19,2},{4,21},{5,... | collective-permute-start | bytes 1376264 | tf_op jit(solution)/shard_map/ppermute | solution.py:162
  872.6 33.0 %collective-permute-start.34 = (bf16[224,2048]{1,0:T(8,128)(2,1)}, bf16[224,2048]{1,0:T(8,128)(2,1)}, u32[]{:S(2)}, u32[]{:S(2)}) collective-permute-start(bf16[224,2048]{1,0:T(8,128)(2,1)} %bitcast.83), channel_id=1, source_target_pairs={{0,16},{16,0},{1,17},{17,1},{2,18},{18,2},{3,19},{19,3},{4,20},{20... | collective-permute-start | bytes 2752520 | tf_op jit(solution)/shard_map/ppermute | solution.py:35
  912.2 41.4 %collective-permute-start.36 = (bf16[8,464,128]{2,1,0:T(8,128)(2,1)}, bf16[8,464,128]{2,1,0:T(8,128)(2,1)}, u32[]{:S(2)}, u32[]{:S(2)}) collective-permute-start(bf16[8,464,128]{2,1,0:T(8,128)(2,1)} %fusion.53), channel_id=1, source_target_pairs={{0,1},{1,0},{2,3},{3,2},{4,5},{5,4},{6,7},{7,6},{8,9},{9,8},{10,11... | collective-permute-start | bytes 2850824 | tf_op jit(solution)/shard_map/ppermute | solution.py:35
  1002.4 32.0 %collective-permute-start.46 = (bf16[256,1536]{0,1:T(8,128)(2,1)S(1)}, bf16[256,1536]{0,1:T(8,128)(2,1)S(1)}, u32[]{:S(2)}, u32[]{:S(2)}) collective-permute-start(bf16[256,1536]{0,1:T(8,128)(2,1)S(1)} %fusion.44), channel_id=1, source_target_pairs={{4,0},{8,4},{12,8},{5,1},{9,5},{13,9},{6,2},{10,6},{14,10},{7,3},{... | collective-permute-start | bytes 2359304 | tf_op jit(solution)/shard_map/ppermute | solution.py:67
  (185 other events, 2019.0 us)
Sparse Core Ops, SparseCore 0:
  12.9 188.5 all-gather.6
  203.6 207.0 all-gather.8
  521.2 147.2 reduce-scatter.3
  672.0 142.3 reduce-scatter.5
  827.4 130.1 reduce-scatter.7

commit v5 on v4

--- a/solution.py
+++ b/solution.py
@@ -86,7 +86,8 @@
     width = parts[0].shape[1]
     counts = [p.shape[0] for p in parts]
     rows = sum(counts)
-    block = LANES
+    step = 4
+    block = step * LANES
 
     def kernel(*refs):
         out = refs[-1]
@@ -98,14 +99,17 @@
                 n += counts[start]
                 start += 1
             first = sum(counts[: start - len(take)])
-            out[0, first : first + n] = take[0] if len(take) == 1 else jnp.concatenate(take, 0)
+            rows_here = take[0] if len(take) == 1 else jnp.concatenate(take, 0)
+            for b in range(step):
+                out[b, first : first + n] = rows_here[:, b * LANES : (b + 1) * LANES]
 
     return pl.pallas_call(
         kernel,
         grid=(width // block,),
         in_specs=[pl.BlockSpec((c, block), lambda j: (0, j)) for c in counts],
-        out_specs=pl.BlockSpec((1, rows, block), lambda j: (j, 0, 0)),
-        out_shape=jax.ShapeDtypeStruct((width // block, rows, block), F32),
+        out_specs=pl.BlockSpec((step, rows, LANES), lambda j: (j, 0, 0)),
+        out_shape=jax.ShapeDtypeStruct((width // LANES, rows, LANES), F32),
+        compiler_params=pltpu.CompilerParams(vmem_limit_bytes=40 << 20),
         name="pack_columns",
     )(*parts)
 
@@ -129,7 +133,16 @@
 
 
 def small_sum(value):
-    value = line_sum(value)
+    count, place = lax.axis_size("z"), lax.axis_index("z")
+    reach = count // 2
+    while reach:
+        value = value.reshape(2, reach, *value.shape[1:])
+        bit = lax.rem(place // reach, 2)
+        give = low(lax.dynamic_index_in_dim(value, 1 - bit, 0, False))
+        got = lax.ppermute(give, "z", [(i, i ^ reach) for i in range(count)])
+        value = lax.dynamic_index_in_dim(value, bit, 0, False) + got.astype(F32)
+        reach //= 2
+    value = value[0]
     return value + swap(value, "y")
 
 
@@ -1051,7 +1064,8 @@
         g_state, final, True, ([grad_gate_in, grad_att, g_gate_low], rec_mix)
     )
     side_near, side_across = half_cols(jnp.stack(rights, 0))
-    rec_all = group_pieces([rec_low])
+    rec_low = rec_low[None]
+    rec_near, rec_across = swap(rec_low, "core"), swap(rec_low, "y")
     g_state_out, value_part = tie(g_state_out, value_part)
     g_rec, g_key, g_val, g_decay_low, wkv_sums = wkv_call(
         wkv_back_kernel, seqs,
@@ -1062,7 +1076,8 @@
     gate_sums, wkv_sums = jnp.sum(gate_sums, 0), jnp.sum(wkv_sums, 0)
     projs = [g_rec, g_key, g_val, g_gate_low]
     main_near, main_across = half_cols(jnp.stack([g_rec, g_key, g_val], 0))
-    main_near, side_across, rec_all = tie(main_near, side_across, rec_all)
+    main_near, side_across, rec_across = tie(main_near, side_across, rec_across)
+    rec_all = (rec_low, rec_near, rec_across, swap(rec_across, "core"))
     side_lefts = [(rec_all, 0, 1), (gated_all, 0, 1), (mix_all, 0, 1)]
     side_give, side_keep = x_rows(side_lefts, quarter_cols(side_near, side_across))
     side_got = swap(side_give, "x")
@@ -1098,14 +1113,17 @@
         g_normed = here if g_normed is None else g_normed + here
         g_prior_sum = back if g_prior_sum is None else g_prior_sum + back
     g_pre_mix = low(jnp.concatenate(hid_grads, 1) * (1.0 - tanh_mix * tanh_mix))
-    g_pre_mix, value_part, key_part = tie(g_pre_mix, value_part, key_part)
     mix_down_grad = tn(g_pre_mix, mix_low)
     g_first_mix = nn(g_pre_mix, down_t[:MIXCOLS])
     maa_first = jnp.sum(g_first_mix * delta, 0, keepdims=True)
     g_prior_sum = g_prior_sum + g_first_mix * vec[2]
     g_normed = g_normed + g_first_mix * (1.0 - vec[2]) + prior_back(g_prior_sum, seqs)
-    back_one, g_gain, g_bias = norm_backward(g_normed, hat, rstd, vec[0])
-    input_grad = (grad_first + back_one).reshape(tokens.shape)
+    g_normed, side_got = tie(g_normed, side_got)
+    side = low(side_keep.astype(F32) + side_got.astype(F32))
+    side = side.reshape(zs, -1, side.shape[1])
+    moving = line_step(side, 1, None)
+    g_gain = jnp.sum(g_normed * hat, 0, keepdims=True)
+    g_bias = jnp.sum(g_normed, 0, keepdims=True)
 
     vec_rows = (
         [g_gain, g_bias, maa_first] + maa_rows
@@ -1113,6 +1131,11 @@
            g_maa_key, g_maa_rec]
     )
     packed = pack_columns(up_grads + [decay_up_grad, mix_down_grad, decay_down_grad] + vec_rows)
+    packed, moving = tie(packed, moving)
+    for t in range(2, zs - 1):
+        moving = line_step(side, t, moving)
+    packed, moving, value_part, key_part = tie(small_core(packed), moving, value_part, key_part)
+    moving = line_step(side, zs - 1, moving)
     first = y == 0
     other = swap(value_part, "y")
     value_share = jnp.concatenate(
@@ -1120,15 +1143,11 @@
     ).astype(F32)
     key_share = spread_cols(key_part[:, None])[0].reshape(-1, 2, 2, zs, 2, half)
     key_share = key_share.transpose(0, 3, 4, 2, 1, 5).reshape(-1, ff)
-    packed, key_share, value_share, side_got = tie(packed, key_share, value_share, side_got)
-    side = low(side_keep.astype(F32) + side_got.astype(F32))
-    side = side.reshape(zs, -1, side.shape[1])
-    moving = line_step(side, 1, None)
-    packed, moving, main = tie(small_core(packed), moving, main)
-    for t in range(2, zs - 1):
-        moving = line_step(side, t, moving)
-    packed, moving = tie(small_cross(packed), moving)
-    side = low(line_end(side, line_step(side, zs - 1, moving)))
+    packed, main, g_normed = tie(packed, main, g_normed)
+    back_one, _, _ = norm_backward(g_normed, hat, rstd, vec[0])
+    input_grad = (grad_first + back_one).reshape(tokens.shape)
+    packed, moving, key_share, value_share = tie(small_cross(packed), moving, key_share, value_share)
+    side = low(line_end(side, moving))
     late = spread_cols(main.reshape(main.shape[0], 3, -1))
     early = spread_cols(side.reshape(side.shape[0], 3, -1))
     packed = small_sum(packed)

time: 1080 us -> 1100 us (1.019)
  waiting for transfers between devices: 361 us -> 411 us
  blocking collectives: 100 us -> 57.6 us
  other arithmetic: 83.9 us -> 100 us
  local copies, waits for them, and re-layouts: 113 us -> 102 us
    all_to_all x1 -> x0, blocking collectives: 42.4 us -> none  [chain(): packed = lax.all_to_all(packed, ALL, 0, 0, tiled=True)]
    all_to_all x1 -> x2, waiting for transfers between devices: 24.7 us -> 57.8 us  [chain(): packed = lax.all_to_all(packed, ALL, 0, 0, tiled=True)]
    all_to_all x2, waiting for transfers between devices: 3.48 us -> 20 us  [chain(): lax.all_to_all(entering, ALL, 0, 0, tiled=True).reshape(state.shape)]
    ppermute x38, starting transfers between devices: 42.5 us -> 29 us  [swap(): return lax.ppermute(value, axis, [(0, 1), (1, 0)])]
    add x1 -> x2, other arithmetic: 0.04 us -> 12.3 us  [the longest x1 12.2 us: body(): g_normed + g_first_mix * (1.0 - vec[2]) + prior_back(g_prior_sum, seqs)]
    ppermute x6 -> x3, starting transfers between devices: 29.7 us -> 40.8 us  [line_step(): lax.ppermute(low(right), 'z', [(i, i + 1) for i in range(count - 1) if i...]
    convert_element_type x17 -> x14, other arithmetic: 22.5 us -> 31.8 us  [low(): return a.astype(BF16)]
    unnamed x301 -> x321, local copies, waits for them, and re-layouts: 56.1 us -> 50.1 us
  transfers between devices with their start and end apart: 65 -> 62, of which waited for: 29 -> 27; matrix products, arithmetic and copies ran while one was open for 16% -> 18% of each run, Pallas kernels for 21% -> 20%
where the time goes in v5:
time: 1100 us; the launch traced here: 1090 us
  waiting for transfers between devices  411 us (37%)
  Pallas kernels  242 us (22%)
  starting transfers between devices  110 us (10%)
  local copies, waits for them, and re-layouts  102 us (9%)
  other arithmetic  100 us (9%)
  blocking collectives  57.6 us (5%)
  matrix products  55.1 us (5%)
  between operations  16.2 us (1%)
    ppermute x38, waiting for transfers between devices, swap(): return lax.ppermute(value, axis, [(0, 1), (1, 0)])  298 us
    pallas_call x6, Pallas kernels, ffn_call(): pl.pallas_call(kernel, grid_spec=pltpu.PrefetchScalarGridSpec(num_scalar_...  69.1 us
    pallas_call x4, Pallas kernels, wkv_call(): pl.pallas_call(kernel, grid=(seqs, width // SPAN), in_specs=[spec(a) for...  64.1 us
    all_to_all x2, waiting for transfers between devices, chain(): packed = lax.all_to_all(packed, ALL, 0, 0, tiled=True)  57.8 us
    all_gather x2, blocking collectives, columns(): gathered = lax.all_gather(shard, WIDE, axis=0)  57.6 us
    unnamed x321, local copies, waits for them, and re-layouts  50.1 us
    ppermute x3, starting transfers between devices, line_step(): lax.ppermute(low(right), 'z', [(i, i + 1) for i in range(count - 1) if i...  40.8 us
    pallas_call x3, Pallas kernels, grad_call(): pl.pallas_call(kernel, grid_spec=pltpu.PrefetchScalarGridSpec(num_scalar_...  39.5 us
  transfers between devices with their start and end apart: 62, of which 27 were waited for; matrix products, arithmetic and copies ran while one was open for 18% of the time, Pallas kernels for 20%

profile of v5, /device:TPU:0, one launch (start us, length us, event | category | flops | bytes accessed | tf_op | source)
XLA Modules:
  0.0 1094.2 jit_solution(6742833443459432076)
XLA Ops:
  24.3 31.5 %all-gather = bf16[3840,128]{1,0:T(8,128)(2,1)S(1)} all-gather(bf16[240,128]{1,0:T(8,128)(2,1)S(1)} %pad_maximum_fusion.13), channel_id=2, replica_groups=mesh['y'=2,'z'=4,'x'=2,'core'=2] {'z','x','core'}, dimensions={0}, use_global_device_ids=true | all-gather | bytes 1044480 | tf_op jit(solution)/shard_map/all_gather | solution.py:964
  60.2 26.2 %all-gather.1 = bf16[3584,128]{1,0:T(8,128)(2,1)S(1)} all-gather(bf16[224,128]{1,0:T(8,128)(2,1)S(1)} %bitcast.623), channel_id=3, replica_groups=mesh['y'=2,'z'=4,'x'=2,'core'=2] {'z','x','core'}, dimensions={0}, use_global_device_ids=true | all-gather | bytes 974848 | tf_op jit(solution)/shard_map/all_gather | solution.py:964
  101.1 91.8 %collective-permute-done.2.refs_10_.refs_2_ = bf16[4,256,2048]{2,1,0:T(8,128)(2,1)} collective-permute-done((bf16[4,256,2048]{2,1,0:T(8,128)(2,1)}, bf16[4,256,2048]{2,1,0:T(8,128)(2,1)}, u32[]{:S(2)}, u32[]{:S(2)}) %collective-permute-start.2) | collective-permute-done | bytes 4194336 | tf_op jit(solution)/shard_map/ppermute | solution.py:35
  239.2 24.7 %all-to-all-done.refs_1_ = bf16[32,80,128]{2,1,0:T(8,128)(2,1)} async-done(((bf16[32,80,128]{2,1,0:T(8,128)(2,1)}), bf16[32,80,128]{2,1,0:T(8,128)(2,1)}, u32[]{:S(2)}, u32[]{:S(2)}) %all-to-all-start) | async-done | bytes 655392 | tf_op jit(solution)/shard_map/all_to_all | solution.py:550
  271.4 40.0 %collective-permute-done.5.g_ref = bf16[16,128,512]{2,1,0:T(8,128)(2,1)} collective-permute-done((bf16[16,128,512]{2,1,0:T(8,128)(2,1)}, bf16[16,128,512]{2,1,0:T(8,128)(2,1)}, u32[]{:S(2)}, u32[]{:S(2)}) %collective-permute-start.5) | collective-permute-done | bytes 2097184 | tf_op jit(solution)/shard_map/ppermute | solution.py:35
  329.2 17.2 %wkv_forward.1 = (f32[256,2048]{1,0:T(8,128)S(1)}, bf16[256,2048]{1,0:T(8,128)(2,1)S(1)}) custom-call(f32[256,2048]{1,0:T(8,128)S(1)} %stack_nn.3.rec_ref, f32[256,2048]{1,0:T(8,128)S(1)} %stack_nn.4.key_ref, f32[256,2048]{1,0:T(8,128)S(1)} %copy-done.10, f32[256,2048]{1,0:T(8,128)S(1)} %copy-done.32, bf16[2,16,64,128]{3,2,1,0:T(8,128)(2,1)} %bitcast.33.state_ref, ...), custom_call_target="tpu_custom_call" | custom-call | flops 1610612736 | bytes 14286848 | tf_op jit(solution)/shard_map/wkv_forward/pallas_call | solution.py:506
  368.8 24.0 %collective-permute-done.10 = bf16[1,256,2048]{2,1,0:T(8,128)(2,1)S(1)} collective-permute-done((bf16[1,256,2048]{2,1,0:T(8,128)(2,1)S(1)}, bf16[1,256,2048]{2,1,0:T(8,128)(2,1)S(1)}, u32[]{:S(2)}, u32[]{:S(2)}) %collective-permute-start.10) | collective-permute-done | bytes 1048608 | tf_op jit(solution)/shard_map/ppermute | solution.py:35
  393.4 17.6 %collective-permute-done.13.refs_6_ = bf16[1,256,2048]{2,1,0:T(8,128)(2,1)S(1)} collective-permute-done((bf16[1,256,2048]{2,1,0:T(8,128)(2,1)S(1)}, bf16[1,256,2048]{2,1,0:T(8,128)(2,1)S(1)}, u32[]{:S(2)}, u32[]{:S(2)}) %collective-permute-start.13) | collective-permute-done | bytes 1048608 | tf_op jit(solution)/shard_map/ppermute | solution.py:35
  415.3 13.4 %key_forward.1 = (bf16[1024,1792]{1,0:T(8,128)(2,1)}, bf16[1024,1792]{1,0:T(8,128)(2,1)}) custom-call(s32[1]{0:T(128)} %bitcast.2.c_ref, bf16[1024,2048]{1,0:T(8,128)(2,1)} %maximum_bitcast_fusion.a_ref, bf16[16,4608,256]{2,1,0:T(8,128)(2,1)} %bitcast.549), custom_call_target="tpu_custom_call" | custom-call | flops 7516192768 | bytes 18874368 | tf_op jit(solution)/shard_map/key_forward/pallas_call | solution.py:759
  428.7 13.1 %value_forward.1 = bf16[1024,2048]{1,0:T(8,128)(2,1)} custom-call(s32[1]{0:T(128)} %bitcast.2.c_ref, bf16[1024,1792]{1,0:T(8,128)(2,1)} %get-tuple-element.92.a_ref, bf16[8,2,4608,256]{3,2,1,0:T(8,128)(2,1)} %bitcast.550), custom_call_target="tpu_custom_call" | custom-call | flops 7516192768 | bytes 15204352 | tf_op jit(solution)/shard_map/value_forward/pallas_call | solution.py:759
  462.4 14.0 %collective-permute-done.16 = bf16[256,2048]{1,0:T(8,128)(2,1)} collective-permute-done((bf16[256,2048]{1,0:T(8,128)(2,1)}, bf16[256,2048]{1,0:T(8,128)(2,1)}, u32[]{:S(2)}, u32[]{:S(2)}) %collective-permute-start.16) | collective-permute-done | bytes 1048608 | tf_op jit(solution)/shard_map/ppermute | solution.py:35
  482.3 23.6 %collective-permute-done.18 = bf16[1,256,2048]{2,1,0:T(8,128)(2,1)S(1)} collective-permute-done((bf16[1,256,2048]{2,1,0:T(8,128)(2,1)S(1)}, bf16[1,256,2048]{2,1,0:T(8,128)(2,1)S(1)}, u32[]{:S(2)}, u32[]{:S(2)}) %collective-permute-start.18) | collective-permute-done | bytes 1048608 | tf_op jit(solution)/shard_map/ppermute | solution.py:35
  521.0 14.2 %value_backward.1.a_ref = bf16[1024,1792]{1,0:T(8,128)(2,1)} custom-call(s32[1]{0:T(128)} %bitcast.2.c_ref, bf16[1024,2048]{1,0:T(8,128)(2,1)} %maximum_bitcast_fusion.1.a_ref, bf16[1024,1792]{1,0:T(8,128)(2,1)} %get-tuple-element.94.r_ref, bf16[8,2,4608,256]{3,2,1,0:T(8,128)(2,1)} %bitcast.552), custom_call_target="tpu_custom_call" | custom-call | flops 7516192768 | bytes 15204352 | tf_op jit(solution)/shard_map/value_backward/pallas_call | solution.py:759
  572.2 17.6 %collective-permute-done.21 = bf16[256,2048]{1,0:T(8,128)(2,1)S(1)} collective-permute-done((bf16[256,2048]{1,0:T(8,128)(2,1)}, bf16[256,2048]{1,0:T(8,128)(2,1)S(1)}, u32[]{:S(2)}, u32[]{:S(2)}) %collective-permute-start.21) | collective-permute-done | bytes 1048608 | tf_op jit(solution)/shard_map/ppermute | solution.py:35
  611.1 13.4 %gate_backward.1 = (bf16[256,2048]{1,0:T(8,128)(2,1)S(1)}, bf16[256,2048]{1,0:T(8,128)(2,1)S(1)}, bf16[2,16,64,128]{3,2,1,0:T(8,128)(2,1)S(1)}, f32[2,8,2048]{2,1,0:T(8,128)S(1)}) custom-call(f32[256,2048]{1,0:T(8,128)S(1)} %half_nt.2.grad_ref, f32[256,2048]{1,0:T(8,128)S(1)} %copy-done.52, f32[256,2048]{1,0:T(8,128)S(1)} %copy-done.16, ...), custom_call_target="tpu_custom_call" | custom-call | flops 1610612736 | bytes 13369344 | tf_op jit(solution)/shard_map/gate_backward/pallas_call | solution.py:506
  635.2 33.0 %all-to-all-done.2.refs_1_ = bf16[32,80,128]{2,1,0:T(8,128)(2,1)S(1)} async-done(((bf16[32,80,128]{2,1,0:T(8,128)(2,1)}), bf16[32,80,128]{2,1,0:T(8,128)(2,1)S(1)}, u32[]{:S(2)}, u32[]{:S(2)}) %all-to-all-start.2) | async-done | bytes 655392 | tf_op jit(solution)/shard_map/all_to_all | solution.py:550
  679.3 19.7 %all-to-all-done.3 = bf16[32,64,128]{2,1,0:T(8,128)(2,1)} async-done(((bf16[32,64,128]{2,1,0:T(8,128)(2,1)}), bf16[32,64,128]{2,1,0:T(8,128)(2,1)}, u32[]{:S(2)}, u32[]{:S(2)}) %all-to-all-start.3) | async-done | bytes 524320 | tf_op jit(solution)/shard_map/all_to_all | solution.py:566
  703.4 24.9 %wkv_backward.1 = (bf16[256,2048]{1,0:T(8,128)(2,1)S(1)}, bf16[256,2048]{1,0:T(8,128)(2,1)S(1)}, bf16[256,2048]{1,0:T(8,128)(2,1)S(1)}, bf16[256,2048]{1,0:T(8,128)(2,1)S(1)}, f32[2,8,2048]{2,1,0:T(8,128)S(1)}) custom-call(f32[256,2048]{1,0:T(8,128)S(1)} %copy-done.14, f32[256,2048]{1,0:T(8,128)S(1)} %copy-done.8, f32[256,2048]{1,0:T(8,128)S(1)} %copy-done.11, ...), custom_call_target="tpu_custom_call" | custom-call | flops 4294967296 | bytes 17039360 | tf_op jit(solution)/shard_map/wkv_backward/pallas_call | solution.py:506
  763.1 16.2 %collective-permute-done.25 = bf16[3,256,1024]{2,1,0:T(8,128)(2,1)} collective-permute-done((bf16[3,256,1024]{2,1,0:T(8,128)(2,1)}, bf16[3,256,1024]{2,1,0:T(8,128)(2,1)}, u32[]{:S(2)}, u32[]{:S(2)}) %collective-permute-start.25) | collective-permute-done | bytes 1572896 | tf_op jit(solution)/shard_map/ppermute | solution.py:35
  785.7 12.6 %weight_grad.5 = bf16[1024,1536]{1,0:T(8,128)(2,1)} custom-call(s32[1]{0:T(128)} %bitcast.80.x_ref, bf16[1,256,2048]{2,1,0:T(8,128)(2,1)S(1)} %bitcast.503, bf16[1,256,2048]{2,1,0:T(8,128)(2,1)} %collective-permute-done.26.refs_1_, bf16[1,256,2048]{2,1,0:T(8,128)(2,1)} %collective-permute-done.24.refs_2_, ...), custom_call_target="tpu_custom_call" | custom-call | flops 3221225472 | bytes 12582912 | tf_op jit(solution)/shard_map/weight_grad/pallas_call | solution.py:228
  801.4 14.9 %weight_grad.4 = bf16[2048,1536]{1,0:T(8,128)(2,1)} custom-call(s32[1]{0:T(128)} %bitcast.80.x_ref, bf16[4,256,2048]{2,1,0:T(8,128)(2,1)} %pad_maximum_fusion.refs_8_.refs_0_, bf16[4,256,2048]{2,1,0:T(8,128)(2,1)} %collective-permute-done.1.refs_9_.refs_1_, bf16[4,256,2048]{2,1,0:T(8,128)(2,1)} %collective-permute-done.2.refs_10_.refs_2_, ...), custom_call_target="tpu_custom_call" | custom-call | flops 6442450944 | bytes 22020096 | tf_op jit(solution)/shard_map/weight_grad/pallas_call | solution.py:228
  945.9 14.1 %collective-permute-done.35 = bf16[256,1536]{0,1:T(8,128)(2,1)} collective-permute-done((bf16[256,1536]{0,1:T(8,128)(2,1)}, bf16[256,1536]{0,1:T(8,128)(2,1)}, u32[]{:S(2)}, u32[]{:S(2)}) %collective-permute-start.35) | collective-permute-done | bytes 786464 | tf_op jit(solution)/shard_map/ppermute | solution.py:66
  963.8 30.1 %collective-permute-start.41 = (bf16[256,1536]{0,1:T(8,128)(2,1)}, bf16[256,1536]{0,1:T(8,128)(2,1)}, u32[]{:S(2)}, u32[]{:S(2)}) collective-permute-start(bf16[256,1536]{0,1:T(8,128)(2,1)} %fusion.45), channel_id=1, source_target_pairs={{0,4},{4,8},{8,12},{1,5},{5,9},{9,13},{2,6},{6,10},{10,14},{3,7},{... | collective-permute-start | bytes 2359304 | tf_op jit(solution)/shard_map/ppermute | solution.py:66
  1037.8 14.1 %collective-permute-done.38 = bf16[128,3,512]{0,2,1:T(8,128)(2,1)S(1)} collective-permute-done((bf16[128,3,512]{0,2,1:T(8,128)(2,1)S(1)}, bf16[128,3,512]{0,2,1:T(8,128)(2,1)S(1)}, u32[]{:S(2)}, u32[]{:S(2)}) %collective-permute-start.38) | collective-permute-done | bytes 393248 | tf_op jit(solution)/shard_map/ppermute | solution.py:35
  (613 shorter events, 516.0 us)
Async XLA Ops:
  7.2 194.2 %all-gather.7.cloned.1.call-start = ((), (), s32[]{:S(2)}) async-start(), calls=%async_computation.10 | async-start | bytes 35651584 | tf_op jit(solution)/shard_map/all_gather | solution.py:973
  12.7 402.6 %all-gather.9.cloned.1.call-start = ((), (), s32[]{:S(2)}) async-start(), calls=%async_computation.11 | async-start | bytes 40108032 | tf_op jit(solution)/shard_map/all_gather | solution.py:980
  100.0 93.0 %collective-permute-start.2 = (bf16[4,256,2048]{2,1,0:T(8,128)(2,1)}, bf16[4,256,2048]{2,1,0:T(8,128)(2,1)}, u32[]{:S(2)}, u32[]{:S(2)}) collective-permute-start(bf16[4,256,2048]{2,1,0:T(8,128)(2,1)} %pad_maximum_fusion.refs_8_.refs_0_), channel_id=1, source_target_pairs={{0,16},{16,0},{1,17},{17,1},{2,18},{18,2},{3,19},{19,3},{4,20},{20... | collective-permute-start | bytes 12582920 | tf_op jit(solution)/shard_map/ppermute | solution.py:35
  101.1 93.5 %collective-permute-start.1 = (bf16[4,256,2048]{2,1,0:T(8,128)(2,1)}, bf16[4,256,2048]{2,1,0:T(8,128)(2,1)}, u32[]{:S(2)}, u32[]{:S(2)}) collective-permute-start(bf16[4,256,2048]{2,1,0:T(8,128)(2,1)} %pad_maximum_fusion.refs_8_.refs_0_), channel_id=1, source_target_pairs={{0,1},{1,0},{2,3},{3,2},{4,5},{5,4},{6,7},{7,6},{8,9},{9,8},{10,11... | collective-permute-start | bytes 12582920 | tf_op jit(solution)/shard_map/ppermute | solution.py:35
  206.2 57.8 %collective-permute-start.4 = (bf16[16,128,512]{2,1,0:T(8,128)(2,1)}, bf16[16,128,512]{2,1,0:T(8,128)(2,1)}, u32[]{:S(2)}, u32[]{:S(2)}) collective-permute-start(bf16[16,128,512]{2,1,0:T(8,128)(2,1)} %get-tuple-element.208), channel_id=1, source_target_pairs={{0,16},{16,0},{1,17},{17,1},{2,18},{18,2},{3,19},{19,3},{4,20},{20... | collective-permute-start | bytes 6291464 | tf_op jit(solution)/shard_map/ppermute | solution.py:35
  237.5 74.0 %collective-permute-start.5 = (bf16[16,128,512]{2,1,0:T(8,128)(2,1)}, bf16[16,128,512]{2,1,0:T(8,128)(2,1)}, u32[]{:S(2)}, u32[]{:S(2)}) collective-permute-start(bf16[16,128,512]{2,1,0:T(8,128)(2,1)} %get-tuple-element.207), channel_id=1, source_target_pairs={{0,16},{16,0},{1,17},{17,1},{2,18},{18,2},{3,19},{19,3},{4,20},{20... | collective-permute-start | bytes 6291464 | tf_op jit(solution)/shard_map/ppermute | solution.py:35
  266.5 45.4 %all-to-all-start.1 = ((bf16[32,64,128]{2,1,0:T(8,128)(2,1)}), bf16[32,64,128]{2,1,0:T(8,128)(2,1)}, u32[]{:S(2)}, u32[]{:S(2)}) async-start(bf16[32,64,128]{2,1,0:T(8,128)(2,1)} %copy-done.50), calls=%async_computation.1 | async-start | bytes 1048576 | tf_op jit(solution)/shard_map/all_to_all | solution.py:566
  269.8 429.1 %reduce-scatter.4.cloned.1.call-start = ((), (), s32[]{:S(2)}) async-start(), calls=%async_computation.7 | async-start | bytes 8257536 | tf_op jit(solution)/shard_map/reduce_scatter | solution.py:1041
  270.3 48.7 %collective-permute-start.6 = (bf16[16,128,512]{2,1,0:T(8,128)(2,1)}, bf16[16,128,512]{2,1,0:T(8,128)(2,1)}, u32[]{:S(2)}, u32[]{:S(2)}) collective-permute-start(bf16[16,128,512]{2,1,0:T(8,128)(2,1)} %collective-permute-done.4.g_ref), channel_id=1, source_target_pairs={{0,1},{1,0},{2,3},{3,2},{4,5},{5,4},{6,7},{7,6},{8,9},{9,8},{10,11... | collective-permute-start | bytes 6291464 | tf_op jit(solution)/shard_map/ppermute | solution.py:35
  311.8 36.0 %collective-permute-start.7 = (bf16[16,128,512]{2,1,0:T(8,128)(2,1)}, bf16[16,128,512]{2,1,0:T(8,128)(2,1)}, u32[]{:S(2)}, u32[]{:S(2)}) collective-permute-start(bf16[16,128,512]{2,1,0:T(8,128)(2,1)} %collective-permute-done.5.g_ref), channel_id=1, source_target_pairs={{0,1},{1,0},{2,3},{3,2},{4,5},{5,4},{6,7},{7,6},{8,9},{9,8},{10,11... | collective-permute-start | bytes 6291464 | tf_op jit(solution)/shard_map/ppermute | solution.py:35
  368.8 42.2 %collective-permute-start.13 = (bf16[1,256,2048]{2,1,0:T(8,128)(2,1)S(1)}, bf16[1,256,2048]{2,1,0:T(8,128)(2,1)S(1)}, u32[]{:S(2)}, u32[]{:S(2)}) collective-permute-start(bf16[1,256,2048]{2,1,0:T(8,128)(2,1)S(1)} %bitcast.508), channel_id=1, source_target_pairs={{0,16},{16,0},{1,17},{17,1},{2,18},{18,2},{3,19},{19,3},{4,20},{20... | collective-permute-start | bytes 3145736 | tf_op jit(solution)/shard_map/ppermute | solution.py:35
  368.8 42.2 %collective-permute-start.9 = (bf16[1,256,2048]{2,1,0:T(8,128)(2,1)S(1)}, bf16[1,256,2048]{2,1,0:T(8,128)(2,1)S(1)}, u32[]{:S(2)}, u32[]{:S(2)}) collective-permute-start(bf16[1,256,2048]{2,1,0:T(8,128)(2,1)S(1)} %get-tuple-element.201), channel_id=1, source_target_pairs={{0,1},{1,0},{2,3},{3,2},{4,5},{5,4},{6,7},{7,6},{8,9},{9,8},{10,11... | collective-permute-start | bytes 3145736 | tf_op jit(solution)/shard_map/ppermute | solution.py:35
  520.8 295.5 %reduce-scatter.6.cloned.1.call-start = ((), (), s32[]{:S(2)}) async-start(), calls=%async_computation.8 | async-start | bytes 8257536 | tf_op jit(solution)/shard_map/reduce_scatter | solution.py:1046
  626.4 41.9 %all-to-all-start.2 = ((bf16[32,80,128]{2,1,0:T(8,128)(2,1)}), bf16[32,80,128]{2,1,0:T(8,128)(2,1)S(1)}, u32[]{:S(2)}, u32[]{:S(2)}) async-start(bf16[32,80,128]{2,1,0:T(8,128)(2,1)} %pad_maximum_fusion.11), calls=%async_computation.2 | async-start | bytes 1310720 | tf_op jit(solution)/shard_map/all_to_all | solution.py:550
  673.1 355.1 %reduce-scatter.8.cloned.1.call-start = ((), (), s32[]{:S(2)}) async-start(), calls=%async_computation.9 | async-start | bytes 7077888 | tf_op jit(solution)/shard_map/reduce_scatter | solution.py:1089
  677.2 62.1 %collective-permute-start.23 = (bf16[3,256,1024]{2,1,0:T(8,128)(2,1)}, bf16[3,256,1024]{2,1,0:T(8,128)(2,1)}, u32[]{:S(2)}, u32[]{:S(2)}) collective-permute-start(bf16[3,256,1024]{2,1,0:T(8,128)(2,1)} %get-tuple-element.230), channel_id=1, source_target_pairs={{0,16},{16,0},{1,17},{17,1},{2,18},{18,2},{3,19},{19,3},{4,20},{20... | collective-permute-start | bytes 4718600 | tf_op jit(solution)/shard_map/ppermute | solution.py:35
  678.8 60.5 %collective-permute-start.24 = (bf16[1,256,2048]{2,1,0:T(8,128)(2,1)S(1)}, bf16[1,256,2048]{2,1,0:T(8,128)(2,1)}, u32[]{:S(2)}, u32[]{:S(2)}) collective-permute-start(bf16[1,256,2048]{2,1,0:T(8,128)(2,1)S(1)} %bitcast.500), channel_id=1, source_target_pairs={{0,16},{16,0},{1,17},{17,1},{2,18},{18,2},{3,19},{19,3},{4,20},{20... | collective-permute-start | bytes 3145736 | tf_op jit(solution)/shard_map/ppermute | solution.py:35
  742.2 37.1 %collective-permute-start.25 = (bf16[3,256,1024]{2,1,0:T(8,128)(2,1)}, bf16[3,256,1024]{2,1,0:T(8,128)(2,1)}, u32[]{:S(2)}, u32[]{:S(2)}) collective-permute-start(bf16[3,256,1024]{2,1,0:T(8,128)(2,1)} %get-tuple-element.231), channel_id=1, source_target_pairs={{0,16},{16,0},{1,17},{17,1},{2,18},{18,2},{3,19},{19,3},{4,20},{20... | collective-permute-start | bytes 4718600 | tf_op jit(solution)/shard_map/ppermute | solution.py:35
  798.4 88.2 %collective-permute-start.31 = (bf16[1024,1536]{1,0:T(8,128)(2,1)}, bf16[1024,1536]{1,0:T(8,128)(2,1)}, u32[]{:S(2)}, u32[]{:S(2)}) collective-permute-start(bf16[1024,1536]{1,0:T(8,128)(2,1)} %weight_grad.5), channel_id=1, source_target_pairs={{0,2},{2,0},{1,3},{3,1},{4,6},{6,4},{5,7},{7,5},{8,10},{10,8},{9,1... | collective-permute-start | bytes 9437192 | tf_op jit(solution)/shard_map/ppermute | solution.py:35
  895.4 31.9 %collective-permute-start.32 = (bf16[256,1536]{0,1:T(8,128)(2,1)}, bf16[256,1536]{0,1:T(8,128)(2,1)}, u32[]{:S(2)}, u32[]{:S(2)}) collective-permute-start(bf16[256,1536]{0,1:T(8,128)(2,1)} %bitcast.620), channel_id=1, source_target_pairs={{0,4},{1,5},{2,6},{3,7},{16,20},{17,21},{18,22},{19,23}} | collective-permute-start | bytes 2359304 | tf_op jit(solution)/shard_map/ppermute | solution.py:66
  960.1 37.8 %collective-permute-start.43 = (bf16[128,1,1792]{2,0,1:T(8,128)(2,1)S(1)}, bf16[128,1,1792]{2,0,1:T(8,128)(2,1)S(1)}, u32[]{:S(2)}, u32[]{:S(2)}) collective-permute-start(bf16[128,1,1792]{2,0,1:T(8,128)(2,1)S(1)} %get-tuple-element.260), channel_id=1, source_target_pairs={{0,1},{1,0},{2,3},{3,2},{4,5},{5,4},{6,7},{7,6},{8,9},{9,8},{10,11... | collective-permute-start | bytes 1376264 | tf_op jit(solution)/shard_map/ppermute | solution.py:35
  960.2 47.1 %collective-permute-start.45 = (bf16[128,1,1792]{2,0,1:T(8,128)(2,1)S(1)}, bf16[128,1,1792]{2,0,1:T(8,128)(2,1)S(1)}, u32[]{:S(2)}, u32[]{:S(2)}) collective-permute-start(bf16[128,1,1792]{2,0,1:T(8,128)(2,1)S(1)} %get-tuple-element.260), channel_id=1, source_target_pairs={{0,17},{1,16},{16,1},{17,0},{2,19},{3,18},{18,3},{19,2},{4,21},{5,... | collective-permute-start | bytes 1376264 | tf_op jit(solution)/shard_map/ppermute | solution.py:175
  963.8 88.6 %collective-permute-start.41 = (bf16[256,1536]{0,1:T(8,128)(2,1)}, bf16[256,1536]{0,1:T(8,128)(2,1)}, u32[]{:S(2)}, u32[]{:S(2)}) collective-permute-start(bf16[256,1536]{0,1:T(8,128)(2,1)} %fusion.45), channel_id=1, source_target_pairs={{0,4},{4,8},{8,12},{1,5},{5,9},{9,13},{2,6},{6,10},{10,14},{3,7},{... | collective-permute-start | bytes 2359304 | tf_op jit(solution)/shard_map/ppermute | solution.py:66
  996.6 55.9 %collective-permute-start.42 = (bf16[256,1536]{0,1:T(8,128)(2,1)}, bf16[256,1536]{0,1:T(8,128)(2,1)}, u32[]{:S(2)}, u32[]{:S(2)}) collective-permute-start(bf16[256,1536]{0,1:T(8,128)(2,1)} %fusion.44), channel_id=1, source_target_pairs={{4,0},{8,4},{12,8},{5,1},{9,5},{13,9},{6,2},{10,6},{14,10},{7,3},{... | collective-permute-start | bytes 2359304 | tf_op jit(solution)/shard_map/ppermute | solution.py:67
  (192 other events, 2741.0 us)
Sparse Core Ops, SparseCore 0:
  12.9 188.5 all-gather.6
  203.6 207.0 all-gather.8
  520.9 147.4 reduce-scatter.3
  671.9 139.9 reduce-scatter.5
  848.8 139.1 reduce-scatter.7

commit v6 on v5

--- a/solution.py
+++ b/solution.py
@@ -1079,13 +1079,14 @@
     main_near, side_across, rec_across = tie(main_near, side_across, rec_across)
     rec_all = (rec_low, rec_near, rec_across, swap(rec_across, "core"))
     side_lefts = [(rec_all, 0, 1), (gated_all, 0, 1), (mix_all, 0, 1)]
-    side_give, side_keep = x_rows(side_lefts, quarter_cols(side_near, side_across))
+    side_right, g_rec, g_key, g_val, g_gate_low, g_decay_low = tie(
+        quarter_cols(side_near, side_across), g_rec, g_key, g_val, g_gate_low, g_decay_low
+    )
+    side_give, side_keep = x_rows(side_lefts, side_right)
     side_got = swap(side_give, "x")
     main_across, side_keep = tie(main_across, side_keep)
     main = all_rows([(mix_all, 1, 3)], quarter_cols(main_near, main_across))
-    main, g_rec, g_key, g_val, g_gate_low, g_decay_low, key_part = tie(
-        main, g_rec, g_key, g_val, g_gate_low, g_decay_low, key_part
-    )
+    main, key_part = tie(main, key_part)
     main = lax.psum_scatter(main, ("z", "x"), scatter_dimension=0, tiled=True)
     projs = [g_rec, g_key, g_val, g_gate_low]
 
@@ -1131,11 +1132,9 @@
            g_maa_key, g_maa_rec]
     )
     packed = pack_columns(up_grads + [decay_up_grad, mix_down_grad, decay_down_grad] + vec_rows)
-    packed, moving = tie(packed, moving)
+    packed, moving, value_part, key_part = tie(packed, moving, value_part, key_part)
     for t in range(2, zs - 1):
         moving = line_step(side, t, moving)
-    packed, moving, value_part, key_part = tie(small_core(packed), moving, value_part, key_part)
-    moving = line_step(side, zs - 1, moving)
     first = y == 0
     other = swap(value_part, "y")
     value_share = jnp.concatenate(
@@ -1143,6 +1142,8 @@
     ).astype(F32)
     key_share = spread_cols(key_part[:, None])[0].reshape(-1, 2, 2, zs, 2, half)
     key_share = key_share.transpose(0, 3, 4, 2, 1, 5).reshape(-1, ff)
+    packed, moving = tie(small_core(packed), moving)
+    moving = line_step(side, zs - 1, moving)
     packed, main, g_normed = tie(packed, main, g_normed)
     back_one, _, _ = norm_backward(g_normed, hat, rstd, vec[0])
     input_grad = (grad_first + back_one).reshape(tokens.shape)

time: 1100 us -> 1060 us (0.964)
  starting transfers between devices: 110 us -> 90.9 us
  waiting for transfers between devices: 411 us -> 394 us
    ppermute x3, starting transfers between devices: 40.8 us -> 9.79 us  [line_step(): lax.ppermute(low(right), 'z', [(i, i + 1) for i in range(count - 1) if i...]
    ppermute x3, waiting for transfers between devices: 26 us -> 0.01 us  [line_step(): lax.ppermute(low(right), 'z', [(i, i + 1) for i in range(count - 1) if i...]
    ppermute x38, starting transfers between devices: 29 us -> 43 us  [swap(): return lax.ppermute(value, axis, [(0, 1), (1, 0)])]
    unnamed x321 -> x317, local copies, waits for them, and re-layouts: 50.1 us -> 50.1 us
  transfers between devices with their start and end apart: 62 -> 62, of which waited for: 27 -> 26; matrix products, arithmetic and copies ran while one was open for 18% -> 19% of each run, Pallas kernels for 20% -> 21%
where the time goes in v6:
time: 1060 us; the launch traced here: 1050 us
  waiting for transfers between devices  394 us (37%)
  Pallas kernels  243 us (23%)
  local copies, waits for them, and re-layouts  101 us (10%)
  other arithmetic  97.5 us (9%)
  starting transfers between devices  90.9 us (9%)
  blocking collectives  57.6 us (5%)
  matrix products  54.7 us (5%)
  between operations  16.3 us (2%)
    ppermute x38, waiting for transfers between devices, swap(): return lax.ppermute(value, axis, [(0, 1), (1, 0)])  306 us
    pallas_call x6, Pallas kernels, ffn_call(): pl.pallas_call(kernel, grid_spec=pltpu.PrefetchScalarGridSpec(num_scalar_...  69.1 us
    pallas_call x4, Pallas kernels, wkv_call(): pl.pallas_call(kernel, grid=(seqs, width // SPAN), in_specs=[spec(a) for...  64.1 us
    all_gather x2, blocking collectives, columns(): gathered = lax.all_gather(shard, WIDE, axis=0)  57.6 us
    all_to_all x2, waiting for transfers between devices, chain(): packed = lax.all_to_all(packed, ALL, 0, 0, tiled=True)  57.6 us
    unnamed x317, local copies, waits for them, and re-layouts  50.1 us
    ppermute x38, starting transfers between devices, swap(): return lax.ppermute(value, axis, [(0, 1), (1, 0)])  43 us
    pallas_call x3, Pallas kernels, grad_call(): pl.pallas_call(kernel, grid_spec=pltpu.PrefetchScalarGridSpec(num_scalar_...  39 us
  transfers between devices with their start and end apart: 62, of which 26 were waited for; matrix products, arithmetic and copies ran while one was open for 19% of the time, Pallas kernels for 21%

profile of v6, /device:TPU:0, one launch (start us, length us, event | category | flops | bytes accessed | tf_op | source)
XLA Modules:
  0.0 1054.5 jit_solution(5953520740563017269)
XLA Ops:
  24.3 31.5 %all-gather = bf16[3840,128]{1,0:T(8,128)(2,1)S(1)} all-gather(bf16[240,128]{1,0:T(8,128)(2,1)S(1)} %pad_maximum_fusion.13), channel_id=2, replica_groups=mesh['y'=2,'z'=4,'x'=2,'core'=2] {'z','x','core'}, dimensions={0}, use_global_device_ids=true | all-gather | bytes 1044480 | tf_op jit(solution)/shard_map/all_gather | solution.py:964
  60.2 26.2 %all-gather.1 = bf16[3584,128]{1,0:T(8,128)(2,1)S(1)} all-gather(bf16[224,128]{1,0:T(8,128)(2,1)S(1)} %bitcast.624), channel_id=3, replica_groups=mesh['y'=2,'z'=4,'x'=2,'core'=2] {'z','x','core'}, dimensions={0}, use_global_device_ids=true | all-gather | bytes 974848 | tf_op jit(solution)/shard_map/all_gather | solution.py:964
  101.2 91.8 %collective-permute-done.2.refs_10_.refs_2_ = bf16[4,256,2048]{2,1,0:T(8,128)(2,1)} collective-permute-done((bf16[4,256,2048]{2,1,0:T(8,128)(2,1)}, bf16[4,256,2048]{2,1,0:T(8,128)(2,1)}, u32[]{:S(2)}, u32[]{:S(2)}) %collective-permute-start.2) | collective-permute-done | bytes 4194336 | tf_op jit(solution)/shard_map/ppermute | solution.py:35
  239.2 24.7 %all-to-all-done.refs_1_ = bf16[32,80,128]{2,1,0:T(8,128)(2,1)} async-done(((bf16[32,80,128]{2,1,0:T(8,128)(2,1)}), bf16[32,80,128]{2,1,0:T(8,128)(2,1)}, u32[]{:S(2)}, u32[]{:S(2)}) %all-to-all-start) | async-done | bytes 655392 | tf_op jit(solution)/shard_map/all_to_all | solution.py:550
  271.5 40.1 %collective-permute-done.5.g_ref = bf16[16,128,512]{2,1,0:T(8,128)(2,1)} collective-permute-done((bf16[16,128,512]{2,1,0:T(8,128)(2,1)}, bf16[16,128,512]{2,1,0:T(8,128)(2,1)}, u32[]{:S(2)}, u32[]{:S(2)}) %collective-permute-start.5) | collective-permute-done | bytes 2097184 | tf_op jit(solution)/shard_map/ppermute | solution.py:35
  329.2 17.2 %wkv_forward.1 = (f32[256,2048]{1,0:T(8,128)S(1)}, bf16[256,2048]{1,0:T(8,128)(2,1)S(1)}) custom-call(f32[256,2048]{1,0:T(8,128)S(1)} %stack_nn.3.rec_ref, f32[256,2048]{1,0:T(8,128)S(1)} %stack_nn.4.key_ref, f32[256,2048]{1,0:T(8,128)S(1)} %copy-done.11, f32[256,2048]{1,0:T(8,128)S(1)} %copy-done.34, bf16[2,16,64,128]{3,2,1,0:T(8,128)(2,1)} %bitcast.33.state_ref, ...), custom_call_target="tpu_custom_call" | custom-call | flops 1610612736 | bytes 14286848 | tf_op jit(solution)/shard_map/wkv_forward/pallas_call | solution.py:506
  368.8 24.0 %collective-permute-done.10 = bf16[1,256,2048]{2,1,0:T(8,128)(2,1)S(1)} collective-permute-done((bf16[1,256,2048]{2,1,0:T(8,128)(2,1)S(1)}, bf16[1,256,2048]{2,1,0:T(8,128)(2,1)S(1)}, u32[]{:S(2)}, u32[]{:S(2)}) %collective-permute-start.10) | collective-permute-done | bytes 1048608 | tf_op jit(solution)/shard_map/ppermute | solution.py:35
  393.4 17.5 %collective-permute-done.13.refs_6_ = bf16[1,256,2048]{2,1,0:T(8,128)(2,1)S(1)} collective-permute-done((bf16[1,256,2048]{2,1,0:T(8,128)(2,1)S(1)}, bf16[1,256,2048]{2,1,0:T(8,128)(2,1)S(1)}, u32[]{:S(2)}, u32[]{:S(2)}) %collective-permute-start.13) | collective-permute-done | bytes 1048608 | tf_op jit(solution)/shard_map/ppermute | solution.py:35
  415.2 13.4 %key_forward.1 = (bf16[1024,1792]{1,0:T(8,128)(2,1)}, bf16[1024,1792]{1,0:T(8,128)(2,1)}) custom-call(s32[1]{0:T(128)} %bitcast.2.c_ref, bf16[1024,2048]{1,0:T(8,128)(2,1)} %maximum_bitcast_fusion.a_ref, bf16[16,4608,256]{2,1,0:T(8,128)(2,1)} %bitcast.549), custom_call_target="tpu_custom_call" | custom-call | flops 7516192768 | bytes 18874368 | tf_op jit(solution)/shard_map/key_forward/pallas_call | solution.py:759
  428.6 13.1 %value_forward.1 = bf16[1024,2048]{1,0:T(8,128)(2,1)} custom-call(s32[1]{0:T(128)} %bitcast.2.c_ref, bf16[1024,1792]{1,0:T(8,128)(2,1)} %get-tuple-element.93.a_ref, bf16[8,2,4608,256]{3,2,1,0:T(8,128)(2,1)} %bitcast.550), custom_call_target="tpu_custom_call" | custom-call | flops 7516192768 | bytes 15204352 | tf_op jit(solution)/shard_map/value_forward/pallas_call | solution.py:759
  462.4 13.8 %collective-permute-done.16 = bf16[256,2048]{1,0:T(8,128)(2,1)} collective-permute-done((bf16[256,2048]{1,0:T(8,128)(2,1)}, bf16[256,2048]{1,0:T(8,128)(2,1)}, u32[]{:S(2)}, u32[]{:S(2)}) %collective-permute-start.16) | collective-permute-done | bytes 1048608 | tf_op jit(solution)/shard_map/ppermute | solution.py:35
  482.3 23.4 %collective-permute-done.18 = bf16[1,256,2048]{2,1,0:T(8,128)(2,1)S(1)} collective-permute-done((bf16[1,256,2048]{2,1,0:T(8,128)(2,1)S(1)}, bf16[1,256,2048]{2,1,0:T(8,128)(2,1)S(1)}, u32[]{:S(2)}, u32[]{:S(2)}) %collective-permute-start.18) | collective-permute-done | bytes 1048608 | tf_op jit(solution)/shard_map/ppermute | solution.py:35
  520.9 14.2 %value_backward.1.a_ref = bf16[1024,1792]{1,0:T(8,128)(2,1)} custom-call(s32[1]{0:T(128)} %bitcast.2.c_ref, bf16[1024,2048]{1,0:T(8,128)(2,1)} %maximum_bitcast_fusion.1.a_ref, bf16[1024,1792]{1,0:T(8,128)(2,1)} %get-tuple-element.95.r_ref, bf16[8,2,4608,256]{3,2,1,0:T(8,128)(2,1)} %bitcast.552), custom_call_target="tpu_custom_call" | custom-call | flops 7516192768 | bytes 15204352 | tf_op jit(solution)/shard_map/value_backward/pallas_call | solution.py:759
  535.1 12.3 %key_backward.1 = bf16[1024,2048]{1,0:T(8,128)(2,1)} custom-call(s32[1]{0:T(128)} %bitcast.2.c_ref, bf16[1024,1792]{1,0:T(8,128)(2,1)} %value_backward.1.a_ref, bf16[16,4608,256]{2,1,0:T(8,128)(2,1)} %bitcast.553), custom_call_target="tpu_custom_call" | custom-call | flops 7516192768 | bytes 15204352 | tf_op jit(solution)/shard_map/key_backward/pallas_call | solution.py:759
  572.4 17.4 %collective-permute-done.21 = bf16[256,2048]{1,0:T(8,128)(2,1)S(1)} collective-permute-done((bf16[256,2048]{1,0:T(8,128)(2,1)}, bf16[256,2048]{1,0:T(8,128)(2,1)S(1)}, u32[]{:S(2)}, u32[]{:S(2)}) %collective-permute-start.21) | collective-permute-done | bytes 1048608 | tf_op jit(solution)/shard_map/ppermute | solution.py:35
  611.1 13.4 %gate_backward.1 = (bf16[256,2048]{1,0:T(8,128)(2,1)S(1)}, bf16[256,2048]{1,0:T(8,128)(2,1)S(1)}, bf16[2,16,64,128]{3,2,1,0:T(8,128)(2,1)S(1)}, f32[2,8,2048]{2,1,0:T(8,128)S(1)}) custom-call(f32[256,2048]{1,0:T(8,128)S(1)} %half_nt.2.grad_ref, f32[256,2048]{1,0:T(8,128)S(1)} %copy-done.52, f32[256,2048]{1,0:T(8,128)S(1)} %copy-done.17, ...), custom_call_target="tpu_custom_call" | custom-call | flops 1610612736 | bytes 13369344 | tf_op jit(solution)/shard_map/gate_backward/pallas_call | solution.py:506
  635.4 32.9 %all-to-all-done.2.refs_1_ = bf16[32,80,128]{2,1,0:T(8,128)(2,1)S(1)} async-done(((bf16[32,80,128]{2,1,0:T(8,128)(2,1)}), bf16[32,80,128]{2,1,0:T(8,128)(2,1)S(1)}, u32[]{:S(2)}, u32[]{:S(2)}) %all-to-all-start.2) | async-done | bytes 655392 | tf_op jit(solution)/shard_map/all_to_all | solution.py:550
  679.3 19.7 %all-to-all-done.3 = bf16[32,64,128]{2,1,0:T(8,128)(2,1)} async-done(((bf16[32,64,128]{2,1,0:T(8,128)(2,1)}), bf16[32,64,128]{2,1,0:T(8,128)(2,1)}, u32[]{:S(2)}, u32[]{:S(2)}) %all-to-all-start.3) | async-done | bytes 524320 | tf_op jit(solution)/shard_map/all_to_all | solution.py:566
  703.4 24.9 %wkv_backward.1 = (bf16[256,2048]{1,0:T(8,128)(2,1)S(1)}, bf16[256,2048]{1,0:T(8,128)(2,1)S(1)}, bf16[256,2048]{1,0:T(8,128)(2,1)S(1)}, bf16[256,2048]{1,0:T(8,128)(2,1)S(1)}, f32[2,8,2048]{2,1,0:T(8,128)S(1)}) custom-call(f32[256,2048]{1,0:T(8,128)S(1)} %copy-done.15, f32[256,2048]{1,0:T(8,128)S(1)} %copy-done.9, f32[256,2048]{1,0:T(8,128)S(1)} %copy-done.12, ...), custom_call_target="tpu_custom_call" | custom-call | flops 4294967296 | bytes 17039360 | tf_op jit(solution)/shard_map/wkv_backward/pallas_call | solution.py:506
  763.9 15.9 %collective-permute-done.30 = bf16[3,256,1024]{2,1,0:T(8,128)(2,1)} collective-permute-done((bf16[3,256,1024]{2,1,0:T(8,128)(2,1)}, bf16[3,256,1024]{2,1,0:T(8,128)(2,1)}, u32[]{:S(2)}, u32[]{:S(2)}) %collective-permute-start.30) | collective-permute-done | bytes 1572896 | tf_op jit(solution)/shard_map/ppermute | solution.py:35
  781.6 12.4 %weight_grad.3 = bf16[1024,1536]{1,0:T(8,128)(2,1)} custom-call(s32[1]{0:T(128)} %bitcast.99.x_ref, bf16[1,256,2048]{2,1,0:T(8,128)(2,1)S(1)} %bitcast.503, bf16[1,256,2048]{2,1,0:T(8,128)(2,1)S(1)} %collective-permute-done.27.refs_1_, bf16[1,256,2048]{2,1,0:T(8,128)(2,1)} %collective-permute-done.24.refs_2_, ...), custom_call_target="tpu_custom_call" | custom-call | flops 3221225472 | bytes 12582912 | tf_op jit(solution)/shard_map/weight_grad/pallas_call | solution.py:228
  825.6 14.8 %weight_grad.5 = bf16[2048,1536]{1,0:T(8,128)(2,1)} custom-call(s32[1]{0:T(128)} %bitcast.99.x_ref, bf16[4,256,2048]{2,1,0:T(8,128)(2,1)} %pad_maximum_fusion.refs_8_.refs_0_, bf16[4,256,2048]{2,1,0:T(8,128)(2,1)} %collective-permute-done.1.refs_9_.refs_1_, bf16[4,256,2048]{2,1,0:T(8,128)(2,1)} %collective-permute-done.2.refs_10_.refs_2_, ...), custom_call_target="tpu_custom_call" | custom-call | flops 6442450944 | bytes 22020096 | tf_op jit(solution)/shard_map/weight_grad/pallas_call | solution.py:228
  915.5 14.3 %collective-permute-start.43 = (bf16[128,1,1792]{2,0,1:T(8,128)(2,1)S(1)}, bf16[128,1,1792]{2,0,1:T(8,128)(2,1)S(1)}, u32[]{:S(2)}, u32[]{:S(2)}) collective-permute-start(bf16[128,1,1792]{2,0,1:T(8,128)(2,1)S(1)} %get-tuple-element.262), channel_id=1, source_target_pairs={{0,1},{1,0},{2,3},{3,2},{4,5},{5,4},{6,7},{7,6},{8,9},{9,8},{10,11... | collective-permute-start | bytes 1376264 | tf_op jit(solution)/shard_map/ppermute | solution.py:35
  999.2 13.7 %collective-permute-done.38 = bf16[128,3,512]{0,2,1:T(8,128)(2,1)S(1)} collective-permute-done((bf16[128,3,512]{0,2,1:T(8,128)(2,1)S(1)}, bf16[128,3,512]{0,2,1:T(8,128)(2,1)S(1)}, u32[]{:S(2)}, u32[]{:S(2)}) %collective-permute-start.38) | collective-permute-done | bytes 393248 | tf_op jit(solution)/shard_map/ppermute | solution.py:35
  (609 shorter events, 495.6 us)
Async XLA Ops:
  7.2 194.3 %all-gather.7.cloned.1.call-start = ((), (), s32[]{:S(2)}) async-start(), calls=%async_computation.10 | async-start | bytes 35651584 | tf_op jit(solution)/shard_map/all_gather | solution.py:973
  12.7 402.5 %all-gather.9.cloned.1.call-start = ((), (), s32[]{:S(2)}) async-start(), calls=%async_computation.11 | async-start | bytes 40108032 | tf_op jit(solution)/shard_map/all_gather | solution.py:980
  100.0 92.9 %collective-permute-start.2 = (bf16[4,256,2048]{2,1,0:T(8,128)(2,1)}, bf16[4,256,2048]{2,1,0:T(8,128)(2,1)}, u32[]{:S(2)}, u32[]{:S(2)}) collective-permute-start(bf16[4,256,2048]{2,1,0:T(8,128)(2,1)} %pad_maximum_fusion.refs_8_.refs_0_), channel_id=1, source_target_pairs={{0,16},{16,0},{1,17},{17,1},{2,18},{18,2},{3,19},{19,3},{4,20},{20... | collective-permute-start | bytes 12582920 | tf_op jit(solution)/shard_map/ppermute | solution.py:35
  101.1 93.5 %collective-permute-start.1 = (bf16[4,256,2048]{2,1,0:T(8,128)(2,1)}, bf16[4,256,2048]{2,1,0:T(8,128)(2,1)}, u32[]{:S(2)}, u32[]{:S(2)}) collective-permute-start(bf16[4,256,2048]{2,1,0:T(8,128)(2,1)} %pad_maximum_fusion.refs_8_.refs_0_), channel_id=1, source_target_pairs={{0,1},{1,0},{2,3},{3,2},{4,5},{5,4},{6,7},{7,6},{8,9},{9,8},{10,11... | collective-permute-start | bytes 12582920 | tf_op jit(solution)/shard_map/ppermute | solution.py:35
  206.2 57.8 %collective-permute-start.4 = (bf16[16,128,512]{2,1,0:T(8,128)(2,1)}, bf16[16,128,512]{2,1,0:T(8,128)(2,1)}, u32[]{:S(2)}, u32[]{:S(2)}) collective-permute-start(bf16[16,128,512]{2,1,0:T(8,128)(2,1)} %get-tuple-element.210), channel_id=1, source_target_pairs={{0,16},{16,0},{1,17},{17,1},{2,18},{18,2},{3,19},{19,3},{4,20},{20... | collective-permute-start | bytes 6291464 | tf_op jit(solution)/shard_map/ppermute | solution.py:35
  237.5 74.0 %collective-permute-start.5 = (bf16[16,128,512]{2,1,0:T(8,128)(2,1)}, bf16[16,128,512]{2,1,0:T(8,128)(2,1)}, u32[]{:S(2)}, u32[]{:S(2)}) collective-permute-start(bf16[16,128,512]{2,1,0:T(8,128)(2,1)} %get-tuple-element.209), channel_id=1, source_target_pairs={{0,16},{16,0},{1,17},{17,1},{2,18},{18,2},{3,19},{19,3},{4,20},{20... | collective-permute-start | bytes 6291464 | tf_op jit(solution)/shard_map/ppermute | solution.py:35
  266.5 45.4 %all-to-all-start.1 = ((bf16[32,64,128]{2,1,0:T(8,128)(2,1)}), bf16[32,64,128]{2,1,0:T(8,128)(2,1)}, u32[]{:S(2)}, u32[]{:S(2)}) async-start(bf16[32,64,128]{2,1,0:T(8,128)(2,1)} %copy-done.50), calls=%async_computation.1 | async-start | bytes 1048576 | tf_op jit(solution)/shard_map/all_to_all | solution.py:566
  269.8 429.1 %reduce-scatter.4.cloned.1.call-start = ((), (), s32[]{:S(2)}) async-start(), calls=%async_computation.7 | async-start | bytes 8257536 | tf_op jit(solution)/shard_map/reduce_scatter | solution.py:1041
  270.4 48.7 %collective-permute-start.6 = (bf16[16,128,512]{2,1,0:T(8,128)(2,1)}, bf16[16,128,512]{2,1,0:T(8,128)(2,1)}, u32[]{:S(2)}, u32[]{:S(2)}) collective-permute-start(bf16[16,128,512]{2,1,0:T(8,128)(2,1)} %collective-permute-done.4.g_ref), channel_id=1, source_target_pairs={{0,1},{1,0},{2,3},{3,2},{4,5},{5,4},{6,7},{7,6},{8,9},{9,8},{10,11... | collective-permute-start | bytes 6291464 | tf_op jit(solution)/shard_map/ppermute | solution.py:35
  311.9 36.0 %collective-permute-start.7 = (bf16[16,128,512]{2,1,0:T(8,128)(2,1)}, bf16[16,128,512]{2,1,0:T(8,128)(2,1)}, u32[]{:S(2)}, u32[]{:S(2)}) collective-permute-start(bf16[16,128,512]{2,1,0:T(8,128)(2,1)} %collective-permute-done.5.g_ref), channel_id=1, source_target_pairs={{0,1},{1,0},{2,3},{3,2},{4,5},{5,4},{6,7},{7,6},{8,9},{9,8},{10,11... | collective-permute-start | bytes 6291464 | tf_op jit(solution)/shard_map/ppermute | solution.py:35
  361.8 31.1 %collective-permute-start.10 = (bf16[1,256,2048]{2,1,0:T(8,128)(2,1)S(1)}, bf16[1,256,2048]{2,1,0:T(8,128)(2,1)S(1)}, u32[]{:S(2)}, u32[]{:S(2)}) collective-permute-start(bf16[1,256,2048]{2,1,0:T(8,128)(2,1)S(1)} %get-tuple-element.203), channel_id=1, source_target_pairs={{0,16},{16,0},{1,17},{17,1},{2,18},{18,2},{3,19},{19,3},{4,20},{20... | collective-permute-start | bytes 3145736 | tf_op jit(solution)/shard_map/ppermute | solution.py:35
  368.8 42.0 %collective-permute-start.13 = (bf16[1,256,2048]{2,1,0:T(8,128)(2,1)S(1)}, bf16[1,256,2048]{2,1,0:T(8,128)(2,1)S(1)}, u32[]{:S(2)}, u32[]{:S(2)}) collective-permute-start(bf16[1,256,2048]{2,1,0:T(8,128)(2,1)S(1)} %bitcast.508), channel_id=1, source_target_pairs={{0,16},{16,0},{1,17},{17,1},{2,18},{18,2},{3,19},{19,3},{4,20},{20... | collective-permute-start | bytes 3145736 | tf_op jit(solution)/shard_map/ppermute | solution.py:35
  368.8 42.0 %collective-permute-start.9 = (bf16[1,256,2048]{2,1,0:T(8,128)(2,1)S(1)}, bf16[1,256,2048]{2,1,0:T(8,128)(2,1)S(1)}, u32[]{:S(2)}, u32[]{:S(2)}) collective-permute-start(bf16[1,256,2048]{2,1,0:T(8,128)(2,1)S(1)} %get-tuple-element.203), channel_id=1, source_target_pairs={{0,1},{1,0},{2,3},{3,2},{4,5},{5,4},{6,7},{7,6},{8,9},{9,8},{10,11... | collective-permute-start | bytes 3145736 | tf_op jit(solution)/shard_map/ppermute | solution.py:35
  520.7 319.8 %reduce-scatter.6.cloned.1.call-start = ((), (), s32[]{:S(2)}) async-start(), calls=%async_computation.8 | async-start | bytes 8257536 | tf_op jit(solution)/shard_map/reduce_scatter | solution.py:1046
  626.4 41.9 %all-to-all-start.2 = ((bf16[32,80,128]{2,1,0:T(8,128)(2,1)}), bf16[32,80,128]{2,1,0:T(8,128)(2,1)S(1)}, u32[]{:S(2)}, u32[]{:S(2)}) async-start(bf16[32,80,128]{2,1,0:T(8,128)(2,1)} %pad_maximum_fusion.11), calls=%async_computation.2 | async-start | bytes 1310720 | tf_op jit(solution)/shard_map/all_to_all | solution.py:550
  673.1 316.2 %reduce-scatter.8.cloned.1.call-start = ((), (), s32[]{:S(2)}) async-start(), calls=%async_computation.9 | async-start | bytes 7077888 | tf_op jit(solution)/shard_map/reduce_scatter | solution.py:1090
  677.2 62.1 %collective-permute-start.23 = (bf16[3,256,1024]{2,1,0:T(8,128)(2,1)}, bf16[3,256,1024]{2,1,0:T(8,128)(2,1)}, u32[]{:S(2)}, u32[]{:S(2)}) collective-permute-start(bf16[3,256,1024]{2,1,0:T(8,128)(2,1)} %get-tuple-element.233), channel_id=1, source_target_pairs={{0,16},{16,0},{1,17},{17,1},{2,18},{18,2},{3,19},{19,3},{4,20},{20... | collective-permute-start | bytes 4718600 | tf_op jit(solution)/shard_map/ppermute | solution.py:35
  678.8 60.5 %collective-permute-start.24 = (bf16[1,256,2048]{2,1,0:T(8,128)(2,1)S(1)}, bf16[1,256,2048]{2,1,0:T(8,128)(2,1)}, u32[]{:S(2)}, u32[]{:S(2)}) collective-permute-start(bf16[1,256,2048]{2,1,0:T(8,128)(2,1)S(1)} %bitcast.500), channel_id=1, source_target_pairs={{0,16},{16,0},{1,17},{17,1},{2,18},{18,2},{3,19},{19,3},{4,20},{20... | collective-permute-start | bytes 3145736 | tf_op jit(solution)/shard_map/ppermute | solution.py:35
  742.7 37.1 %collective-permute-start.30 = (bf16[3,256,1024]{2,1,0:T(8,128)(2,1)}, bf16[3,256,1024]{2,1,0:T(8,128)(2,1)}, u32[]{:S(2)}, u32[]{:S(2)}) collective-permute-start(bf16[3,256,1024]{2,1,0:T(8,128)(2,1)} %get-tuple-element.229), channel_id=1, source_target_pairs={{0,16},{16,0},{1,17},{17,1},{2,18},{18,2},{3,19},{19,3},{4,20},{20... | collective-permute-start | bytes 4718600 | tf_op jit(solution)/shard_map/ppermute | solution.py:35
  781.5 43.6 %collective-permute-start.33 = (bf16[3,2,256,512]{3,2,0,1:T(8,128)(2,1)S(1)}, bf16[3,2,256,512]{3,2,0,1:T(8,128)(2,1)S(1)}, u32[]{:S(2)}, u32[]{:S(2)}) collective-permute-start(bf16[3,2,256,512]{3,2,0,1:T(8,128)(2,1)S(1)} %get-tuple-element.228), channel_id=1, source_target_pairs={{0,1},{1,0},{2,3},{3,2},{4,5},{5,4},{6,7},{7,6},{8,9},{9,8},{10,11... | collective-permute-start | bytes 4718600 | tf_op jit(solution)/shard_map/ppermute | solution.py:35
  799.9 82.0 %collective-permute-start.29 = (bf16[1024,1536]{1,0:T(8,128)(2,1)}, bf16[1024,1536]{1,0:T(8,128)(2,1)}, u32[]{:S(2)}, u32[]{:S(2)}) collective-permute-start(bf16[1024,1536]{1,0:T(8,128)(2,1)} %weight_grad.3), channel_id=1, source_target_pairs={{0,2},{2,0},{1,3},{3,1},{4,6},{6,4},{5,7},{7,5},{8,10},{10,8},{9,1... | collective-permute-start | bytes 9437192 | tf_op jit(solution)/shard_map/ppermute | solution.py:35
  930.0 48.5 %collective-permute-start.34 = (bf16[8,464,128]{2,1,0:T(8,128)(2,1)S(1)}, bf16[8,464,128]{2,1,0:T(8,128)(2,1)S(1)}, u32[]{:S(2)}, u32[]{:S(2)}) collective-permute-start(bf16[8,464,128]{2,1,0:T(8,128)(2,1)S(1)} %fusion.53), channel_id=1, source_target_pairs={{0,1},{1,0},{2,3},{3,2},{4,5},{5,4},{6,7},{7,6},{8,9},{9,8},{10,11... | collective-permute-start | bytes 2850824 | tf_op jit(solution)/shard_map/ppermute | solution.py:35
  932.7 48.2 %collective-permute-start.35 = (bf16[256,1536]{0,1:T(8,128)(2,1)}, bf16[256,1536]{0,1:T(8,128)(2,1)}, u32[]{:S(2)}, u32[]{:S(2)}) collective-permute-start(bf16[256,1536]{0,1:T(8,128)(2,1)} %fusion.49), channel_id=1, source_target_pairs={{0,4},{4,8},{1,5},{5,9},{2,6},{6,10},{3,7},{7,11},{16,20},{20,24},... | collective-permute-start | bytes 2359304 | tf_op jit(solution)/shard_map/ppermute | solution.py:66
  938.9 42.1 %collective-permute-start.36 = (bf16[256,1536]{0,1:T(8,128)(2,1)}, bf16[256,1536]{0,1:T(8,128)(2,1)}, u32[]{:S(2)}, u32[]{:S(2)}) collective-permute-start(bf16[256,1536]{0,1:T(8,128)(2,1)} %fusion.48), channel_id=1, source_target_pairs={{8,4},{12,8},{9,5},{13,9},{10,6},{14,10},{11,7},{15,11},{24,20},{2... | collective-permute-start | bytes 2359304 | tf_op jit(solution)/shard_map/ppermute | solution.py:67
  (190 other events, 2705.4 us)
Sparse Core Ops, SparseCore 0:
  12.9 188.5 all-gather.6
  203.6 206.9 all-gather.8
  520.8 147.5 reduce-scatter.3
  671.8 140.0 reduce-scatter.5
  840.7 137.1 reduce-scatter.7

commit v7 on v5

--- a/solution.py
+++ b/solution.py
@@ -247,13 +247,14 @@
     return grad_call(lefts, rights, 512, lefts[0][0][0].shape[2] // 512, lambda j, x: j)
 
 
-def x_rows(lefts, rights):
+def x_rows(lefts, rights, own):
     z = lax.axis_size("z")
     block = lefts[0][0][0].shape[2] // (2 * z)
     if block % LANES:
-        return x_parts(all_rows(lefts, rights))
-    give = grad_call(lefts, rights, block, z, lambda j, x: 2 * j + 1 - x)
-    return give, grad_call(lefts, rights, block, z, lambda j, x: 2 * j + x)
+        return x_parts(all_rows(lefts, rights))[int(own)]
+    if own:
+        return grad_call(lefts, rights, block, z, lambda j, x: 2 * j + x)
+    return grad_call(lefts, rights, block, z, lambda j, x: 2 * j + 1 - x)
 
 
 def group_pieces(values):
@@ -1079,13 +1080,15 @@
     main_near, side_across, rec_across = tie(main_near, side_across, rec_across)
     rec_all = (rec_low, rec_near, rec_across, swap(rec_across, "core"))
     side_lefts = [(rec_all, 0, 1), (gated_all, 0, 1), (mix_all, 0, 1)]
-    side_give, side_keep = x_rows(side_lefts, quarter_cols(side_near, side_across))
+    side_right, g_rec, g_key = tie(quarter_cols(side_near, side_across), g_rec, g_key)
+    side_give = x_rows(side_lefts, side_right, False)
     side_got = swap(side_give, "x")
-    main_across, side_keep = tie(main_across, side_keep)
+    main_across, side_give = tie(main_across, side_give)
     main = all_rows([(mix_all, 1, 3)], quarter_cols(main_near, main_across))
-    main, g_rec, g_key, g_val, g_gate_low, g_decay_low, key_part = tie(
-        main, g_rec, g_key, g_val, g_gate_low, g_decay_low, key_part
-    )
+    main, key_part, side_right, g_val, g_gate_low, g_decay_low = tie(
+        main, key_part, side_right, g_val, g_gate_low, g_decay_low
+    )
+    side_keep = x_rows(side_lefts, side_right, True)
     main = lax.psum_scatter(main, ("z", "x"), scatter_dimension=0, tiled=True)
     projs = [g_rec, g_key, g_val, g_gate_low]
 
@@ -1131,24 +1134,26 @@
            g_maa_key, g_maa_rec]
     )
     packed = pack_columns(up_grads + [decay_up_grad, mix_down_grad, decay_down_grad] + vec_rows)
-    packed, moving = tie(packed, moving)
+    packed, moving, value_part = tie(packed, moving, value_part)
     for t in range(2, zs - 1):
         moving = line_step(side, t, moving)
-    packed, moving, value_part, key_part = tie(small_core(packed), moving, value_part, key_part)
-    moving = line_step(side, zs - 1, moving)
     first = y == 0
     other = swap(value_part, "y")
     value_share = jnp.concatenate(
         [jnp.where(first, value_part, other), jnp.where(first, other, value_part)], 0
     ).astype(F32)
+    packed, moving, value_share, main, g_normed, key_part = tie(
+        packed, moving, value_share, main, g_normed, key_part
+    )
+    late = spread_cols(main.reshape(main.shape[0], 3, -1))
     key_share = spread_cols(key_part[:, None])[0].reshape(-1, 2, 2, zs, 2, half)
     key_share = key_share.transpose(0, 3, 4, 2, 1, 5).reshape(-1, ff)
-    packed, main, g_normed = tie(packed, main, g_normed)
+    moving = line_step(side, zs - 1, moving)
     back_one, _, _ = norm_backward(g_normed, hat, rstd, vec[0])
     input_grad = (grad_first + back_one).reshape(tokens.shape)
-    packed, moving, key_share, value_share = tie(small_cross(packed), moving, key_share, value_share)
+    packed = small_cross(small_core(packed))
+    packed, moving, key_share, late = tie(packed, moving, key_share, late)
     side = low(line_end(side, moving))
-    late = spread_cols(main.reshape(main.shape[0], 3, -1))
     early = spread_cols(side.reshape(side.shape[0], 3, -1))
     packed = small_sum(packed)
     rec_share = early[0]

time: 1100 us -> 1110 us (level)
  waiting for transfers between devices: 411 us -> 434 us
  starting transfers between devices: 110 us -> 93.6 us
  local copies, waits for them, and re-layouts: 102 us -> 114 us
    ppermute x3, starting transfers between devices: 40.8 us -> 21.6 us  [line_step(): lax.ppermute(low(right), 'z', [(i, i + 1) for i in range(count - 1) if i...]
    ppermute x38, waiting for transfers between devices: 298 us -> 316 us  [swap(): return lax.ppermute(value, axis, [(0, 1), (1, 0)])]
    ppermute x3, waiting for transfers between devices: 26 us -> 12.7 us  [line_step(): lax.ppermute(low(right), 'z', [(i, i + 1) for i in range(count - 1) if i...]
    reduce_scatter x1, waiting for transfers between devices: 0.01 us -> 11.9 us  [body(): lax.psum_scatter(key_part, ('z', 'x'), scatter_dimension=0, tiled=True)]
    unnamed x321 -> x356, local copies, waits for them, and re-layouts: 50.1 us -> 61.2 us
  transfers between devices with their start and end apart: 62 -> 62, of which waited for: 27 -> 30; matrix products, arithmetic and copies ran while one was open for 18% -> 18% of each run, Pallas kernels for 20% -> 20%
where the time goes in v7:
time: 1110 us; the launch traced here: 1100 us
  waiting for transfers between devices  434 us (39%)
  Pallas kernels  243 us (22%)
  local copies, waits for them, and re-layouts  114 us (10%)
  other arithmetic  97.3 us (9%)
  starting transfers between devices  93.6 us (8%)
  blocking collectives  57.6 us (5%)
  matrix products  46.3 us (4%)
  between operations  16.6 us (1%)
    ppermute x38, waiting for transfers between devices, swap(): return lax.ppermute(value, axis, [(0, 1), (1, 0)])  316 us
    pallas_call x6, Pallas kernels, ffn_call(): pl.pallas_call(kernel, grid_spec=pltpu.PrefetchScalarGridSpec(num_scalar_...  69.1 us
    pallas_call x4, Pallas kernels, wkv_call(): pl.pallas_call(kernel, grid=(seqs, width // SPAN), in_specs=[spec(a) for...  64.5 us
    unnamed x356, local copies, waits for them, and re-layouts  61.2 us
    all_to_all x2, waiting for transfers between devices, chain(): packed = lax.all_to_all(packed, ALL, 0, 0, tiled=True)  57.8 us
    all_gather x2, blocking collectives, columns(): gathered = lax.all_gather(shard, WIDE, axis=0)  57.6 us
    pallas_call x3, Pallas kernels, grad_call(): pl.pallas_call(kernel, grid_spec=pltpu.PrefetchScalarGridSpec(num_scalar_...  38.8 us
    ppermute x38, starting transfers between devices, swap(): return lax.ppermute(value, axis, [(0, 1), (1, 0)])  37.6 us
  transfers between devices with their start and end apart: 62, of which 30 were waited for; matrix products, arithmetic and copies ran while one was open for 18% of the time, Pallas kernels for 20%

profile of v7, /device:TPU:0, one launch (start us, length us, event | category | flops | bytes accessed | tf_op | source)
XLA Modules:
  0.0 1102.6 jit_solution(3002170828416324694)
XLA Ops:
  24.3 31.5 %all-gather = bf16[3840,128]{1,0:T(8,128)(2,1)S(1)} all-gather(bf16[240,128]{1,0:T(8,128)(2,1)S(1)} %pad_maximum_fusion.13), channel_id=2, replica_groups=mesh['y'=2,'z'=4,'x'=2,'core'=2] {'z','x','core'}, dimensions={0}, use_global_device_ids=true | all-gather | bytes 1044480 | tf_op jit(solution)/shard_map/all_gather | solution.py:965
  60.2 26.1 %all-gather.1 = bf16[3584,128]{1,0:T(8,128)(2,1)S(1)} all-gather(bf16[224,128]{1,0:T(8,128)(2,1)S(1)} %bitcast.624), channel_id=3, replica_groups=mesh['y'=2,'z'=4,'x'=2,'core'=2] {'z','x','core'}, dimensions={0}, use_global_device_ids=true | all-gather | bytes 974848 | tf_op jit(solution)/shard_map/all_gather | solution.py:965
  101.1 91.8 %collective-permute-done.2.refs_10_.refs_2_ = bf16[4,256,2048]{2,1,0:T(8,128)(2,1)} collective-permute-done((bf16[4,256,2048]{2,1,0:T(8,128)(2,1)}, bf16[4,256,2048]{2,1,0:T(8,128)(2,1)}, u32[]{:S(2)}, u32[]{:S(2)}) %collective-permute-start.2) | collective-permute-done | bytes 4194336 | tf_op jit(solution)/shard_map/ppermute | solution.py:35
  239.2 24.7 %all-to-all-done.refs_1_ = bf16[32,80,128]{2,1,0:T(8,128)(2,1)} async-done(((bf16[32,80,128]{2,1,0:T(8,128)(2,1)}), bf16[32,80,128]{2,1,0:T(8,128)(2,1)}, u32[]{:S(2)}, u32[]{:S(2)}) %all-to-all-start) | async-done | bytes 655392 | tf_op jit(solution)/shard_map/all_to_all | solution.py:551
  271.4 40.1 %collective-permute-done.5.g_ref = bf16[16,128,512]{2,1,0:T(8,128)(2,1)} collective-permute-done((bf16[16,128,512]{2,1,0:T(8,128)(2,1)}, bf16[16,128,512]{2,1,0:T(8,128)(2,1)}, u32[]{:S(2)}, u32[]{:S(2)}) %collective-permute-start.5) | collective-permute-done | bytes 2097184 | tf_op jit(solution)/shard_map/ppermute | solution.py:35
  329.2 17.2 %wkv_forward.1 = (f32[256,2048]{1,0:T(8,128)S(1)}, bf16[256,2048]{1,0:T(8,128)(2,1)S(1)}) custom-call(f32[256,2048]{1,0:T(8,128)S(1)} %stack_nn.3.rec_ref, f32[256,2048]{1,0:T(8,128)S(1)} %stack_nn.4.key_ref, f32[256,2048]{1,0:T(8,128)S(1)} %copy-done.8, f32[256,2048]{1,0:T(8,128)S(1)} %copy-done.32, bf16[2,16,64,128]{3,2,1,0:T(8,128)(2,1)} %bitcast.33.state_ref, ...), custom_call_target="tpu_custom_call" | custom-call | flops 1610612736 | bytes 14286848 | tf_op jit(solution)/shard_map/wkv_forward/pallas_call | solution.py:507
  368.7 24.0 %collective-permute-done.10 = bf16[1,256,2048]{2,1,0:T(8,128)(2,1)S(1)} collective-permute-done((bf16[1,256,2048]{2,1,0:T(8,128)(2,1)S(1)}, bf16[1,256,2048]{2,1,0:T(8,128)(2,1)S(1)}, u32[]{:S(2)}, u32[]{:S(2)}) %collective-permute-start.10) | collective-permute-done | bytes 1048608 | tf_op jit(solution)/shard_map/ppermute | solution.py:35
  393.3 17.5 %collective-permute-done.13.refs_6_ = bf16[1,256,2048]{2,1,0:T(8,128)(2,1)S(1)} collective-permute-done((bf16[1,256,2048]{2,1,0:T(8,128)(2,1)S(1)}, bf16[1,256,2048]{2,1,0:T(8,128)(2,1)S(1)}, u32[]{:S(2)}, u32[]{:S(2)}) %collective-permute-start.13) | collective-permute-done | bytes 1048608 | tf_op jit(solution)/shard_map/ppermute | solution.py:35
  415.1 13.4 %key_forward.1 = (bf16[1024,1792]{1,0:T(8,128)(2,1)}, bf16[1024,1792]{1,0:T(8,128)(2,1)}) custom-call(s32[1]{0:T(128)} %bitcast.2.c_ref, bf16[1024,2048]{1,0:T(8,128)(2,1)} %maximum_bitcast_fusion.a_ref, bf16[16,4608,256]{2,1,0:T(8,128)(2,1)} %bitcast.549), custom_call_target="tpu_custom_call" | custom-call | flops 7516192768 | bytes 18874368 | tf_op jit(solution)/shard_map/key_forward/pallas_call | solution.py:760
  428.5 13.1 %value_forward.1 = bf16[1024,2048]{1,0:T(8,128)(2,1)} custom-call(s32[1]{0:T(128)} %bitcast.2.c_ref, bf16[1024,1792]{1,0:T(8,128)(2,1)} %get-tuple-element.95.a_ref, bf16[8,2,4608,256]{3,2,1,0:T(8,128)(2,1)} %bitcast.550), custom_call_target="tpu_custom_call" | custom-call | flops 7516192768 | bytes 15204352 | tf_op jit(solution)/shard_map/value_forward/pallas_call | solution.py:760
  462.3 13.9 %collective-permute-done.16 = bf16[256,2048]{1,0:T(8,128)(2,1)} collective-permute-done((bf16[256,2048]{1,0:T(8,128)(2,1)}, bf16[256,2048]{1,0:T(8,128)(2,1)}, u32[]{:S(2)}, u32[]{:S(2)}) %collective-permute-start.16) | collective-permute-done | bytes 1048608 | tf_op jit(solution)/shard_map/ppermute | solution.py:35
  482.1 23.5 %collective-permute-done.18 = bf16[1,256,2048]{2,1,0:T(8,128)(2,1)S(1)} collective-permute-done((bf16[1,256,2048]{2,1,0:T(8,128)(2,1)S(1)}, bf16[1,256,2048]{2,1,0:T(8,128)(2,1)S(1)}, u32[]{:S(2)}, u32[]{:S(2)}) %collective-permute-start.18) | collective-permute-done | bytes 1048608 | tf_op jit(solution)/shard_map/ppermute | solution.py:35
  520.7 14.2 %value_backward.1.a_ref = bf16[1024,1792]{1,0:T(8,128)(2,1)} custom-call(s32[1]{0:T(128)} %bitcast.2.c_ref, bf16[1024,2048]{1,0:T(8,128)(2,1)} %maximum_bitcast_fusion.1.a_ref, bf16[1024,1792]{1,0:T(8,128)(2,1)} %get-tuple-element.97.r_ref, bf16[8,2,4608,256]{3,2,1,0:T(8,128)(2,1)} %bitcast.552), custom_call_target="tpu_custom_call" | custom-call | flops 7516192768 | bytes 15204352 | tf_op jit(solution)/shard_map/value_backward/pallas_call | solution.py:760
  534.9 12.3 %key_backward.1 = bf16[1024,2048]{1,0:T(8,128)(2,1)} custom-call(s32[1]{0:T(128)} %bitcast.2.c_ref, bf16[1024,1792]{1,0:T(8,128)(2,1)} %value_backward.1.a_ref, bf16[16,4608,256]{2,1,0:T(8,128)(2,1)} %bitcast.553), custom_call_target="tpu_custom_call" | custom-call | flops 7516192768 | bytes 15204352 | tf_op jit(solution)/shard_map/key_backward/pallas_call | solution.py:760
  572.0 17.5 %collective-permute-done.21 = bf16[256,2048]{1,0:T(8,128)(2,1)S(1)} collective-permute-done((bf16[256,2048]{1,0:T(8,128)(2,1)}, bf16[256,2048]{1,0:T(8,128)(2,1)S(1)}, u32[]{:S(2)}, u32[]{:S(2)}) %collective-permute-start.21) | collective-permute-done | bytes 1048608 | tf_op jit(solution)/shard_map/ppermute | solution.py:35
  610.8 13.4 %gate_backward.1 = (bf16[256,2048]{1,0:T(8,128)(2,1)S(1)}, bf16[256,2048]{1,0:T(8,128)(2,1)S(1)}, bf16[2,16,64,128]{3,2,1,0:T(8,128)(2,1)S(1)}, f32[2,8,2048]{2,1,0:T(8,128)S(1)}) custom-call(f32[256,2048]{1,0:T(8,128)S(1)} %half_nt.2.grad_ref, f32[256,2048]{1,0:T(8,128)S(1)} %copy-done.58, f32[256,2048]{1,0:T(8,128)S(1)} %copy-done.14, ...), custom_call_target="tpu_custom_call" | custom-call | flops 1610612736 | bytes 13369344 | tf_op jit(solution)/shard_map/gate_backward/pallas_call | solution.py:507
  635.0 33.1 %all-to-all-done.2.refs_1_ = bf16[32,80,128]{2,1,0:T(8,128)(2,1)S(1)} async-done(((bf16[32,80,128]{2,1,0:T(8,128)(2,1)}), bf16[32,80,128]{2,1,0:T(8,128)(2,1)S(1)}, u32[]{:S(2)}, u32[]{:S(2)}) %all-to-all-start.2) | async-done | bytes 655392 | tf_op jit(solution)/shard_map/all_to_all | solution.py:551
  678.7 20.1 %all-to-all-done.3 = bf16[32,64,128]{2,1,0:T(8,128)(2,1)} async-done(((bf16[32,64,128]{2,1,0:T(8,128)(2,1)}), bf16[32,64,128]{2,1,0:T(8,128)(2,1)}, u32[]{:S(2)}, u32[]{:S(2)}) %all-to-all-start.3) | async-done | bytes 524320 | tf_op jit(solution)/shard_map/all_to_all | solution.py:567
  703.2 25.3 %wkv_backward.1 = (bf16[256,2048]{1,0:T(8,128)(2,1)S(1)}, bf16[256,2048]{1,0:T(8,128)(2,1)S(1)}, bf16[256,2048]{1,0:T(8,128)(2,1)S(1)}, bf16[256,2048]{1,0:T(8,128)(2,1)S(1)}, f32[2,8,2048]{2,1,0:T(8,128)S(1)}) custom-call(f32[256,2048]{1,0:T(8,128)S(1)} %copy-done.12, f32[256,2048]{1,0:T(8,128)S(1)} %copy-done.6, f32[256,2048]{1,0:T(8,128)S(1)} %copy-done.9, ...), custom_call_target="tpu_custom_call" | custom-call | flops 4294967296 | bytes 17039360 | tf_op jit(solution)/shard_map/wkv_backward/pallas_call | solution.py:507
  764.3 15.1 %collective-permute-done.25 = bf16[3,256,1024]{2,1,0:T(8,128)(2,1)} collective-permute-done((bf16[3,256,1024]{2,1,0:T(8,128)(2,1)}, bf16[3,256,1024]{2,1,0:T(8,128)(2,1)}, u32[]{:S(2)}, u32[]{:S(2)}) %collective-permute-start.25) | collective-permute-done | bytes 1572896 | tf_op jit(solution)/shard_map/ppermute | solution.py:35
  785.0 14.8 %weight_grad.4 = bf16[2048,1536]{1,0:T(8,128)(2,1)} custom-call(s32[1]{0:T(128)} %bitcast.80.x_ref, bf16[4,256,2048]{2,1,0:T(8,128)(2,1)} %pad_maximum_fusion.refs_8_.refs_0_, bf16[4,256,2048]{2,1,0:T(8,128)(2,1)} %collective-permute-done.1.refs_9_.refs_1_, bf16[4,256,2048]{2,1,0:T(8,128)(2,1)} %collective-permute-done.2.refs_10_.refs_2_, ...), custom_call_target="tpu_custom_call" | custom-call | flops 6442450944 | bytes 22020096 | tf_op jit(solution)/shard_map/weight_grad/pallas_call | solution.py:228
  892.5 23.0 %collective-permute-done.31 = bf16[1024,1536]{1,0:T(8,128)(2,1)} collective-permute-done((bf16[1024,1536]{1,0:T(8,128)(2,1)}, bf16[1024,1536]{1,0:T(8,128)(2,1)}, u32[]{:S(2)}, u32[]{:S(2)}) %collective-permute-start.31) | collective-permute-done | bytes 3145760 | tf_op jit(solution)/shard_map/ppermute | solution.py:35
  1001.7 15.6 %collective-permute-done.45 = bf16[128,3,512]{0,2,1:T(8,128)(2,1)S(1)} collective-permute-done((bf16[128,3,512]{0,2,1:T(8,128)(2,1)S(1)}, bf16[128,3,512]{0,2,1:T(8,128)(2,1)S(1)}, u32[]{:S(2)}, u32[]{:S(2)}) %collective-permute-start.45) | collective-permute-done | bytes 393248 | tf_op jit(solution)/shard_map/ppermute | solution.py:35
  1017.3 12.2 %collective-permute-start.39 = (bf16[256,1536]{0,1:T(8,128)(2,1)}, bf16[256,1536]{0,1:T(8,128)(2,1)}, u32[]{:S(2)}, u32[]{:S(2)}) collective-permute-start(bf16[256,1536]{0,1:T(8,128)(2,1)} %fusion.47), channel_id=1, source_target_pairs={{0,4},{4,8},{8,12},{1,5},{5,9},{9,13},{2,6},{6,10},{10,14},{3,7},{... | collective-permute-start | bytes 2359304 | tf_op jit(solution)/shard_map/ppermute | solution.py:66
  (648 shorter events, 532.7 us)
Async XLA Ops:
  7.2 194.2 %all-gather.7.cloned.1.call-start = ((), (), s32[]{:S(2)}) async-start(), calls=%async_computation.10 | async-start | bytes 35651584 | tf_op jit(solution)/shard_map/all_gather | solution.py:974
  12.7 402.4 %all-gather.9.cloned.1.call-start = ((), (), s32[]{:S(2)}) async-start(), calls=%async_computation.11 | async-start | bytes 40108032 | tf_op jit(solution)/shard_map/all_gather | solution.py:981
  100.0 92.9 %collective-permute-start.2 = (bf16[4,256,2048]{2,1,0:T(8,128)(2,1)}, bf16[4,256,2048]{2,1,0:T(8,128)(2,1)}, u32[]{:S(2)}, u32[]{:S(2)}) collective-permute-start(bf16[4,256,2048]{2,1,0:T(8,128)(2,1)} %pad_maximum_fusion.refs_8_.refs_0_), channel_id=1, source_target_pairs={{0,16},{16,0},{1,17},{17,1},{2,18},{18,2},{3,19},{19,3},{4,20},{20... | collective-permute-start | bytes 12582920 | tf_op jit(solution)/shard_map/ppermute | solution.py:35
  101.0 93.5 %collective-permute-start.1 = (bf16[4,256,2048]{2,1,0:T(8,128)(2,1)}, bf16[4,256,2048]{2,1,0:T(8,128)(2,1)}, u32[]{:S(2)}, u32[]{:S(2)}) collective-permute-start(bf16[4,256,2048]{2,1,0:T(8,128)(2,1)} %pad_maximum_fusion.refs_8_.refs_0_), channel_id=1, source_target_pairs={{0,1},{1,0},{2,3},{3,2},{4,5},{5,4},{6,7},{7,6},{8,9},{9,8},{10,11... | collective-permute-start | bytes 12582920 | tf_op jit(solution)/shard_map/ppermute | solution.py:35
  206.1 57.9 %collective-permute-start.4 = (bf16[16,128,512]{2,1,0:T(8,128)(2,1)}, bf16[16,128,512]{2,1,0:T(8,128)(2,1)}, u32[]{:S(2)}, u32[]{:S(2)}) collective-permute-start(bf16[16,128,512]{2,1,0:T(8,128)(2,1)} %get-tuple-element.214), channel_id=1, source_target_pairs={{0,16},{16,0},{1,17},{17,1},{2,18},{18,2},{3,19},{19,3},{4,20},{20... | collective-permute-start | bytes 6291464 | tf_op jit(solution)/shard_map/ppermute | solution.py:35
  237.5 74.0 %collective-permute-start.5 = (bf16[16,128,512]{2,1,0:T(8,128)(2,1)}, bf16[16,128,512]{2,1,0:T(8,128)(2,1)}, u32[]{:S(2)}, u32[]{:S(2)}) collective-permute-start(bf16[16,128,512]{2,1,0:T(8,128)(2,1)} %get-tuple-element.213), channel_id=1, source_target_pairs={{0,16},{16,0},{1,17},{17,1},{2,18},{18,2},{3,19},{19,3},{4,20},{20... | collective-permute-start | bytes 6291464 | tf_op jit(solution)/shard_map/ppermute | solution.py:35
  266.5 45.3 %all-to-all-start.1 = ((bf16[32,64,128]{2,1,0:T(8,128)(2,1)}), bf16[32,64,128]{2,1,0:T(8,128)(2,1)}, u32[]{:S(2)}, u32[]{:S(2)}) async-start(bf16[32,64,128]{2,1,0:T(8,128)(2,1)} %copy-done.56), calls=%async_computation.1 | async-start | bytes 1048576 | tf_op jit(solution)/shard_map/all_to_all | solution.py:567
  269.9 428.9 %reduce-scatter.4.cloned.1.call-start = ((), (), s32[]{:S(2)}) async-start(), calls=%async_computation.7 | async-start | bytes 8257536 | tf_op jit(solution)/shard_map/reduce_scatter | solution.py:1042
  270.3 48.7 %collective-permute-start.6 = (bf16[16,128,512]{2,1,0:T(8,128)(2,1)}, bf16[16,128,512]{2,1,0:T(8,128)(2,1)}, u32[]{:S(2)}, u32[]{:S(2)}) collective-permute-start(bf16[16,128,512]{2,1,0:T(8,128)(2,1)} %collective-permute-done.4.g_ref), channel_id=1, source_target_pairs={{0,1},{1,0},{2,3},{3,2},{4,5},{5,4},{6,7},{7,6},{8,9},{9,8},{10,11... | collective-permute-start | bytes 6291464 | tf_op jit(solution)/shard_map/ppermute | solution.py:35
  311.8 36.0 %collective-permute-start.7 = (bf16[16,128,512]{2,1,0:T(8,128)(2,1)}, bf16[16,128,512]{2,1,0:T(8,128)(2,1)}, u32[]{:S(2)}, u32[]{:S(2)}) collective-permute-start(bf16[16,128,512]{2,1,0:T(8,128)(2,1)} %collective-permute-done.5.g_ref), channel_id=1, source_target_pairs={{0,1},{1,0},{2,3},{3,2},{4,5},{5,4},{6,7},{7,6},{8,9},{9,8},{10,11... | collective-permute-start | bytes 6291464 | tf_op jit(solution)/shard_map/ppermute | solution.py:35
  368.7 42.1 %collective-permute-start.13 = (bf16[1,256,2048]{2,1,0:T(8,128)(2,1)S(1)}, bf16[1,256,2048]{2,1,0:T(8,128)(2,1)S(1)}, u32[]{:S(2)}, u32[]{:S(2)}) collective-permute-start(bf16[1,256,2048]{2,1,0:T(8,128)(2,1)S(1)} %bitcast.508), channel_id=1, source_target_pairs={{0,16},{16,0},{1,17},{17,1},{2,18},{18,2},{3,19},{19,3},{4,20},{20... | collective-permute-start | bytes 3145736 | tf_op jit(solution)/shard_map/ppermute | solution.py:35
  368.7 42.1 %collective-permute-start.9 = (bf16[1,256,2048]{2,1,0:T(8,128)(2,1)S(1)}, bf16[1,256,2048]{2,1,0:T(8,128)(2,1)S(1)}, u32[]{:S(2)}, u32[]{:S(2)}) collective-permute-start(bf16[1,256,2048]{2,1,0:T(8,128)(2,1)S(1)} %get-tuple-element.207), channel_id=1, source_target_pairs={{0,1},{1,0},{2,3},{3,2},{4,5},{5,4},{6,7},{7,6},{8,9},{9,8},{10,11... | collective-permute-start | bytes 3145736 | tf_op jit(solution)/shard_map/ppermute | solution.py:35
  520.5 291.2 %reduce-scatter.6.cloned.1.call-start = ((), (), s32[]{:S(2)}) async-start(), calls=%async_computation.8 | async-start | bytes 8257536 | tf_op jit(solution)/shard_map/reduce_scatter | solution.py:1047
  626.1 42.0 %all-to-all-start.2 = ((bf16[32,80,128]{2,1,0:T(8,128)(2,1)}), bf16[32,80,128]{2,1,0:T(8,128)(2,1)S(1)}, u32[]{:S(2)}, u32[]{:S(2)}) async-start(bf16[32,80,128]{2,1,0:T(8,128)(2,1)} %pad_maximum_fusion.11), calls=%async_computation.2 | async-start | bytes 1310720 | tf_op jit(solution)/shard_map/all_to_all | solution.py:551
  672.9 303.0 %reduce-scatter.8.cloned.1.call-start = ((), (), s32[]{:S(2)}) async-start(), calls=%async_computation.9 | async-start | bytes 7077888 | tf_op jit(solution)/shard_map/reduce_scatter | solution.py:1092
  676.7 62.2 %collective-permute-start.23 = (bf16[3,256,1024]{2,1,0:T(8,128)(2,1)}, bf16[3,256,1024]{2,1,0:T(8,128)(2,1)}, u32[]{:S(2)}, u32[]{:S(2)}) collective-permute-start(bf16[3,256,1024]{2,1,0:T(8,128)(2,1)} %get-tuple-element.236), channel_id=1, source_target_pairs={{0,16},{16,0},{1,17},{17,1},{2,18},{18,2},{3,19},{19,3},{4,20},{20... | collective-permute-start | bytes 4718600 | tf_op jit(solution)/shard_map/ppermute | solution.py:35
  678.2 60.7 %collective-permute-start.24 = (bf16[1,256,2048]{2,1,0:T(8,128)(2,1)S(1)}, bf16[1,256,2048]{2,1,0:T(8,128)(2,1)}, u32[]{:S(2)}, u32[]{:S(2)}) collective-permute-start(bf16[1,256,2048]{2,1,0:T(8,128)(2,1)S(1)} %bitcast.500), channel_id=1, source_target_pairs={{0,16},{16,0},{1,17},{17,1},{2,18},{18,2},{3,19},{19,3},{4,20},{20... | collective-permute-start | bytes 3145736 | tf_op jit(solution)/shard_map/ppermute | solution.py:35
  742.2 37.1 %collective-permute-start.25 = (bf16[3,256,1024]{2,1,0:T(8,128)(2,1)}, bf16[3,256,1024]{2,1,0:T(8,128)(2,1)}, u32[]{:S(2)}, u32[]{:S(2)}) collective-permute-start(bf16[3,256,1024]{2,1,0:T(8,128)(2,1)} %get-tuple-element.237), channel_id=1, source_target_pairs={{0,16},{16,0},{1,17},{17,1},{2,18},{18,2},{3,19},{19,3},{4,20},{20... | collective-permute-start | bytes 4718600 | tf_op jit(solution)/shard_map/ppermute | solution.py:35
  812.4 103.0 %collective-permute-start.31 = (bf16[1024,1536]{1,0:T(8,128)(2,1)}, bf16[1024,1536]{1,0:T(8,128)(2,1)}, u32[]{:S(2)}, u32[]{:S(2)}) collective-permute-start(bf16[1024,1536]{1,0:T(8,128)(2,1)} %copy-done.55), channel_id=1, source_target_pairs={{0,2},{2,0},{1,3},{3,1},{4,6},{6,4},{5,7},{7,5},{8,10},{10,8},{9,1... | collective-permute-start | bytes 9437192 | tf_op jit(solution)/shard_map/ppermute | solution.py:35
  978.0 54.5 %collective-permute-start.41 = (bf16[128,1,1792]{2,0,1:T(8,128)(2,1)}, bf16[128,1,1792]{2,0,1:T(8,128)(2,1)}, u32[]{:S(2)}, u32[]{:S(2)}) collective-permute-start(bf16[128,1,1792]{2,0,1:T(8,128)(2,1)} %get-tuple-element.266), channel_id=1, source_target_pairs={{0,1},{1,0},{2,3},{3,2},{4,5},{5,4},{6,7},{7,6},{8,9},{9,8},{10,11... | collective-permute-start | bytes 1376264 | tf_op jit(solution)/shard_map/ppermute | solution.py:35
  987.4 54.1 %collective-permute-start.43 = (bf16[128,1,1792]{2,0,1:T(8,128)(2,1)}, bf16[128,1,1792]{2,0,1:T(8,128)(2,1)}, u32[]{:S(2)}, u32[]{:S(2)}) collective-permute-start(bf16[128,1,1792]{2,0,1:T(8,128)(2,1)} %get-tuple-element.266), channel_id=1, source_target_pairs={{0,17},{1,16},{16,1},{17,0},{2,19},{3,18},{18,3},{19,2},{4,21},{5,... | collective-permute-start | bytes 1376264 | tf_op jit(solution)/shard_map/ppermute | solution.py:175
  992.2 37.2 %collective-permute-start.46 = (bf16[128,3,512]{0,2,1:T(8,128)(2,1)S(1)}, bf16[128,3,512]{0,2,1:T(8,128)(2,1)S(1)}, u32[]{:S(2)}, u32[]{:S(2)}) collective-permute-start(bf16[128,3,512]{0,2,1:T(8,128)(2,1)S(1)} %get-tuple-element.270), channel_id=1, source_target_pairs={{0,17},{1,16},{16,1},{17,0},{2,19},{3,18},{18,3},{19,2},{4,21},{5,... | collective-permute-start | bytes 1179656 | tf_op jit(solution)/shard_map/ppermute | solution.py:175
  1001.5 41.3 %collective-permute-start.37 = (bf16[8,464,128]{2,1,0:T(8,128)(2,1)S(1)}, bf16[8,464,128]{2,1,0:T(8,128)(2,1)S(1)}, u32[]{:S(2)}, u32[]{:S(2)}) collective-permute-start(bf16[8,464,128]{2,1,0:T(8,128)(2,1)S(1)} %fusion.53), channel_id=1, source_target_pairs={{0,1},{1,0},{2,3},{3,2},{4,5},{5,4},{6,7},{7,6},{8,9},{9,8},{10,11... | collective-permute-start | bytes 2850824 | tf_op jit(solution)/shard_map/ppermute | solution.py:35
  1017.3 38.8 %collective-permute-start.39 = (bf16[256,1536]{0,1:T(8,128)(2,1)}, bf16[256,1536]{0,1:T(8,128)(2,1)}, u32[]{:S(2)}, u32[]{:S(2)}) collective-permute-start(bf16[256,1536]{0,1:T(8,128)(2,1)} %fusion.47), channel_id=1, source_target_pairs={{0,4},{4,8},{8,12},{1,5},{5,9},{9,13},{2,6},{6,10},{10,14},{3,7},{... | collective-permute-start | bytes 2359304 | tf_op jit(solution)/shard_map/ppermute | solution.py:66
  (208 other events, 2869.3 us)
Sparse Core Ops, SparseCore 0:
  12.9 188.4 all-gather.6
  203.5 207.0 all-gather.8
  520.6 147.6 reduce-scatter.3
  671.8 139.8 reduce-scatter.5
  815.1 151.8 reduce-scatter.7

commit v8 on v7

--- a/solution.py
+++ b/solution.py
@@ -1134,7 +1134,7 @@
            g_maa_key, g_maa_rec]
     )
     packed = pack_columns(up_grads + [decay_up_grad, mix_down_grad, decay_down_grad] + vec_rows)
-    packed, moving, value_part = tie(packed, moving, value_part)
+    packed, moving, value_part, key_part = tie(packed, moving, value_part, key_part)
     for t in range(2, zs - 1):
         moving = line_step(side, t, moving)
     first = y == 0
@@ -1142,12 +1142,10 @@
     value_share = jnp.concatenate(
         [jnp.where(first, value_part, other), jnp.where(first, other, value_part)], 0
     ).astype(F32)
-    packed, moving, value_share, main, g_normed, key_part = tie(
-        packed, moving, value_share, main, g_normed, key_part
-    )
-    late = spread_cols(main.reshape(main.shape[0], 3, -1))
     key_share = spread_cols(key_part[:, None])[0].reshape(-1, 2, 2, zs, 2, half)
     key_share = key_share.transpose(0, 3, 4, 2, 1, 5).reshape(-1, ff)
+    packed, moving, value_share, main, g_normed = tie(packed, moving, value_share, main, g_normed)
+    late = spread_cols(main.reshape(main.shape[0], 3, -1))
     moving = line_step(side, zs - 1, moving)
     back_one, _, _ = norm_backward(g_normed, hat, rstd, vec[0])
     input_grad = (grad_first + back_one).reshape(tokens.shape)

time: 1110 us -> 1060 us (0.955)
  waiting for transfers between devices: 434 us -> 393 us
    ppermute x38, waiting for transfers between devices: 316 us -> 297 us  [swap(): return lax.ppermute(value, axis, [(0, 1), (1, 0)])]
    ppermute x3, waiting for transfers between devices: 12.7 us -> 0.01 us  [line_step(): lax.ppermute(low(right), 'z', [(i, i + 1) for i in range(count - 1) if i...]
    reduce_scatter x1, waiting for transfers between devices: 11.9 us -> 0.01 us  [body(): lax.psum_scatter(key_part, ('z', 'x'), scatter_dimension=0, tiled=True)]
  transfers between devices with their start and end apart: 62 -> 62, of which waited for: 30 -> 26; matrix products, arithmetic and copies ran while one was open for 18% -> 18% of each run, Pallas kernels for 20% -> 20%
where the time goes in v8:
time: 1060 us
  waiting for transfers between devices  393 us (37%)
  Pallas kernels  242 us (23%)
  local copies, waits for them, and re-layouts  114 us (11%)
  other arithmetic  94.4 us (9%)
  starting transfers between devices  92.3 us (9%)
  blocking collectives  57.6 us (5%)
  matrix products  46.4 us (4%)
  between operations  16.5 us (2%)
    ppermute x38, waiting for transfers between devices, swap(): return lax.ppermute(value, axis, [(0, 1), (1, 0)])  297 us
    pallas_call x6, Pallas kernels, ffn_call(): pl.pallas_call(kernel, grid_spec=pltpu.PrefetchScalarGridSpec(num_scalar_...  69.1 us
    pallas_call x4, Pallas kernels, wkv_call(): pl.pallas_call(kernel, grid=(seqs, width // SPAN), in_specs=[spec(a) for...  64.5 us
    unnamed x356, local copies, waits for them, and re-layouts  62.5 us
    all_to_all x2, waiting for transfers between devices, chain(): packed = lax.all_to_all(packed, ALL, 0, 0, tiled=True)  57.8 us
    all_gather x2, blocking collectives, columns(): gathered = lax.all_gather(shard, WIDE, axis=0)  57.6 us
    pallas_call x3, Pallas kernels, grad_call(): pl.pallas_call(kernel, grid_spec=pltpu.PrefetchScalarGridSpec(num_scalar_...  39 us
    ppermute x38, starting transfers between devices, swap(): return lax.ppermute(value, axis, [(0, 1), (1, 0)])  33.8 us
  transfers between devices with their start and end apart: 62, of which 26 were waited for; matrix products, arithmetic and copies ran while one was open for 18% of the time, Pallas kernels for 20%

profile of v8, /device:TPU:0, one launch (start us, length us, event | category | flops | bytes accessed | tf_op | source)
XLA Modules:
  0.0 1056.7 jit_solution(11409071298010852258)
XLA Ops:
  24.3 31.5 %all-gather = bf16[3840,128]{1,0:T(8,128)(2,1)S(1)} all-gather(bf16[240,128]{1,0:T(8,128)(2,1)S(1)} %pad_maximum_fusion.13), channel_id=2, replica_groups=mesh['y'=2,'z'=4,'x'=2,'core'=2] {'z','x','core'}, dimensions={0}, use_global_device_ids=true | all-gather | bytes 1044480 | tf_op jit(solution)/shard_map/all_gather | solution.py:965
  60.2 26.2 %all-gather.1 = bf16[3584,128]{1,0:T(8,128)(2,1)S(1)} all-gather(bf16[224,128]{1,0:T(8,128)(2,1)S(1)} %bitcast.623), channel_id=3, replica_groups=mesh['y'=2,'z'=4,'x'=2,'core'=2] {'z','x','core'}, dimensions={0}, use_global_device_ids=true | all-gather | bytes 974848 | tf_op jit(solution)/shard_map/all_gather | solution.py:965
  101.1 91.8 %collective-permute-done.2.refs_10_.refs_2_ = bf16[4,256,2048]{2,1,0:T(8,128)(2,1)} collective-permute-done((bf16[4,256,2048]{2,1,0:T(8,128)(2,1)}, bf16[4,256,2048]{2,1,0:T(8,128)(2,1)}, u32[]{:S(2)}, u32[]{:S(2)}) %collective-permute-start.2) | collective-permute-done | bytes 4194336 | tf_op jit(solution)/shard_map/ppermute | solution.py:35
  239.2 24.7 %all-to-all-done.refs_1_ = bf16[32,80,128]{2,1,0:T(8,128)(2,1)} async-done(((bf16[32,80,128]{2,1,0:T(8,128)(2,1)}), bf16[32,80,128]{2,1,0:T(8,128)(2,1)}, u32[]{:S(2)}, u32[]{:S(2)}) %all-to-all-start) | async-done | bytes 655392 | tf_op jit(solution)/shard_map/all_to_all | solution.py:551
  271.4 40.0 %collective-permute-done.5.g_ref = bf16[16,128,512]{2,1,0:T(8,128)(2,1)} collective-permute-done((bf16[16,128,512]{2,1,0:T(8,128)(2,1)}, bf16[16,128,512]{2,1,0:T(8,128)(2,1)}, u32[]{:S(2)}, u32[]{:S(2)}) %collective-permute-start.5) | collective-permute-done | bytes 2097184 | tf_op jit(solution)/shard_map/ppermute | solution.py:35
  329.2 17.2 %wkv_forward.1 = (f32[256,2048]{1,0:T(8,128)S(1)}, bf16[256,2048]{1,0:T(8,128)(2,1)S(1)}) custom-call(f32[256,2048]{1,0:T(8,128)S(1)} %stack_nn.3.rec_ref, f32[256,2048]{1,0:T(8,128)S(1)} %stack_nn.4.key_ref, f32[256,2048]{1,0:T(8,128)S(1)} %copy-done.9, f32[256,2048]{1,0:T(8,128)S(1)} %copy-done.33, bf16[2,16,64,128]{3,2,1,0:T(8,128)(2,1)} %bitcast.33.state_ref, ...), custom_call_target="tpu_custom_call" | custom-call | flops 1610612736 | bytes 14286848 | tf_op jit(solution)/shard_map/wkv_forward/pallas_call | solution.py:507
  368.8 24.0 %collective-permute-done.10 = bf16[1,256,2048]{2,1,0:T(8,128)(2,1)S(1)} collective-permute-done((bf16[1,256,2048]{2,1,0:T(8,128)(2,1)S(1)}, bf16[1,256,2048]{2,1,0:T(8,128)(2,1)S(1)}, u32[]{:S(2)}, u32[]{:S(2)}) %collective-permute-start.10) | collective-permute-done | bytes 1048608 | tf_op jit(solution)/shard_map/ppermute | solution.py:35
  393.3 17.6 %collective-permute-done.13.refs_6_ = bf16[1,256,2048]{2,1,0:T(8,128)(2,1)S(1)} collective-permute-done((bf16[1,256,2048]{2,1,0:T(8,128)(2,1)S(1)}, bf16[1,256,2048]{2,1,0:T(8,128)(2,1)S(1)}, u32[]{:S(2)}, u32[]{:S(2)}) %collective-permute-start.13) | collective-permute-done | bytes 1048608 | tf_op jit(solution)/shard_map/ppermute | solution.py:35
  415.3 13.4 %key_forward.1 = (bf16[1024,1792]{1,0:T(8,128)(2,1)}, bf16[1024,1792]{1,0:T(8,128)(2,1)}) custom-call(s32[1]{0:T(128)} %bitcast.2.c_ref, bf16[1024,2048]{1,0:T(8,128)(2,1)} %maximum_bitcast_fusion.a_ref, bf16[16,4608,256]{2,1,0:T(8,128)(2,1)} %bitcast.549), custom_call_target="tpu_custom_call" | custom-call | flops 7516192768 | bytes 18874368 | tf_op jit(solution)/shard_map/key_forward/pallas_call | solution.py:760
  428.7 13.1 %value_forward.1 = bf16[1024,2048]{1,0:T(8,128)(2,1)} custom-call(s32[1]{0:T(128)} %bitcast.2.c_ref, bf16[1024,1792]{1,0:T(8,128)(2,1)} %get-tuple-element.95.a_ref, bf16[8,2,4608,256]{3,2,1,0:T(8,128)(2,1)} %bitcast.550), custom_call_target="tpu_custom_call" | custom-call | flops 7516192768 | bytes 15204352 | tf_op jit(solution)/shard_map/value_forward/pallas_call | solution.py:760
  462.4 14.0 %collective-permute-done.16 = bf16[256,2048]{1,0:T(8,128)(2,1)} collective-permute-done((bf16[256,2048]{1,0:T(8,128)(2,1)}, bf16[256,2048]{1,0:T(8,128)(2,1)}, u32[]{:S(2)}, u32[]{:S(2)}) %collective-permute-start.16) | collective-permute-done | bytes 1048608 | tf_op jit(solution)/shard_map/ppermute | solution.py:35
  482.2 23.6 %collective-permute-done.18 = bf16[1,256,2048]{2,1,0:T(8,128)(2,1)S(1)} collective-permute-done((bf16[1,256,2048]{2,1,0:T(8,128)(2,1)S(1)}, bf16[1,256,2048]{2,1,0:T(8,128)(2,1)S(1)}, u32[]{:S(2)}, u32[]{:S(2)}) %collective-permute-start.18) | collective-permute-done | bytes 1048608 | tf_op jit(solution)/shard_map/ppermute | solution.py:35
  520.9 14.2 %value_backward.1.a_ref = bf16[1024,1792]{1,0:T(8,128)(2,1)} custom-call(s32[1]{0:T(128)} %bitcast.2.c_ref, bf16[1024,2048]{1,0:T(8,128)(2,1)} %maximum_bitcast_fusion.1.a_ref, bf16[1024,1792]{1,0:T(8,128)(2,1)} %get-tuple-element.97.r_ref, bf16[8,2,4608,256]{3,2,1,0:T(8,128)(2,1)} %bitcast.552), custom_call_target="tpu_custom_call" | custom-call | flops 7516192768 | bytes 15204352 | tf_op jit(solution)/shard_map/value_backward/pallas_call | solution.py:760
  535.0 12.3 %key_backward.1 = bf16[1024,2048]{1,0:T(8,128)(2,1)} custom-call(s32[1]{0:T(128)} %bitcast.2.c_ref, bf16[1024,1792]{1,0:T(8,128)(2,1)} %value_backward.1.a_ref, bf16[16,4608,256]{2,1,0:T(8,128)(2,1)} %bitcast.553), custom_call_target="tpu_custom_call" | custom-call | flops 7516192768 | bytes 15204352 | tf_op jit(solution)/shard_map/key_backward/pallas_call | solution.py:760
  572.1 17.6 %collective-permute-done.21 = bf16[256,2048]{1,0:T(8,128)(2,1)S(1)} collective-permute-done((bf16[256,2048]{1,0:T(8,128)(2,1)}, bf16[256,2048]{1,0:T(8,128)(2,1)S(1)}, u32[]{:S(2)}, u32[]{:S(2)}) %collective-permute-start.21) | collective-permute-done | bytes 1048608 | tf_op jit(solution)/shard_map/ppermute | solution.py:35
  610.9 13.4 %gate_backward.1 = (bf16[256,2048]{1,0:T(8,128)(2,1)S(1)}, bf16[256,2048]{1,0:T(8,128)(2,1)S(1)}, bf16[2,16,64,128]{3,2,1,0:T(8,128)(2,1)S(1)}, f32[2,8,2048]{2,1,0:T(8,128)S(1)}) custom-call(f32[256,2048]{1,0:T(8,128)S(1)} %half_nt.2.grad_ref, f32[256,2048]{1,0:T(8,128)S(1)} %copy-done.59, f32[256,2048]{1,0:T(8,128)S(1)} %copy-done.15, ...), custom_call_target="tpu_custom_call" | custom-call | flops 1610612736 | bytes 13369344 | tf_op jit(solution)/shard_map/gate_backward/pallas_call | solution.py:507
  635.0 33.1 %all-to-all-done.2.refs_1_ = bf16[32,80,128]{2,1,0:T(8,128)(2,1)S(1)} async-done(((bf16[32,80,128]{2,1,0:T(8,128)(2,1)}), bf16[32,80,128]{2,1,0:T(8,128)(2,1)S(1)}, u32[]{:S(2)}, u32[]{:S(2)}) %all-to-all-start.2) | async-done | bytes 655392 | tf_op jit(solution)/shard_map/all_to_all | solution.py:551
  678.7 20.1 %all-to-all-done.3 = bf16[32,64,128]{2,1,0:T(8,128)(2,1)} async-done(((bf16[32,64,128]{2,1,0:T(8,128)(2,1)}), bf16[32,64,128]{2,1,0:T(8,128)(2,1)}, u32[]{:S(2)}, u32[]{:S(2)}) %all-to-all-start.3) | async-done | bytes 524320 | tf_op jit(solution)/shard_map/all_to_all | solution.py:567
  703.2 25.3 %wkv_backward.1 = (bf16[256,2048]{1,0:T(8,128)(2,1)S(1)}, bf16[256,2048]{1,0:T(8,128)(2,1)S(1)}, bf16[256,2048]{1,0:T(8,128)(2,1)S(1)}, bf16[256,2048]{1,0:T(8,128)(2,1)S(1)}, f32[2,8,2048]{2,1,0:T(8,128)S(1)}) custom-call(f32[256,2048]{1,0:T(8,128)S(1)} %copy-done.13, f32[256,2048]{1,0:T(8,128)S(1)} %copy-done.7, f32[256,2048]{1,0:T(8,128)S(1)} %copy-done.10, ...), custom_call_target="tpu_custom_call" | custom-call | flops 4294967296 | bytes 17039360 | tf_op jit(solution)/shard_map/wkv_backward/pallas_call | solution.py:507
  752.4 11.9 %weight_grad.3 = bf16[1024,1536]{1,0:T(8,128)(2,1)S(1)} custom-call(s32[1]{0:T(128)} %bitcast.80.x_ref, bf16[1,256,2048]{2,1,0:T(8,128)(2,1)S(1)} %bitcast.502, bf16[1,256,2048]{2,1,0:T(8,128)(2,1)S(1)} %collective-permute-done.26.refs_1_, bf16[1,256,2048]{2,1,0:T(8,128)(2,1)} %collective-permute-done.24.refs_2_, ...), custom_call_target="tpu_custom_call" | custom-call | flops 3221225472 | bytes 12582912 | tf_op jit(solution)/shard_map/weight_grad/pallas_call | solution.py:228
  764.3 15.1 %collective-permute-done.25 = bf16[3,256,1024]{2,1,0:T(8,128)(2,1)} collective-permute-done((bf16[3,256,1024]{2,1,0:T(8,128)(2,1)}, bf16[3,256,1024]{2,1,0:T(8,128)(2,1)}, u32[]{:S(2)}, u32[]{:S(2)}) %collective-permute-start.25) | collective-permute-done | bytes 1572896 | tf_op jit(solution)/shard_map/ppermute | solution.py:35
  800.1 14.7 %weight_grad.4 = bf16[2048,1536]{1,0:T(8,128)(2,1)} custom-call(s32[1]{0:T(128)} %bitcast.80.x_ref, bf16[4,256,2048]{2,1,0:T(8,128)(2,1)} %pad_maximum_fusion.refs_8_.refs_0_, bf16[4,256,2048]{2,1,0:T(8,128)(2,1)} %collective-permute-done.1.refs_9_.refs_1_, bf16[4,256,2048]{2,1,0:T(8,128)(2,1)} %collective-permute-done.2.refs_10_.refs_2_, ...), custom_call_target="tpu_custom_call" | custom-call | flops 6442450944 | bytes 22020096 | tf_op jit(solution)/shard_map/weight_grad/pallas_call | solution.py:228
  853.2 12.4 %weight_grad.5 = bf16[1024,1536]{1,0:T(8,128)(2,1)S(1)} custom-call(s32[1]{0:T(128)} %bitcast.80.x_ref, bf16[1,256,2048]{2,1,0:T(8,128)(2,1)S(1)} %bitcast.503, bf16[1,256,2048]{2,1,0:T(8,128)(2,1)S(1)} %copy-done.45, bf16[1,256,2048]{2,1,0:T(8,128)(2,1)} %collective-permute-done.24.refs_2_, bf16[1,256,2048]{2,1,0:T(8,128)(2,1)S(1)} %copy-done.47, ...), custom_call_target="tpu_custom_call" | custom-call | flops 3221225472 | bytes 12582912 | tf_op jit(solution)/shard_map/weight_grad/pallas_call | solution.py:228
  868.9 12.2 %bitcast_add_fusion = f32[256,2048]{1,0:T(8,128)} fusion(f32[2,128,2048]{2,1,0:T(8,128)} %pad_maximum_fusion.10, f32[256,2048]{1,0:T(8,128)} %get-tuple-element.326, f32[256,2048]{1,0:T(8,128)} %copy-done.5, f32[256,2048]{1,0:T(8,128)} %copy-done.82, f32[256,2048]{1,0:T(8,128)S(1)} %stack_nt.5, f32[256,2048]{1,0:T(8,128)} %copy-done.80, ...), kind=kLoop, calls=%fused_computation.49 | loop fusion | flops 8912896 | bytes 27271168 | tf_op jit(solution)/shard_map/add | solution.py:1123
  (648 shorter events, 500.8 us)
Async XLA Ops:
  7.2 194.2 %all-gather.7.cloned.1.call-start = ((), (), s32[]{:S(2)}) async-start(), calls=%async_computation.10 | async-start | bytes 35651584 | tf_op jit(solution)/shard_map/all_gather | solution.py:974
  12.7 402.5 %all-gather.9.cloned.1.call-start = ((), (), s32[]{:S(2)}) async-start(), calls=%async_computation.11 | async-start | bytes 40108032 | tf_op jit(solution)/shard_map/all_gather | solution.py:981
  100.0 92.9 %collective-permute-start.2 = (bf16[4,256,2048]{2,1,0:T(8,128)(2,1)}, bf16[4,256,2048]{2,1,0:T(8,128)(2,1)}, u32[]{:S(2)}, u32[]{:S(2)}) collective-permute-start(bf16[4,256,2048]{2,1,0:T(8,128)(2,1)} %pad_maximum_fusion.refs_8_.refs_0_), channel_id=1, source_target_pairs={{0,16},{16,0},{1,17},{17,1},{2,18},{18,2},{3,19},{19,3},{4,20},{20... | collective-permute-start | bytes 12582920 | tf_op jit(solution)/shard_map/ppermute | solution.py:35
  101.1 93.5 %collective-permute-start.1 = (bf16[4,256,2048]{2,1,0:T(8,128)(2,1)}, bf16[4,256,2048]{2,1,0:T(8,128)(2,1)}, u32[]{:S(2)}, u32[]{:S(2)}) collective-permute-start(bf16[4,256,2048]{2,1,0:T(8,128)(2,1)} %pad_maximum_fusion.refs_8_.refs_0_), channel_id=1, source_target_pairs={{0,1},{1,0},{2,3},{3,2},{4,5},{5,4},{6,7},{7,6},{8,9},{9,8},{10,11... | collective-permute-start | bytes 12582920 | tf_op jit(solution)/shard_map/ppermute | solution.py:35
  206.1 57.8 %collective-permute-start.4 = (bf16[16,128,512]{2,1,0:T(8,128)(2,1)}, bf16[16,128,512]{2,1,0:T(8,128)(2,1)}, u32[]{:S(2)}, u32[]{:S(2)}) collective-permute-start(bf16[16,128,512]{2,1,0:T(8,128)(2,1)} %get-tuple-element.214), channel_id=1, source_target_pairs={{0,16},{16,0},{1,17},{17,1},{2,18},{18,2},{3,19},{19,3},{4,20},{20... | collective-permute-start | bytes 6291464 | tf_op jit(solution)/shard_map/ppermute | solution.py:35
  233.1 30.9 %all-to-all-start = ((bf16[32,80,128]{2,1,0:T(8,128)(2,1)}), bf16[32,80,128]{2,1,0:T(8,128)(2,1)}, u32[]{:S(2)}, u32[]{:S(2)}) async-start(bf16[32,80,128]{2,1,0:T(8,128)(2,1)} %pad_maximum_fusion.12), calls=%async_computation | async-start | bytes 1310720 | tf_op jit(solution)/shard_map/all_to_all | solution.py:551
  237.5 74.0 %collective-permute-start.5 = (bf16[16,128,512]{2,1,0:T(8,128)(2,1)}, bf16[16,128,512]{2,1,0:T(8,128)(2,1)}, u32[]{:S(2)}, u32[]{:S(2)}) collective-permute-start(bf16[16,128,512]{2,1,0:T(8,128)(2,1)} %get-tuple-element.213), channel_id=1, source_target_pairs={{0,16},{16,0},{1,17},{17,1},{2,18},{18,2},{3,19},{19,3},{4,20},{20... | collective-permute-start | bytes 6291464 | tf_op jit(solution)/shard_map/ppermute | solution.py:35
  266.5 45.3 %all-to-all-start.1 = ((bf16[32,64,128]{2,1,0:T(8,128)(2,1)}), bf16[32,64,128]{2,1,0:T(8,128)(2,1)}, u32[]{:S(2)}, u32[]{:S(2)}) async-start(bf16[32,64,128]{2,1,0:T(8,128)(2,1)} %copy-done.57), calls=%async_computation.1 | async-start | bytes 1048576 | tf_op jit(solution)/shard_map/all_to_all | solution.py:567
  269.9 428.9 %reduce-scatter.4.cloned.1.call-start = ((), (), s32[]{:S(2)}) async-start(), calls=%async_computation.7 | async-start | bytes 8257536 | tf_op jit(solution)/shard_map/reduce_scatter | solution.py:1042
  270.4 48.7 %collective-permute-start.6 = (bf16[16,128,512]{2,1,0:T(8,128)(2,1)}, bf16[16,128,512]{2,1,0:T(8,128)(2,1)}, u32[]{:S(2)}, u32[]{:S(2)}) collective-permute-start(bf16[16,128,512]{2,1,0:T(8,128)(2,1)} %collective-permute-done.4.g_ref), channel_id=1, source_target_pairs={{0,1},{1,0},{2,3},{3,2},{4,5},{5,4},{6,7},{7,6},{8,9},{9,8},{10,11... | collective-permute-start | bytes 6291464 | tf_op jit(solution)/shard_map/ppermute | solution.py:35
  311.8 36.0 %collective-permute-start.7 = (bf16[16,128,512]{2,1,0:T(8,128)(2,1)}, bf16[16,128,512]{2,1,0:T(8,128)(2,1)}, u32[]{:S(2)}, u32[]{:S(2)}) collective-permute-start(bf16[16,128,512]{2,1,0:T(8,128)(2,1)} %collective-permute-done.5.g_ref), channel_id=1, source_target_pairs={{0,1},{1,0},{2,3},{3,2},{4,5},{5,4},{6,7},{7,6},{8,9},{9,8},{10,11... | collective-permute-start | bytes 6291464 | tf_op jit(solution)/shard_map/ppermute | solution.py:35
  361.7 31.1 %collective-permute-start.10 = (bf16[1,256,2048]{2,1,0:T(8,128)(2,1)S(1)}, bf16[1,256,2048]{2,1,0:T(8,128)(2,1)S(1)}, u32[]{:S(2)}, u32[]{:S(2)}) collective-permute-start(bf16[1,256,2048]{2,1,0:T(8,128)(2,1)S(1)} %get-tuple-element.207), channel_id=1, source_target_pairs={{0,16},{16,0},{1,17},{17,1},{2,18},{18,2},{3,19},{19,3},{4,20},{20... | collective-permute-start | bytes 3145736 | tf_op jit(solution)/shard_map/ppermute | solution.py:35
  368.7 42.2 %collective-permute-start.13 = (bf16[1,256,2048]{2,1,0:T(8,128)(2,1)S(1)}, bf16[1,256,2048]{2,1,0:T(8,128)(2,1)S(1)}, u32[]{:S(2)}, u32[]{:S(2)}) collective-permute-start(bf16[1,256,2048]{2,1,0:T(8,128)(2,1)S(1)} %bitcast.508), channel_id=1, source_target_pairs={{0,16},{16,0},{1,17},{17,1},{2,18},{18,2},{3,19},{19,3},{4,20},{20... | collective-permute-start | bytes 3145736 | tf_op jit(solution)/shard_map/ppermute | solution.py:35
  368.8 42.2 %collective-permute-start.9 = (bf16[1,256,2048]{2,1,0:T(8,128)(2,1)S(1)}, bf16[1,256,2048]{2,1,0:T(8,128)(2,1)S(1)}, u32[]{:S(2)}, u32[]{:S(2)}) collective-permute-start(bf16[1,256,2048]{2,1,0:T(8,128)(2,1)S(1)} %get-tuple-element.207), channel_id=1, source_target_pairs={{0,1},{1,0},{2,3},{3,2},{4,5},{5,4},{6,7},{7,6},{8,9},{9,8},{10,11... | collective-permute-start | bytes 3145736 | tf_op jit(solution)/shard_map/ppermute | solution.py:35
  520.6 294.2 %reduce-scatter.6.cloned.1.call-start = ((), (), s32[]{:S(2)}) async-start(), calls=%async_computation.8 | async-start | bytes 8257536 | tf_op jit(solution)/shard_map/reduce_scatter | solution.py:1047
  626.2 41.9 %all-to-all-start.2 = ((bf16[32,80,128]{2,1,0:T(8,128)(2,1)}), bf16[32,80,128]{2,1,0:T(8,128)(2,1)S(1)}, u32[]{:S(2)}, u32[]{:S(2)}) async-start(bf16[32,80,128]{2,1,0:T(8,128)(2,1)} %pad_maximum_fusion.11), calls=%async_computation.2 | async-start | bytes 1310720 | tf_op jit(solution)/shard_map/all_to_all | solution.py:551
  672.9 294.3 %reduce-scatter.8.cloned.1.call-start = ((), (), s32[]{:S(2)}) async-start(), calls=%async_computation.9 | async-start | bytes 7077888 | tf_op jit(solution)/shard_map/reduce_scatter | solution.py:1092
  676.7 62.2 %collective-permute-start.23 = (bf16[3,256,1024]{2,1,0:T(8,128)(2,1)}, bf16[3,256,1024]{2,1,0:T(8,128)(2,1)}, u32[]{:S(2)}, u32[]{:S(2)}) collective-permute-start(bf16[3,256,1024]{2,1,0:T(8,128)(2,1)} %get-tuple-element.236), channel_id=1, source_target_pairs={{0,16},{16,0},{1,17},{17,1},{2,18},{18,2},{3,19},{19,3},{4,20},{20... | collective-permute-start | bytes 4718600 | tf_op jit(solution)/shard_map/ppermute | solution.py:35
  678.3 60.7 %collective-permute-start.24 = (bf16[1,256,2048]{2,1,0:T(8,128)(2,1)S(1)}, bf16[1,256,2048]{2,1,0:T(8,128)(2,1)}, u32[]{:S(2)}, u32[]{:S(2)}) collective-permute-start(bf16[1,256,2048]{2,1,0:T(8,128)(2,1)S(1)} %bitcast.500), channel_id=1, source_target_pairs={{0,16},{16,0},{1,17},{17,1},{2,18},{18,2},{3,19},{19,3},{4,20},{20... | collective-permute-start | bytes 3145736 | tf_op jit(solution)/shard_map/ppermute | solution.py:35
  742.3 37.1 %collective-permute-start.25 = (bf16[3,256,1024]{2,1,0:T(8,128)(2,1)}, bf16[3,256,1024]{2,1,0:T(8,128)(2,1)}, u32[]{:S(2)}, u32[]{:S(2)}) collective-permute-start(bf16[3,256,1024]{2,1,0:T(8,128)(2,1)} %get-tuple-element.237), channel_id=1, source_target_pairs={{0,16},{16,0},{1,17},{17,1},{2,18},{18,2},{3,19},{19,3},{4,20},{20... | collective-permute-start | bytes 4718600 | tf_op jit(solution)/shard_map/ppermute | solution.py:35
  783.4 97.7 %collective-permute-start.31 = (bf16[1024,1536]{1,0:T(8,128)(2,1)}, bf16[1024,1536]{1,0:T(8,128)(2,1)}, u32[]{:S(2)}, u32[]{:S(2)}) collective-permute-start(bf16[1024,1536]{1,0:T(8,128)(2,1)} %copy-done.56), channel_id=1, source_target_pairs={{0,2},{2,0},{1,3},{3,1},{4,6},{6,4},{5,7},{7,5},{8,10},{10,8},{9,1... | collective-permute-start | bytes 9437192 | tf_op jit(solution)/shard_map/ppermute | solution.py:35
  926.5 40.8 %collective-permute-start.34 = (bf16[256,1536]{0,1:T(8,128)(2,1)}, bf16[256,1536]{0,1:T(8,128)(2,1)}, u32[]{:S(2)}, u32[]{:S(2)}) collective-permute-start(bf16[256,1536]{0,1:T(8,128)(2,1)} %fusion.49), channel_id=1, source_target_pairs={{0,4},{4,8},{1,5},{5,9},{2,6},{6,10},{3,7},{7,11},{16,20},{20,24},... | collective-permute-start | bytes 2359304 | tf_op jit(solution)/shard_map/ppermute | solution.py:66
  934.0 33.2 %collective-permute-start.35 = (bf16[256,1536]{0,1:T(8,128)(2,1)}, bf16[256,1536]{0,1:T(8,128)(2,1)}, u32[]{:S(2)}, u32[]{:S(2)}) collective-permute-start(bf16[256,1536]{0,1:T(8,128)(2,1)} %fusion.48), channel_id=1, source_target_pairs={{8,4},{12,8},{9,5},{13,9},{10,6},{14,10},{11,7},{15,11},{24,20},{2... | collective-permute-start | bytes 2359304 | tf_op jit(solution)/shard_map/ppermute | solution.py:67
  975.7 29.9 %collective-permute-start.39 = (bf16[256,1536]{0,1:T(8,128)(2,1)S(1)}, bf16[256,1536]{0,1:T(8,128)(2,1)S(1)}, u32[]{:S(2)}, u32[]{:S(2)}) collective-permute-start(bf16[256,1536]{0,1:T(8,128)(2,1)S(1)} %fusion.47), channel_id=1, source_target_pairs={{0,4},{4,8},{8,12},{1,5},{5,9},{9,13},{2,6},{6,10},{10,14},{3,7},{... | collective-permute-start | bytes 2359304 | tf_op jit(solution)/shard_map/ppermute | solution.py:66
  (208 other events, 2815.9 us)
Sparse Core Ops, SparseCore 0:
  12.9 188.5 all-gather.6
  203.6 207.0 all-gather.8
  520.8 147.5 reduce-scatter.3
  671.8 139.8 reduce-scatter.5
  815.1 130.1 reduce-scatter.7
